TPU v7x, 32 devices: a whole 2x2x4 slice. The times are simulated.
32 devices in a mesh: wide: 8 (over z, x), blk: 4 (over y, core).
Axes of the slice: x: 2, y: 2, z: 4, core: 2. Of those that a mesh axis runs over, the one named last changes fastest.
Arguments:
- patches: bfloat16 [32, 256, 768], P('wide', 'blk'), may hold values from -6 to 6
- norm_gain: bfloat16 [2, 768], P(None, ('wide', 'blk')), may hold values from 0.099609375 to 1.8984375
- norm_bias: bfloat16 [2, 768], P(None, ('wide', 'blk')), may hold values from -3 to 3
- qkv_weight: bfloat16 [768, 2304], P(('wide', 'blk')), may hold values from -0.21875 to 0.21875
- qv_bias: bfloat16 [2, 768], P(None, ('wide', 'blk')), may hold values from -3 to 3
- out_weight: bfloat16 [768, 768], P(('wide', 'blk')), may hold values from -0.875 to 0.875
- fc1_weight: bfloat16 [768, 3072], P(('wide', 'blk')), may hold values from -0.21875 to 0.21875
- fc1_bias: bfloat16 [3072], P(('wide', 'blk')), may hold values from -3 to 3
- fc2_weight: bfloat16 [3072, 768], P(('wide', 'blk')), may hold values from -0.109375 to 0.109375
- res_bias: bfloat16 [2, 768], P(None, ('wide', 'blk')), may hold values from -3 to 3
- cotangent: bfloat16 [32, 256, 768], P('wide', 'blk'), may hold values from -6 to 6
- frame_valid: int32 [32], P('wide'), may hold values 0 or 1
Outputs:
- encoded: bfloat16 [32, 256, 768], P('wide', 'blk')
- grad_patches: float32 [32, 256, 768], P('wide', 'blk')
- grad_norm_gain: float32 [2, 768], P(None, ('wide', 'blk'))
- grad_norm_bias: float32 [2, 768], P(None, ('wide', 'blk'))
- grad_qkv_weight: float32 [768, 2304], P(('wide', 'blk'))
- grad_qv_bias: float32 [2, 768], P(None, ('wide', 'blk'))
- grad_out_weight: float32 [768, 768], P(('wide', 'blk'))
- grad_fc1_weight: float32 [768, 3072], P(('wide', 'blk'))
- grad_fc1_bias: float32 [3072], P(('wide', 'blk'))
- grad_fc2_weight: float32 [3072, 768], P(('wide', 'blk'))
- grad_res_bias: float32 [2, 768], P(None, ('wide', 'blk'))
All inputs are finite; a program needn't handle non-finite values. No bound on the sum of `frame_valid` on one device may be relied on, other than what follows from the above.
Results may differ from a plain program's by a relative error of at most 0.013.
Values may be sent and summed in bfloat16 or wider, within the bound.
A program may use at most 128 MiB of HBM per device.

v0:
```python
from functools import partial
import math

import jax
import jax.numpy as jnp
from jax import lax
from jax.sharding import PartitionSpec as P

D = 768
HEADS = 12
HEAD = 64


EPSILON = 1e-06


def layer_normalize(token_rows, norm_gain_vector, norm_bias_vector):
    row_average = jnp.mean(token_rows, axis=-1, keepdims=True)
    centered_rows = token_rows - row_average
    inverse_deviation_scale = lax.rsqrt(
        jnp.mean(centered_rows * centered_rows, axis=-1, keepdims=True) + EPSILON
    )
    standardized_rows = centered_rows * inverse_deviation_scale
    return (
        standardized_rows * norm_gain_vector + norm_bias_vector,
        standardized_rows,
        inverse_deviation_scale,
    )


def layer_normalize_backward(
    incoming_gradient, standardized_rows, inverse_deviation_scale, norm_gain_vector
):
    gain_weighted_gradient = incoming_gradient * norm_gain_vector
    inner_product_sum = (
        gain_weighted_gradient
        - jnp.mean(gain_weighted_gradient, axis=-1, keepdims=True)
        - standardized_rows
        * jnp.mean(gain_weighted_gradient * standardized_rows, axis=-1, keepdims=True)
    )
    return (
        inverse_deviation_scale * inner_product_sum,
        jnp.sum(incoming_gradient * standardized_rows, axis=0),
        jnp.sum(incoming_gradient, axis=0),
    )


def frame_groups(array, count):
    return array.reshape((array.shape[0] // count, count) + array.shape[1:])


def attend_forward(query, keys, values):
    scores = jnp.einsum("gqhe,gkhe->ghqk", query, keys, preferred_element_type=jnp.float32)
    top = jnp.max(scores, axis=-1, keepdims=True)
    expo = jnp.exp(scores - top)
    total = jnp.sum(expo, axis=-1, keepdims=True)
    probs = (expo / total).astype(jnp.bfloat16)
    attended = jnp.einsum("ghqk,gkhe->gqhe", probs, values, preferred_element_type=jnp.float32)
    return (attended, top + jnp.log(total))


def attend_back(query, keys, values, logsum, grad_out):
    scores = jnp.einsum("gqhe,gkhe->ghqk", query, keys, preferred_element_type=jnp.float32)
    probs = jnp.exp(scores - logsum)
    grad_probs = jnp.einsum("gqhe,gkhe->ghqk", grad_out, values, preferred_element_type=jnp.float32)
    grad_values = jnp.einsum(
        "ghqk,gqhe->gkhe", probs.astype(jnp.bfloat16), grad_out, preferred_element_type=jnp.float32
    )
    grad_scores = (
        probs * (grad_probs - jnp.sum(probs * grad_probs, axis=-1, keepdims=True))
    ).astype(jnp.bfloat16)
    grad_query = jnp.einsum(
        "ghqk,gkhe->gqhe", grad_scores, keys, preferred_element_type=jnp.float32
    )
    grad_keys = jnp.einsum(
        "ghqk,gqhe->gkhe", grad_scores, query, preferred_element_type=jnp.float32
    )
    return (grad_query, grad_keys, grad_values)


def local(
    patches,
    norm_gain,
    norm_bias,
    qkv_weight,
    qv_bias,
    out_weight,
    fc1_weight,
    fc1_bias,
    fc2_weight,
    res_bias,
    cotangent,
    frame_valid,
):
    frames, frame_rows, width = patches.shape
    count = frames * frame_rows
    group = math.gcd(frames, 8)
    params = (
        lax.all_gather(norm_gain, ("wide", "blk"), axis=1, tiled=True),
        lax.all_gather(norm_bias, ("wide", "blk"), axis=1, tiled=True),
        lax.all_gather(qkv_weight, ("wide", "blk"), axis=0, tiled=True),
        lax.all_gather(qv_bias, ("wide", "blk"), axis=1, tiled=True),
        lax.all_gather(out_weight, ("wide", "blk"), axis=0, tiled=True),
        lax.all_gather(fc1_weight, ("wide", "blk"), axis=0, tiled=True),
        lax.all_gather(fc1_bias, ("wide", "blk"), axis=0, tiled=True),
        lax.all_gather(fc2_weight, ("wide", "blk"), axis=0, tiled=True),
        lax.all_gather(res_bias, ("wide", "blk"), axis=1, tiled=True),
    )
    norm_gain_pair = params[0].astype(jnp.float32)
    norm_bias_pair = params[1].astype(jnp.float32)
    biases_qv = params[3].astype(jnp.float32)
    bias_fc1 = params[6].astype(jnp.float32)
    biases_res = params[8].astype(jnp.float32)
    token_rows = patches.reshape(count, width).astype(jnp.float32)
    valid = jnp.repeat(frame_valid.astype(jnp.float32), frame_rows)[:, None]
    first_branch, first_standardized_rows, first_norm_scale = layer_normalize(
        token_rows, norm_gain_pair[0], norm_bias_pair[0]
    )
    normed = first_branch.astype(jnp.bfloat16)
    mixed = jnp.dot(normed, params[2], preferred_element_type=jnp.float32)
    query = ((mixed[:, :D] + biases_qv[0]) * 0.125).astype(jnp.bfloat16)
    keys = mixed[:, D : 2 * D].astype(jnp.bfloat16).reshape(frames, frame_rows, width)
    values = (
        (mixed[:, 2 * D :] + biases_qv[1]).astype(jnp.bfloat16).reshape(frames, frame_rows, width)
    )
    keys_all, values_all = (
        lax.all_gather(keys, "blk", axis=1, tiled=True),
        lax.all_gather(values, "blk", axis=1, tiled=True),
    )
    query_heads = frame_groups(query.reshape(frames, frame_rows, HEADS, HEAD), group)
    keys_heads = frame_groups(keys_all.reshape(frames, -1, HEADS, HEAD), group)
    values_heads = frame_groups(values_all.reshape(frames, -1, HEADS, HEAD), group)
    attended, logsum = lax.map(
        lambda item: attend_forward(item[0], item[1], item[2]),
        (query_heads, keys_heads, values_heads),
    )
    attended = attended.reshape(count, width).astype(jnp.bfloat16)
    middle_activation = (
        token_rows
        + jnp.dot(attended, params[4], preferred_element_type=jnp.float32)
        + biases_res[0]
    )
    second_branch, second_standardized_rows, second_norm_scale = layer_normalize(
        middle_activation, norm_gain_pair[1], norm_bias_pair[1]
    )
    normed2 = second_branch.astype(jnp.bfloat16)
    hidden = jnp.dot(normed2, params[5], preferred_element_type=jnp.float32) + bias_fc1
    active = jax.nn.gelu(hidden, approximate=False).astype(jnp.bfloat16)
    branch2 = jnp.dot(active, params[7], preferred_element_type=jnp.float32) + biases_res[1]
    encoded = (
        ((middle_activation + branch2) * valid)
        .astype(jnp.bfloat16)
        .reshape(frames, frame_rows, width)
    )
    params = (
        lax.all_gather(norm_gain, ("wide", "blk"), axis=1, tiled=True),
        lax.all_gather(norm_bias, ("wide", "blk"), axis=1, tiled=True),
        lax.all_gather(qkv_weight, ("wide", "blk"), axis=0, tiled=True),
        lax.all_gather(qv_bias, ("wide", "blk"), axis=1, tiled=True),
        lax.all_gather(out_weight, ("wide", "blk"), axis=0, tiled=True),
        lax.all_gather(fc1_weight, ("wide", "blk"), axis=0, tiled=True),
        lax.all_gather(fc1_bias, ("wide", "blk"), axis=0, tiled=True),
        lax.all_gather(fc2_weight, ("wide", "blk"), axis=0, tiled=True),
        lax.all_gather(res_bias, ("wide", "blk"), axis=1, tiled=True),
    )
    grad_out = cotangent.reshape(count, width).astype(jnp.float32) * valid
    grad_branch2 = grad_out.astype(jnp.bfloat16)
    grad_fc2 = jnp.dot(active.T, grad_branch2, preferred_element_type=jnp.float32)
    grad_res_two = jnp.sum(grad_branch2.astype(jnp.float32), axis=0)
    grad_active = jnp.dot(grad_branch2, params[7].T, preferred_element_type=jnp.float32)
    gelu_back = jax.vjp(partial(jax.nn.gelu, approximate=False), hidden)[1]
    grad_hidden = gelu_back(grad_active)[0].astype(jnp.bfloat16)
    grad_fc1 = jnp.dot(normed2.T, grad_hidden, preferred_element_type=jnp.float32)
    grad_bias_fc1 = jnp.sum(grad_hidden.astype(jnp.float32), axis=0)
    normed_input_gradient2 = jnp.dot(grad_hidden, params[5].T, preferred_element_type=jnp.float32)
    second_norm_gradient, second_norm_gain, second_norm_bias = layer_normalize_backward(
        normed_input_gradient2, second_standardized_rows, second_norm_scale, norm_gain_pair[1]
    )
    grad_middle = grad_out + second_norm_gradient
    grad_branch = grad_middle.astype(jnp.bfloat16)
    grad_out_proj = jnp.dot(attended.T, grad_branch, preferred_element_type=jnp.float32)
    grad_res_one = jnp.sum(grad_branch.astype(jnp.float32), axis=0)
    grad_attended = jnp.dot(grad_branch, params[4].T, preferred_element_type=jnp.float32).astype(
        jnp.bfloat16
    )
    grad_heads = frame_groups(grad_attended.reshape(frames, frame_rows, HEADS, HEAD), group)
    grad_query, grad_keys, grad_values = lax.map(
        lambda item: attend_back(item[0], item[1], item[2], item[3], item[4]),
        (query_heads, keys_heads, values_heads, logsum, grad_heads),
    )
    grad_keys, grad_values = (
        lax.psum_scatter(
            grad_keys.reshape(frames, -1, width).astype(jnp.bfloat16),
            "blk",
            scatter_dimension=1,
            tiled=True,
        ).astype(jnp.float32),
        lax.psum_scatter(
            grad_values.reshape(frames, -1, width).astype(jnp.bfloat16),
            "blk",
            scatter_dimension=1,
            tiled=True,
        ).astype(jnp.float32),
    )
    grad_query = grad_query.reshape(count, width).astype(jnp.bfloat16) * 0.125
    grad_keys = grad_keys.reshape(count, width).astype(jnp.bfloat16)
    grad_values = grad_values.reshape(count, width).astype(jnp.bfloat16)
    grad_mixed = jnp.concatenate([grad_query, grad_keys, grad_values], axis=1)
    grad_qkv = jnp.dot(normed.T, grad_mixed, preferred_element_type=jnp.float32)
    grad_qv = jnp.stack(
        [
            jnp.sum(grad_query.astype(jnp.float32), axis=0),
            jnp.sum(grad_values.astype(jnp.float32), axis=0),
        ]
    )
    normed_input_gradient = jnp.dot(grad_mixed, params[2].T, preferred_element_type=jnp.float32)
    first_norm_gradient, first_norm_gain, first_norm_bias = layer_normalize_backward(
        normed_input_gradient, first_standardized_rows, first_norm_scale, norm_gain_pair[0]
    )
    grad_rows = (grad_middle + first_norm_gradient).reshape(frames, frame_rows, width)
    grad_gain = jnp.stack([first_norm_gain, second_norm_gain])
    grad_shift = jnp.stack([first_norm_bias, second_norm_bias])
    grad_res = jnp.stack([grad_res_one, grad_res_two])
    summed = (
        lax.psum_scatter(grad_gain, ("wide", "blk"), scatter_dimension=1, tiled=True),
        lax.psum_scatter(grad_shift, ("wide", "blk"), scatter_dimension=1, tiled=True),
        lax.psum_scatter(grad_qkv, ("wide", "blk"), scatter_dimension=0, tiled=True),
        lax.psum_scatter(grad_qv, ("wide", "blk"), scatter_dimension=1, tiled=True),
        lax.psum_scatter(grad_out_proj, ("wide", "blk"), scatter_dimension=0, tiled=True),
        lax.psum_scatter(grad_fc1, ("wide", "blk"), scatter_dimension=0, tiled=True),
        lax.psum_scatter(grad_bias_fc1, ("wide", "blk"), scatter_dimension=0, tiled=True),
        lax.psum_scatter(grad_fc2, ("wide", "blk"), scatter_dimension=0, tiled=True),
        lax.psum_scatter(grad_res, ("wide", "blk"), scatter_dimension=1, tiled=True),
    )
    return (
        encoded,
        grad_rows,
        summed[0],
        summed[1],
        summed[2],
        summed[3],
        summed[4],
        summed[5],
        summed[6],
        summed[7],
        summed[8],
    )


def solution(mesh):
    in_specs = (
        P("wide", "blk", None),
        P(None, ("wide", "blk")),
        P(None, ("wide", "blk")),
        P(("wide", "blk"), None),
        P(None, ("wide", "blk")),
        P(("wide", "blk"), None),
        P(("wide", "blk"), None),
        P(("wide", "blk")),
        P(("wide", "blk"), None),
        P(None, ("wide", "blk")),
        P("wide", "blk", None),
        P("wide"),
    )
    out_specs = (
        P("wide", "blk", None),
        P("wide", "blk", None),
        P(None, ("wide", "blk")),
        P(None, ("wide", "blk")),
        P(("wide", "blk"), None),
        P(None, ("wide", "blk")),
        P(("wide", "blk"), None),
        P(("wide", "blk"), None),
        P(("wide", "blk")),
        P(("wide", "blk"), None),
        P(None, ("wide", "blk")),
    )
    return jax.shard_map(local, mesh=mesh, in_specs=in_specs, out_specs=out_specs, check_vma=False)
```

profile of v0, /device:TPU:0, one launch (start us, length us, event | category | flops | bytes accessed | tf_op | source)
XLA Modules:
  0.0 945.6 jit_solution(4312519391309911998)
XLA Ops:
  9.2 1.2 multiply_reduce_fusion.6
  10.5 43.2 %all-gather = bf16[32,24,2]{1,2,0:T(2,128)(2,1)S(1)} all-gather(bf16[1,24,2]{1,2,0:T(2,128)(2,1)} %bitcast.118), channel_id=1, replica_groups=mesh['wide'=8,'blk'=4] {'wide','blk'}, dimensions={0}, use_global_device_ids=true | all-gather | bytes 3168 | tf_op jit(solution)/shard_map/all_gather | solution.py:99
  53.8 36.6 %all-gather.1 = bf16[32,24,2]{1,2,0:T(2,128)(2,1)S(1)} all-gather(bf16[1,24,2]{1,2,0:T(2,128)(2,1)} %bitcast.119), channel_id=1, replica_groups=mesh['wide'=8,'blk'=4] {'wide','blk'}, dimensions={0}, use_global_device_ids=true | all-gather | bytes 3168 | tf_op jit(solution)/shard_map/all_gather | solution.py:100
  90.9 1.2 add_convert_fusion.2
  92.2 3.2 fusion.34
  96.4 37.9 %all-gather.2 = bf16[32,24,2]{1,2,0:T(2,128)(2,1)S(1)} all-gather(bf16[1,24,2]{1,2,0:T(2,128)(2,1)S(1)} %bitcast.120), channel_id=1, replica_groups=mesh['wide'=8,'blk'=4] {'wide','blk'}, dimensions={0}, use_global_device_ids=true | all-gather | bytes 3168 | tf_op jit(solution)/shard_map/all_gather | solution.py:102
  138.0 37.0 %all-reduce = bf16[3072]{0:T(1024)(128)(2,1)S(1)} all-reduce(bf16[3072]{0:T(1024)(128)(2,1)S(1)} %dynamic-update-slice), channel_id=1, replica_groups=mesh['wide'=8,'blk'=4] {'wide','blk'}, use_global_device_ids=true, to_apply=%add | all-reduce | flops 3072 | bytes 12288
  175.7 40.1 %all-gather.3 = bf16[32,24,2]{1,2,0:T(2,128)(2,1)S(1)} all-gather(bf16[1,24,2]{1,2,0:T(2,128)(2,1)S(1)} %bitcast.121), channel_id=1, replica_groups=mesh['wide'=8,'blk'=4] {'wide','blk'}, dimensions={0}, use_global_device_ids=true | all-gather | bytes 3168 | tf_op jit(solution)/shard_map/all_gather | solution.py:107
  218.2 1.5 copy.81
  219.7 2.6 copy.73
  222.3 2.7 copy.71
  225.0 2.5 fusion.32
  228.5 1.8 fusion.13
  230.3 1.5 copy.75
  231.8 2.5 convert_element_type.159
  234.3 2.0 fusion.33
  238.7 35.3 %all-gather.19.cloned.1.call-done = bf16[768,3072]{1,0:T(8,128)(2,1)} async-done(((bf16[24,3072]{1,0:T(8,128)(2,1)}), bf16[768,3072]{1,0:T(8,128)(2,1)}) %all-gather.19.cloned.1.call-update) | async-done | bytes 4718608 | tf_op jit(solution)/shard_map/all_gather | solution.py:104
  273.9 5.7 convolution_add_fusion
  279.6 59.5 %all-gather.21.cloned.1.call-done = bf16[3072,768]{1,0:T(8,128)(2,1)} async-done(((bf16[96,768]{1,0:T(8,128)(2,1)}), bf16[3072,768]{1,0:T(8,128)(2,1)}) %all-gather.21.cloned.1.call-update) | async-done | bytes 4718608 | tf_op jit(solution)/shard_map/all_gather | solution.py:106
  339.1 12.3 %convert_reduce_fusion = (f32[3072]{0:T(1024)}, bf16[256,3072]{1,0:T(8,128)(2,1)S(1)}, f32[256,3072]{1,0:T(8,128)}) fusion(f32[256,3072]{1,0:T(8,128)} %convolution_add_fusion, bf16[256,768]{1,0:T(8,128)(2,1)} %fusion.22, bf16[3072,768]{1,0:T(8,128)(2,1)} %all-gather.21.cloned.1.call-done), kind=kOutput, calls=%fused_computation.3 | convolution fusion | flops 1266152448 | bytes 12988416 | tf_op jit(solution)/shard_map/dot_general | solution.py:170
  351.4 2.1 multiply_reduce_fusion.1
  355.4 1.3 convolution_convert_fusion.3
  356.7 2.4 reshape.181
  359.1 2.5 copy.83
  361.6 3.0 convolution_convert_fusion
  364.6 2.6 copy.84
  367.3 3.0 multiply_reduce_fusion
  373.2 1.7 copy.82
  375.0 3.3 fusion.27
  378.4 2.0 convert_reduce_fusion.1
  380.4 1.6 copy.80
  382.5 11.9 %reduce-scatter.13.cloned.1.call-done = bf16[4,64,768]{2,1,0:T(8,128)(2,1)} async-done(((bf16[4,256,768]{2,1,0:T(8,128)(2,1)}), bf16[4,64,768]{2,1,0:T(8,128)(2,1)}) %reduce-scatter.13.cloned.1.call-update) | async-done | bytes 393232 | tf_op jit(solution)/shard_map/reduce_scatter | solution.py:198
  394.4 1.2 copy.86
  395.6 29.7 %reduce-scatter.11.cloned.1.call-done = bf16[4,64,768]{2,1,0:T(8,128)(2,1)} async-done(((bf16[4,256,768]{2,1,0:T(8,128)(2,1)}), bf16[4,64,768]{2,1,0:T(8,128)(2,1)}) %reduce-scatter.11.cloned.1.call-update) | async-done | bytes 393232 | tf_op jit(solution)/shard_map/reduce_scatter | solution.py:192
  425.3 1.2 copy.85
  426.5 4.0 fusion.23
  432.2 5.2 fusion.30
  437.7 3.5 multiply_convert_fusion.1
  441.2 5.1 fusion.35
  448.2 1.3 stack.37
  450.9 4.7 fusion.17
  455.8 1.4 multiply_reduce_fusion.2
  457.2 40.2 %all-reduce.6 = (f32[2,768]{1,0:T(2,128)S(1)}, f32[2,768]{1,0:T(2,128)S(1)}, f32[2,768]{1,0:T(2,128)S(1)}, f32[3072]{0:T(1024)S(1)}, f32[2,768]{1,0:T(2,128)S(1)}) all-reduce(f32[2,768]{1,0:T(2,128)S(1)} %pad_maximum_fusion.3, f32[2,768]{1,0:T(2,128)S(1)} %pad_maximum_fusion.4, ...), channel_id=4, replica_groups=mesh['wide'=8,'blk'=4] {'wide','blk'}, use_global_device_ids=true, to_apply=%region_15.16.clone | all-reduce | flops 9216 | bytes 73728
  500.6 1.2 multiply_add_fusion
  501.8 28.5 %reduce-scatter.17.cloned.1.call-done = f32[24,768]{1,0:T(8,128)} async-done(((f32[768,768]{1,0:T(8,128)}), f32[24,768]{1,0:T(8,128)}) %reduce-scatter.17.cloned.1.call-update) | async-done | bytes 73744 | tf_op jit(solution)/shard_map/reduce_scatter | solution.py:229
  530.3 125.3 %reduce-scatter.15.cloned.1.call-done = f32[24,2304]{1,0:T(8,128)} async-done(((f32[768,2304]{1,0:T(8,128)}), f32[24,2304]{1,0:T(8,128)}) %reduce-scatter.15.cloned.1.call-update) | async-done | bytes 221200 | tf_op jit(solution)/shard_map/reduce_scatter | solution.py:227
  655.6 141.4 %reduce-scatter.19.cloned.1.call-done = f32[24,3072]{1,0:T(8,128)} async-done(((f32[768,3072]{1,0:T(8,128)}), f32[24,3072]{1,0:T(8,128)}) %reduce-scatter.19.cloned.1.call-update) | async-done | bytes 294928 | tf_op jit(solution)/shard_map/reduce_scatter | solution.py:230
  797.0 141.7 %reduce-scatter.21.cloned.1.call-done = f32[96,768]{1,0:T(8,128)} async-done(((f32[3072,768]{1,0:T(8,128)}), f32[96,768]{1,0:T(8,128)}) %reduce-scatter.21.cloned.1.call-update) | async-done | bytes 294928 | tf_op jit(solution)/shard_map/reduce_scatter | solution.py:232
  (193 shorter events, 27.2 us)
Async XLA Ops:
  7.2 85.0 %all-gather.11.cloned.1.call-start = ((), (), s32[]{:S(2)}) async-start(), calls=%async_computation.6 | async-start | bytes 3649536 | tf_op jit(solution)/shard_map/all_gather | solution.py:101
  7.9 211.8 %all-gather.15.cloned.1.call-start = ((), (), s32[]{:S(2)}) async-start(), calls=%async_computation.8 | async-start | bytes 1966080 | tf_op jit(solution)/shard_map/all_gather | solution.py:127
  9.2 83.0 %copy-start.40 = (f32[256]{0:T(256)}, f32[256]{0:T(256)S(1)}, u32[]{:S(2)}) copy-start(f32[256]{0:T(256)S(1)} %div.39) | copy-start | bytes 3076
  10.5 81.6 %copy-start.43 = (f32[256]{0:T(256)}, f32[256]{0:T(256)S(1)}, u32[]{:S(2)}) copy-start(f32[256]{0:T(256)S(1)} %rsqrt.20) | copy-start | bytes 3076
  92.2 3.3 copy-start.12
  92.2 4.2 copy-start.47
  95.4 41.8 %copy-start.50 = (s32[4]{0:T(128)S(1)}, s32[4]{0:T(128)}, u32[]{:S(2)}) copy-start(s32[4]{0:T(128)} %param.23) | copy-start | bytes 52
  95.5 42.4 %copy-start.51 = (bf16[96]{0:T(256)(128)(2,1)S(1)}, bf16[96]{0:T(256)(128)(2,1)}, u32[]{:S(2)}) copy-start(bf16[96]{0:T(256)(128)(2,1)} %param.19) | copy-start | bytes 580
  95.5 80.2 %copy-start.48 = (bf16[2,24]{1,0:T(2,128)(2,1)S(1)}, bf16[2,24]{1,0:T(2,128)(2,1)}, u32[]{:S(2)}) copy-start(bf16[2,24]{1,0:T(2,128)(2,1)} %param.21) | copy-start | bytes 292
  95.5 121.2 %copy-start.15 = (bf16[4,64,768]{2,1,0:T(8,128)(2,1)S(1)}, bf16[4,64,768]{2,1,0:T(8,128)(2,1)}, u32[]{:S(2)}) copy-start(bf16[4,64,768]{2,1,0:T(8,128)(2,1)} %param.22) | copy-start | bytes 1179652
  96.3 126.0 %all-gather.13.cloned.1.call-start = ((), (), s32[]{:S(2)}) async-start(), calls=%async_computation.7 | async-start | bytes 1966080 | tf_op jit(solution)/shard_map/all_gather | solution.py:128
  135.5 98.8 %all-gather.17.cloned.1.call-start = ((), (), s32[]{:S(2)}) async-start(), calls=%async_computation.9 | async-start | bytes 1216512 | tf_op jit(solution)/shard_map/all_gather | solution.py:103
  136.1 137.8 %all-gather.19.cloned.1.call-start = ((), (), s32[]{:S(2)}) async-start(), calls=%async_computation.10 | async-start | bytes 4866048 | tf_op jit(solution)/shard_map/all_gather | solution.py:104
  136.7 202.4 %all-gather.21.cloned.1.call-start = ((), (), s32[]{:S(2)}) async-start(), calls=%async_computation.11 | async-start | bytes 4866048 | tf_op jit(solution)/shard_map/all_gather | solution.py:106
  137.2 257.2 %reduce-scatter.13.cloned.1.call-start = ((), (), s32[]{:S(2)}) async-start(), calls=%async_computation.13 | async-start | bytes 1966080 | tf_op jit(solution)/shard_map/reduce_scatter | solution.py:198
  137.5 84.9 %copy-start.38 = (f32[256]{0:T(256)}, f32[256]{0:T(256)S(1)}, u32[]{:S(2)}) copy-start(f32[256]{0:T(256)S(1)} %mul.193) | copy-start | bytes 3076
  225.0 3.5 copy-start.10
  227.5 2.8 copy-start.27
  228.5 5.8 copy-start.8
  234.3 3.7 copy-start.28
  234.3 3.7 copy-start.30
  339.1 12.3 %copy-start.6 = (f32[256,768]{1,0:T(8,128)S(1)}, f32[256,768]{1,0:T(8,128)}, u32[]{:S(2)}) copy-start(f32[256,768]{1,0:T(8,128)} %copy-done.5) | copy-start | bytes 2359300
  339.1 12.3 %copy-start.33 = (f32[256]{0:T(256)S(1)}, f32[256]{0:T(256)}, u32[]{:S(2)}) copy-start(f32[256]{0:T(256)} %add_rsqrt_fusion.1) | copy-start | bytes 3076
  339.1 12.3 %copy-start.49 = (bf16[768,3072]{1,0:T(8,128)(2,1)S(1)}, bf16[768,3072]{1,0:T(8,128)(2,1)}, u32[]{:S(2)}) copy-start(bf16[768,3072]{1,0:T(8,128)(2,1)} %all-gather.19.cloned.1.call-done) | copy-start | bytes 14155780
  367.3 58.0 %reduce-scatter.11.cloned.1.call-start = ((), (), s32[]{:S(2)}) async-start(), calls=%async_computation.12 | async-start | bytes 1966080 | tf_op jit(solution)/shard_map/reduce_scatter | solution.py:192
  367.3 3.1 copy-start.26
  370.4 2.3 copy-start.9
  374.9 3.5 copy-start
  374.9 3.5 copy-start.2
  374.9 155.4 %reduce-scatter.17.cloned.1.call-start = ((), (), s32[]{:S(2)}) async-start(), calls=%async_computation.15 | async-start | bytes 2433024 | tf_op jit(solution)/shard_map/reduce_scatter | solution.py:229
  378.3 277.3 %reduce-scatter.15.cloned.1.call-start = ((), (), s32[]{:S(2)}) async-start(), calls=%async_computation.14 | async-start | bytes 7299072 | tf_op jit(solution)/shard_map/reduce_scatter | solution.py:227
  380.4 46.0 %copy-start.13 = (bf16[256,768]{1,0:T(8,128)(2,1)S(1)}, bf16[256,768]{1,0:T(8,128)(2,1)}, u32[]{:S(2)}) copy-start(bf16[256,768]{1,0:T(8,128)(2,1)} %copy-done.12) | copy-start | bytes 1179652
  382.5 48.0 %copy-start.21 = (bf16[256,768]{0,1:T(8,128)(2,1)}, bf16[256,768]{0,1:T(8,128)(2,1)S(1)}, u32[]{:S(2)}) copy-start(bf16[256,768]{0,1:T(8,128)(2,1)S(1)} %mul.214) | copy-start | bytes 1179652
  426.5 4.0 copy-start.19
  430.6 366.5 %reduce-scatter.19.cloned.1.call-start = ((), (), s32[]{:S(2)}) async-start(), calls=%async_computation.16 | async-start | bytes 9732096 | tf_op jit(solution)/shard_map/reduce_scatter | solution.py:230
  437.4 501.4 %reduce-scatter.21.cloned.1.call-start = ((), (), s32[]{:S(2)}) async-start(), calls=%async_computation.17 | async-start | bytes 9732096 | tf_op jit(solution)/shard_map/reduce_scatter | solution.py:232
  437.7 3.5 copy-start.18
  446.3 3.1 copy-start.32
  446.3 3.8 copy-start.31
  450.8 4.8 copy-start.23
  450.8 4.8 copy-start.14
  450.8 4.8 copy-start.20
  450.8 4.8 copy-start.22
  450.8 4.8 copy-start.41
  450.9 4.8 copy-start.44
  455.7 44.9 %copy-start.4 = (f32[256,768]{1,0:T(8,128)S(1)}, f32[256,768]{1,0:T(8,128)}, u32[]{:S(2)}) copy-start(f32[256,768]{1,0:T(8,128)} %copy-done.3) | copy-start | bytes 2359300
  455.8 44.8 %copy-start.42 = (f32[256]{0:T(256)S(1)}, f32[256]{0:T(256)}, u32[]{:S(2)}) copy-start(f32[256]{0:T(256)} %copy-done.40) | copy-start | bytes 3076
  455.8 44.8 %copy-start.45 = (f32[256]{0:T(256)S(1)}, f32[256]{0:T(256)}, u32[]{:S(2)}) copy-start(f32[256]{0:T(256)} %copy-done.43) | copy-start | bytes 3076
  (16 other events, 23.5 us)
Sparse Core Ops, SparseCore 0:
  10.9 62.8 all-gather.10
  96.4 17.2 all-gather.14
  135.6 16.3 all-gather.12
  154.8 53.8 all-gather.16
  211.4 62.4 all-gather.18
  276.7 62.3 all-gather.20
  367.4 26.9 reduce-scatter.12
  397.1 28.1 reduce-scatter.10
  431.2 99.1 reduce-scatter.16
  537.4 118.1 reduce-scatter.14
  662.1 134.9 reduce-scatter.18
  804.4 134.3 reduce-scatter.20
where the time goes:
time: 946 us
  waiting for transfers between devices  576 us (61%)
  blocking collectives  235 us (25%)
  matrix products  63.2 us (7%)
  local copies, waits for them, and re-layouts  39.8 us (4%)
  other arithmetic  16.1 us (2%)
  between operations  15 us (2%)
    reduce_scatter x1, waiting for transfers between devices, local(): lax.psum_scatter(grad_fc2, ('wide', 'blk'), scatter_dimension=0, tiled=True)  142 us
    reduce_scatter x1, waiting for transfers between devices, local(): lax.psum_scatter(grad_fc1, ('wide', 'blk'), scatter_dimension=0, tiled=True)  141 us
    reduce_scatter x1, waiting for transfers between devices, local(): lax.psum_scatter(grad_qkv, ('wide', 'blk'), scatter_dimension=0, tiled=True)  125 us
    unnamed x2, blocking collectives  77.2 us
    all_gather x1, waiting for transfers between devices, local(): lax.all_gather(fc2_weight, ('wide', 'blk'), axis=0, tiled=True)  59.5 us
    all_gather x1, blocking collectives, local(): lax.all_gather(norm_gain, ('wide', 'blk'), axis=1, tiled=True)  43.2 us
    all_gather x1, blocking collectives, local(): lax.all_gather(res_bias, ('wide', 'blk'), axis=1, tiled=True)  40.1 us
    all_gather x1, blocking collectives, local(): lax.all_gather(qv_bias, ('wide', 'blk'), axis=1, tiled=True)  37.9 us
  transfers between devices with their start and end apart: 12, of which 8 were waited for; matrix products, arithmetic and copies ran while one was open for 9% of the time, Pallas kernels for 0%

commit v1 on v0

--- a/solution.py
+++ b/solution.py
@@ -1,9 +1,12 @@
 from functools import partial
 import math
+import types
 
 import jax
 import jax.numpy as jnp
 from jax import lax
+from jax.experimental import pallas as pl
+from jax.experimental.pallas import tpu as pltpu
 from jax.sharding import PartitionSpec as P
 
 D = 768
@@ -247,6 +250,828 @@
     )
 
 
+MESH_ID = pl.DeviceIdType.MESH
+BF16 = jnp.bfloat16
+F32 = jnp.float32
+FF = 3072
+TOKENS = 256
+ROWS = 64
+ALL, LOW, HIGH = pl.ds(0, 4), pl.ds(0, 2), pl.ds(2, 2)
+
+
+def dot(left, right):
+    return lax.dot_general(left, right, (((1,), (0,)), ((), ())), preferred_element_type=F32)
+
+
+def dot_nt(left, right):
+    return lax.dot_general(left, right, (((1,), (1,)), ((), ())), preferred_element_type=F32)
+
+
+def dot_tn(left, right):
+    return lax.dot_general(left, right, (((0,), (0,)), ((), ())), preferred_element_type=F32)
+
+
+COPIES = 300
+
+
+def scratch_shapes():
+    def vm(*shape, dtype=BF16):
+        return pltpu.VMEM(shape, dtype)
+
+    return dict(
+        w_small=vm(4, 4, 16, 256),
+        w_qkv=vm(4, 4, 48, 2304),
+        w_out=vm(4, 4, 48, 768),
+        w_fc1=vm(4, 4, 48, 3072),
+        w_fc2=vm(4, 4, 2, 96, 768),
+        own_small=vm(16, 128, dtype=F32),
+        pair_rows=vm(48, 3072, dtype=F32),
+        pair_send=vm(24, 3072, dtype=F32),
+        par=vm(16, 768, dtype=F32),
+        par_fc1=vm(8, 3072, dtype=F32),
+        rows_in=vm(256, 768),
+        cot_in=vm(256, 768),
+        normed=vm(256, 768),
+        normed_t=vm(768, 256),
+        mixed=vm(256, 2304),
+        attended=vm(256, 768),
+        attended_t=vm(768, 256),
+        middle=vm(256, 768, dtype=F32),
+        normed2=vm(256, 768),
+        normed2_t=vm(768, 256),
+        slope=vm(256, 3072, dtype=F32),
+        active=vm(256, 3072),
+        active_t=vm(32, 96, 256),
+        g_branch2=vm(256, 768),
+        total=vm(256, 768, dtype=F32),
+        g_middle=vm(256, 768, dtype=F32),
+        g_branch=vm(256, 768),
+        g_attended=vm(256, 768),
+        g_mixed=vm(256, 2304),
+        enc_send=vm(256, 768),
+        gx_send=vm(256, 768),
+        gx_recv=vm(4, 64, 768),
+        sums=vm(16, 768, dtype=F32),
+        sums_fc1=vm(8, 3072, dtype=F32),
+        g_small=vm(4, 4, 16, 256),
+        g_fc1=vm(4, 4, 48, 3072),
+        g_fc2=vm(4, 4, 2, 96, 768),
+        pr_small=vm(4, 4, 16, 128),
+        pr_a=vm(4, 4, 48, 3072),
+        pr_fc2=vm(4, 4, 2, 96, 384),
+        dx_small=vm(2, 16, 128),
+        dx_a=vm(2, 48, 3072),
+        dx_fc2=vm(2, 2, 96, 384),
+        dy_small=vm(2, 16, 128),
+        dy_a=vm(2, 48, 3072),
+        dy_fc2=vm(2, 2, 96, 384),
+        px_small=vm(4, 16, 128),
+        px_a=vm(4, 48, 3072),
+        px_fc2=vm(4, 2, 96, 384),
+        py_small=vm(4, 16, 128),
+        py_a=vm(4, 48, 3072),
+        py_fc2=vm(4, 2, 96, 384),
+        pz_small=vm(3, 16, 128),
+        pz_a=vm(3, 48, 3072),
+        pz_fc2=vm(3, 2, 96, 384),
+        last_a=vm(48, 3072, dtype=F32),
+        last_fc2=vm(96, 384, dtype=F32),
+        send_sem=pltpu.SemaphoreType.DMA((COPIES,)),
+        recv_sem=pltpu.SemaphoreType.DMA((COPIES,)),
+    )
+
+
+def layer_kernel(
+    patches,
+    norm_gain,
+    norm_bias,
+    qkv_weight,
+    qv_bias,
+    out_weight,
+    fc1_weight,
+    fc1_bias,
+    fc2_weight,
+    res_bias,
+    cotangent,
+    frame_valid,
+    encoded,
+    grad_patches,
+    grad_gain,
+    grad_shift,
+    grad_qkv,
+    grad_qv,
+    grad_out,
+    grad_fc1,
+    grad_fc1_bias,
+    grad_fc2,
+    grad_res,
+    *scratch,
+):
+    s = types.SimpleNamespace(**dict(zip(scratch_shapes(), scratch)))
+    wide, blk = lax.axis_index("wide"), lax.axis_index("blk")
+    z, x = lax.div(wide, 2), lax.rem(wide, 2)
+    y, core = lax.div(blk, 2), lax.rem(blk, 2)
+    here, at_x, at_y, at_d = 2 * x + y, 2 * (1 - x) + y, 2 * x + 1 - y, 2 * (1 - x) + 1 - y
+    sibling = (wide, 2 * y + 1 - core)
+    x_peer = (2 * z + 1 - x, blk)
+    y_peer = (wide, 2 * (1 - y) + core)
+    y_cross = (wide, 2 * (1 - y) + 1 - core)
+    z_of = [lax.rem(z + step, 4) for step in range(4)]
+    z_peers = [(2 * z_of[step] + x, blk) for step in range(4)]
+    blk_peers = [(y, 1 - core), (1 - y, core), (1 - y, 1 - core)]
+
+    barrier = pltpu.get_barrier_semaphore()
+    peers = [sibling, x_peer, y_peer, y_cross] + z_peers[1:]
+    for peer in peers:
+        pl.semaphore_signal(barrier, inc=1, device_id=peer, device_id_type=MESH_ID)
+
+    started, waited = [], set()
+
+    def sent(copies):
+        for copy in copies:
+            if id(copy) not in waited:
+                waited.add(id(copy))
+                copy.wait_send()
+
+    def remote(source, target, peer):
+        spot = len(started)
+        copy = pltpu.make_async_remote_copy(
+            src_ref=source,
+            dst_ref=target,
+            send_sem=s.send_sem.at[spot],
+            recv_sem=s.recv_sem.at[spot],
+            device_id=peer,
+            device_id_type=MESH_ID,
+        )
+        copy.start()
+        started.append(copy)
+        return copy
+
+    def lanes(start, size):
+        return pl.ds(pl.multiple_of(start, 128), size)
+
+    s.own_small[...] = jnp.zeros((16, 128), F32)
+    s.sums[...] = jnp.zeros((16, D), F32)
+    s.own_small[0:2, 0:24] = norm_gain[...].astype(F32)
+    s.own_small[2:4, 0:24] = norm_bias[...].astype(F32)
+    s.own_small[4:6, 0:24] = qv_bias[...].astype(F32)
+    s.own_small[6:8, 0:24] = res_bias[...].astype(F32)
+    s.own_small[8:9, 0:96] = fc1_bias[...].astype(F32)
+    s.w_small[z, here, :, lanes(128 * core, 128)] = s.own_small[...].astype(BF16)
+    own_rows = pl.ds(pl.multiple_of(24 * core, 8), 24)
+    for ref, half, start in ((qkv_weight, 1152, 0), (out_weight, 384, 1152), (fc1_weight, 1536, 1536)):
+        s.pair_send[:, start : start + half] = ref[:, lanes((1 - core) * half, half)].astype(F32)
+        s.pair_rows[own_rows, start : start + half] = ref[:, lanes(core * half, half)].astype(F32)
+    s.w_fc2[z, here, core] = fc2_weight[...]
+
+    pl.semaphore_wait(barrier, len(peers))
+
+    pair = remote(s.pair_send, s.pair_rows.at[own_rows, :], sibling)
+
+    mine = pl.ds(pl.multiple_of(64 * blk, 64), 64)
+
+    def to_frames(source, target):
+        return [remote(source.at[2 * py + pc], target.at[mine, :], (wide, 2 * py + pc)) for py, pc in blk_peers]
+
+    rows_moved = to_frames(patches, s.rows_in)
+    s.rows_in[mine, :] = patches[blk]
+    s.cot_in[mine, :] = cotangent[blk]
+
+    class Gather:
+        def __init__(self, part):
+            self.part = part
+
+        def along_z(self):
+            own = self.part(z, here)
+            self.z = [remote(own, own, z_peers[step]) for step in (1, 2, 3)]
+
+        def to_plane(self):
+            for copy in self.z:
+                copy.wait_recv()
+            column = self.part(ALL, here)
+            self.x, self.y = remote(column, column, x_peer), remote(column, column, y_peer)
+            self.pair = [remote(column, column, sibling)]
+
+        def forward(self):
+            self.x.wait_recv()
+            some = self.part(LOW, at_x)
+            self.dy = remote(some, some, y_peer)
+            self.y.wait_recv()
+            some = self.part(HIGH, at_y)
+            self.dx = remote(some, some, x_peer)
+            for column in (self.part(ALL, at_x), self.part(ALL, at_y)):
+                self.pair.append(remote(column, column, sibling))
+
+        def last(self):
+            self.dy.wait_recv()
+            self.dx.wait_recv()
+            column = self.part(ALL, at_d)
+            self.pair.append(remote(column, column, sibling))
+
+        def done(self):
+            for copy in self.pair:
+                copy.wait_recv()
+
+        def copies(self):
+            return self.z + self.pair + [self.x, self.y, self.dx, self.dy]
+
+    def column_part(ref, half, start, size):
+        return lambda levels, place: ref.at[levels, place, :, lanes(half * core + start, size)]
+
+    def row_part(ref, start, size):
+        return lambda levels, place: ref.at[levels, place, core, pl.ds(start, size), :]
+
+    gathers = [Gather(column_part(s.w_small, 128, 0, 128))]
+    gathers += [Gather(column_part(s.w_qkv, 1152, 384 * j, 384)) for j in range(3)]
+    gathers += [Gather(column_part(s.w_out, 384, 0, 384))]
+    gathers += [Gather(column_part(s.w_fc1, 1536, 384 * j, 384)) for j in range(4)]
+    gathers += [Gather(row_part(s.w_fc2, 32 * j, 32)) for j in range(3)]
+
+    gathers[0].along_z()
+    pair.wait_recv()
+    for ref, half, start in ((s.w_qkv, 1152, 0), (s.w_out, 384, 1152), (s.w_fc1, 1536, 1536)):
+        ref[z, here, :, lanes(core * half, half)] = s.pair_rows[:, start : start + half].astype(BF16)
+    for gather in gathers[1:3]:
+        gather.along_z()
+    gathers[0].to_plane()
+
+
+    def by_rows(body, carry=None):
+        def step(i, held):
+            return body(pl.ds(pl.multiple_of(ROWS * i, ROWS), ROWS), held)
+
+        return lax.fori_loop(0, TOKENS // ROWS, step, carry)
+
+    def over(shape, axis):
+        return lax.broadcasted_iota(jnp.int32, shape, axis)
+
+    def piece24(columns):
+        return lax.shift_right_logical(columns * 43691, 20)
+
+    def piece96(columns):
+        return lax.shift_right_logical(columns * 10923, 20)
+
+    def spread24():
+        columns = over((128, D), 1)
+        return (columns - 24 * piece24(columns) == over((128, D), 0)).astype(F32).astype(BF16)
+
+    def spread96():
+        columns = over((128, FF), 1)
+        return (columns - 96 * piece96(columns) == over((128, FF), 0)).astype(F32).astype(BF16)
+
+    def unpack_small():
+        flat = s.w_small[...].reshape(256, 256)
+        chips = lax.shift_right_logical(over((256, D), 0), 4)
+        pieces = piece24(over((256, D), 1))
+        spread = spread24()
+        found = jnp.zeros((16, D), F32)
+        for side in (0, 1):
+            wide_rows = dot(flat[:, 128 * side : 128 * side + 128], spread)
+            wide_rows = jnp.where(pieces == 2 * chips + side, wide_rows, 0.0)
+            found = found + jnp.sum(wide_rows.reshape(16, 16, D), axis=0)
+        s.par[...] = found
+        pick = (over((16, 256), 1) == 16 * over((16, 256), 0) + 8).astype(F32).astype(BF16)
+        spread = spread96()
+        pieces = piece96(over((16, FF), 1))
+        found = jnp.zeros((16, FF), F32)
+        for side in (0, 1):
+            rows = dot(pick, flat[:, 128 * side : 128 * side + 128]).astype(BF16)
+            found = found + jnp.where(pieces == 2 * over((16, FF), 0) + side, dot(rows, spread), 0.0)
+        s.par_fc1[0:1, :] = jnp.sum(found, axis=0, keepdims=True)
+
+    def standardized(rows):
+        centered = rows - jnp.mean(rows, axis=-1, keepdims=True)
+        scale = lax.rsqrt(jnp.mean(centered * centered, axis=-1, keepdims=True) + EPSILON)
+        return centered * scale, scale
+
+    def first_norm():
+        def body(rows, _):
+            found, _ = standardized(s.rows_in[rows, :].astype(F32))
+            s.normed[rows, :] = (found * s.par[0:1, :] + s.par[2:3, :]).astype(BF16)
+            return 0
+
+        by_rows(body, 0)
+        s.normed_t[...] = s.normed[...].T
+
+    def project_qkv(tile):
+        start = 384 * tile
+        found = dot(s.normed[...], s.w_qkv[:, :, :, start : start + 384].reshape(D, 384))
+        if tile < 2:
+            found = (found + s.par[4:5, start : start + 384]) * 0.125
+        if tile >= 4:
+            found = found + s.par[5:6, start - 1536 : start - 1152]
+        s.mixed[:, start : start + 384] = found.astype(BF16)
+
+    def head_masks():
+        first = (over((TOKENS, 128), 1) < 64).astype(F32)
+        return first.astype(BF16), (1.0 - first).astype(BF16)
+
+    def softmax(scores):
+        expo = jnp.exp(scores - jnp.max(scores, axis=-1, keepdims=True))
+        return expo * (1.0 / jnp.sum(expo, axis=-1, keepdims=True))
+
+    def attend():
+        def body(two, _):
+            query, key, value = (s.mixed[:, lanes(128 * two + part, 128)] for part in (0, D, 2 * D))
+            found = jnp.zeros((TOKENS, 128), F32)
+            for mask in head_masks():
+                probs = softmax(dot_nt(query * mask, key)).astype(BF16)
+                found = found + dot(probs, value * mask)
+            s.attended[:, lanes(128 * two, 128)] = found.astype(BF16)
+            return 0
+
+        lax.fori_loop(0, HEADS // 2, body, 0)
+
+    def project_out():
+        s.middle[...] = dot(s.attended[...], s.w_out[...].reshape(D, D))
+
+        def body(rows, _):
+            middle = s.rows_in[rows, :].astype(F32) + (s.middle[rows, :] + s.par[6:7, :])
+            s.middle[rows, :] = middle
+            found, _ = standardized(middle)
+            s.normed2[rows, :] = (found * s.par[1:2, :] + s.par[3:4, :]).astype(BF16)
+            return 0
+
+        by_rows(body, 0)
+        s.attended_t[...] = s.attended[...].T
+        s.normed2_t[...] = s.normed2[...].T
+
+    def feed(j):
+        def body(side, _):
+            start = 1536 * side + 384 * j
+            columns = lanes(start, 384)
+            s.total[:, 0:384] = dot(s.normed2[...], s.w_fc1[:, :, :, columns].reshape(D, 384))
+
+            def gelu(rows, _):
+                hidden = s.total[rows, 0:384] + s.par_fc1[0:1, columns]
+                normal = 0.5 + 0.5 * lax.erf(hidden * (1.0 / math.sqrt(2.0)))
+                bell = jnp.exp(-0.5 * hidden * hidden) * (1.0 / math.sqrt(2.0 * math.pi))
+                s.slope[rows, columns] = normal + hidden * bell
+                s.active[rows, columns] = (hidden * normal).astype(BF16)
+                return 0
+
+            by_rows(gelu, 0)
+            s.active_t[pl.ds(16 * side + 4 * j, 4)] = s.active[:, columns].T.reshape(4, 96, 256)
+            return 0
+
+        lax.fori_loop(0, 2, body, 0)
+
+    def gather_step(at):
+        if at + 3 < len(gathers):
+            gathers[at + 3].along_z()
+        if at + 1 < len(gathers):
+            gathers[at + 1].to_plane()
+        if at < len(gathers):
+            gathers[at].forward()
+        if 0 <= at - 1 < len(gathers):
+            gathers[at - 1].last()
+        if 0 <= at - 2 < len(gathers):
+            gathers[at - 2].done()
+
+    gathers_at = [0]
+
+    def next_gather():
+        gather_step(gathers_at[0])
+        gathers_at[0] += 1
+
+    next_gather()
+    next_gather()
+    next_gather()
+    unpack_small()
+    for copy in rows_moved:
+        copy.wait_recv()
+    first_norm()
+    cot_moved = to_frames(cotangent, s.cot_in)
+    for j in range(3):
+        next_gather()
+        project_qkv(j)
+        project_qkv(j + 3)
+    attend()
+    next_gather()
+    project_out()
+    for j in range(4):
+        next_gather()
+        feed(j)
+
+    for copy in cot_moved:
+        copy.wait_recv()
+    valid = frame_valid[blk].astype(F32)
+
+    def mask_cotangent(rows, _):
+        s.g_branch2[rows, :] = (s.cot_in[rows, :].astype(F32) * valid).astype(BF16)
+        return 0
+
+    by_rows(mask_cotangent, 0)
+
+    class Scatter:
+        def __init__(self, own, other, pr, dx, dy, px, py, pz, finish):
+            self.own, self.other, self.finish = own, other, finish
+            self.pr, self.dx, self.dy, self.px, self.py, self.pz = pr, dx, dy, px, py, pz
+
+        def pair(self):
+            self.s = remote(self.other(), self.pr(ALL, ALL), sibling)
+
+        def plane(self):
+            self.s.wait_recv()
+
+            def add(level, _):
+                ref = self.own(level, ALL)
+                ref[...] = ref[...] + self.pr(level, ALL)[...]
+                return 0
+
+            lax.fori_loop(0, 4, add, 0)
+            self.a = remote(self.own(LOW, at_d), self.dx(), x_peer)
+            self.b = remote(self.own(HIGH, at_d), self.dy(), y_peer)
+            self.c = remote(self.own(LOW, at_x), self.px(LOW), x_peer)
+            self.d = remote(self.own(HIGH, at_y), self.py(HIGH), y_peer)
+
+        def plane2(self):
+            self.a.wait_recv()
+            ref = self.own(LOW, at_y)
+            ref[...] = ref[...] + self.dx()[...]
+            self.e = remote(ref, self.py(LOW), y_peer)
+            self.b.wait_recv()
+            ref = self.own(HIGH, at_x)
+            ref[...] = ref[...] + self.dy()[...]
+            self.f = remote(ref, self.px(HIGH), x_peer)
+
+        def along_z(self):
+            for copy in (self.c, self.d, self.e, self.f):
+                copy.wait_recv()
+
+            def add(level, _):
+                ref = self.own(level, here)
+                ref[...] = (
+                    ref[...].astype(F32)
+                    + self.px(level)[...].astype(F32)
+                    + self.py(level)[...].astype(F32)
+                ).astype(BF16)
+                return 0
+
+            lax.fori_loop(0, 4, add, 0)
+            self.z = [remote(self.own(z_of[step], here), self.pz(step - 1), z_peers[step]) for step in (1, 2, 3)]
+
+        def last(self):
+            for copy in self.z:
+                copy.wait_recv()
+            self.finish(self)
+
+        def summed(self, view):
+            found = view(self.own(z, here))[...].astype(F32)
+            for i in range(3):
+                found = found + view(self.pz(i))[...].astype(F32)
+            return found
+
+    def columns_of(ref, base, half, start, size):
+        def own(levels, places):
+            return ref.at[levels, places, :, lanes(base + half * core + start, size)]
+
+        def other():
+            return ref.at[:, :, :, lanes(base + half * (1 - core) + start, size)]
+
+        return own, other
+
+    def column_scatter(ref, base, half, start, size, spot, output):
+        at = pl.ds(spot, size)
+
+        def finish(scatter):
+            s.last_a[:, at] = scatter.summed(lambda ref: ref)
+            target = lanes(half * core + start, size)
+            other_rows = pl.ds(pl.multiple_of(24 * (1 - core), 8), 24)
+            finals.append(remote(s.last_a.at[other_rows, at], output.at[:, target], sibling))
+            output[:, target] = s.last_a[own_rows, at]
+
+        return Scatter(
+            *columns_of(ref, base, half, start, size),
+            lambda levels, places: s.pr_a.at[levels, places, :, at],
+            lambda: s.dx_a.at[:, :, at],
+            lambda: s.dy_a.at[:, :, at],
+            lambda levels: s.px_a.at[levels, :, at],
+            lambda levels: s.py_a.at[levels, :, at],
+            lambda i: s.pz_a.at[i, :, at],
+            finish,
+        )
+
+    def fc2_scatter(j):
+        rows = pl.ds(32 * j, 32)
+        half = lanes(384 * core, 384)
+
+        def finish(scatter):
+            s.last_fc2[rows, :] = scatter.summed(lambda ref: ref.at[1 - core])
+            finals.append(remote(s.last_fc2.at[rows, :], grad_fc2.at[rows, half], sibling))
+            grad_fc2[rows, half] = scatter.summed(lambda ref: ref.at[core])
+
+        return Scatter(
+            lambda levels, places: s.g_fc2.at[levels, places, :, rows, half],
+            lambda: s.g_fc2.at[:, :, :, rows, lanes(384 * (1 - core), 384)],
+            lambda levels, places: s.pr_fc2.at[levels, places, :, rows, :],
+            lambda: s.dx_fc2.at[:, :, rows, :],
+            lambda: s.dy_fc2.at[:, :, rows, :],
+            lambda levels: s.px_fc2.at[levels, :, rows, :],
+            lambda levels: s.py_fc2.at[levels, :, rows, :],
+            lambda i: s.pz_fc2.at[i, :, rows, :],
+            finish,
+        )
+
+    def small_finish(scatter):
+        found = scatter.summed(lambda ref: ref)
+        grad_gain[...] = found[0:2, 0:24]
+        grad_shift[...] = found[2:4, 0:24]
+        grad_qv[...] = found[4:6, 0:24]
+        grad_res[...] = found[6:8, 0:24]
+        grad_fc1_bias[...] = found[8:9, 0:96]
+
+    finals = []
+    scatters = [fc2_scatter(j) for j in range(3)]
+    scatters += [column_scatter(s.g_fc1, 0, 1536, 384 * j, 384, 384 * j, grad_fc1) for j in range(4)]
+    scatters += [column_scatter(s.w_fc1, 0, 384, 0, 384, 1536, grad_out)]
+    scatters += [column_scatter(s.w_fc1, 768, 1152, 384 * j, 384, 1920 + 384 * j, grad_qkv) for j in range(3)]
+    scatters += [
+        Scatter(
+            *columns_of(s.g_small, 0, 128, 0, 128),
+            lambda levels, places: s.pr_small.at[levels, places],
+            lambda: s.dx_small,
+            lambda: s.dy_small,
+            lambda levels: s.px_small.at[levels],
+            lambda levels: s.py_small.at[levels],
+            lambda i: s.pz_small.at[i],
+            small_finish,
+        )
+    ]
+
+    def scatter_step(at):
+        if at < len(scatters):
+            scatters[at].plane()
+        if 0 <= at - 1 < len(scatters):
+            scatters[at - 1].plane2()
+        if 0 <= at - 2 < len(scatters):
+            scatters[at - 2].along_z()
+        if 0 <= at - 3 < len(scatters):
+            scatters[at - 3].last()
+
+    scatters_at = [0]
+
+    def next_scatter():
+        scatter_step(scatters_at[0])
+        scatters_at[0] += 1
+
+    def weight_grad_fc2(j):
+        def body(turn, _):
+            columns = lanes(384 * (turn * core + (1 - turn) * (1 - core)), 384)
+            found = dot(s.active_t[:, 32 * j : 32 * j + 32, :].reshape(1024, 256), s.g_branch2[:, columns])
+            s.g_fc2[:, :, :, 32 * j : 32 * j + 32, columns] = found.astype(BF16).reshape(4, 4, 2, 32, 384)
+            return 0
+
+        lax.fori_loop(0, 2, body, 0)
+
+    def column_grad(left, right, start, ref, base, half, size):
+        def body(turn, _):
+            side = turn * core + (1 - turn) * (1 - core)
+            found = dot(left[...], right[:, lanes(half * side + start, size)])
+            ref[:, :, :, lanes(base + half * side + start, size)] = found.astype(BF16).reshape(4, 4, 48, size)
+            return 0
+
+        lax.fori_loop(0, 2, body, 0)
+
+    def column_sums(ref, width):
+        return jnp.sum(ref[...].astype(F32), axis=0, keepdims=True)
+
+    def feed_back():
+        s.total[...] = jnp.zeros((TOKENS, D), F32)
+
+        def body(level, _):
+            columns = lanes(D * level, D)
+            weight = s.w_fc2[level].reshape(D, D)
+            s.total[...] += dot(s.active[:, columns], weight)
+            s.g_middle[...] = dot_nt(s.g_branch2[...], weight)
+
+            def slope(rows, sums):
+                found = (s.g_middle[rows, :] * s.slope[rows, columns]).astype(BF16)
+                s.active[rows, columns] = found
+                return sums + jnp.sum(found.astype(F32), axis=0, keepdims=True)
+
+            s.sums_fc1[0:1, columns] = by_rows(slope, jnp.zeros((1, D), F32))
+            return 0
+
+        lax.fori_loop(0, 4, body, 0)
+
+        def finish(rows, sums):
+            found = valid * (s.middle[rows, :] + (s.total[rows, :] + s.par[7:8, :]))
+            s.enc_send[rows, :] = found.astype(BF16)
+            return sums + jnp.sum(s.g_branch2[rows, :].astype(F32), axis=0, keepdims=True)
+
+        s.sums[7:8, :] = by_rows(finish, jnp.zeros((1, D), F32))
+
+    def norm_back(upstream, found, scale, gain):
+        weighted = upstream * gain
+        return scale * (
+            weighted
+            - jnp.mean(weighted, axis=-1, keepdims=True)
+            - found * jnp.mean(weighted * found, axis=-1, keepdims=True)
+        )
+
+    def column_sum(values):
+        return jnp.sum(values, axis=0, keepdims=True)
+
+    def second_norm_back():
+        s.total[...] = jnp.zeros((TOKENS, D), F32)
+
+        def body(level, _):
+            columns = lanes(D * level, D)
+            s.total[...] += dot_nt(s.active[:, columns], s.w_fc1[:, :, :, columns].reshape(D, D))
+            return 0
+
+        lax.fori_loop(0, 4, body, 0)
+
+        def rows_back(rows, sums):
+            upstream = s.total[rows, :]
+            found, scale = standardized(s.middle[rows, :])
+            middle = s.g_branch2[rows, :].astype(F32) + norm_back(upstream, found, scale, s.par[1:2, :])
+            s.g_middle[rows, :] = middle
+            branch = middle.astype(BF16)
+            s.g_branch[rows, :] = branch
+            return (
+                sums[0] + column_sum(upstream * found),
+                sums[1] + column_sum(upstream),
+                sums[2] + column_sum(branch.astype(F32)),
+            )
+
+        empty = jnp.zeros((1, D), F32)
+        s.sums[1:2, :], s.sums[3:4, :], s.sums[6:7, :] = by_rows(rows_back, (empty, empty, empty))
+
+    def attend_back():
+        def body(two, _):
+            spots = [lanes(128 * two + part, 128) for part in (0, D, 2 * D)]
+            query, key, value = (s.mixed[:, spot] for spot in spots)
+            upstream = s.g_attended[:, spots[0]]
+            g_query, g_key, g_value = (jnp.zeros((TOKENS, 128), F32) for _ in range(3))
+            for mask in head_masks():
+                probs = softmax(dot_nt(query * mask, key))
+                g_probs = dot_nt(upstream * mask, value)
+                g_value = g_value + dot_tn(probs.astype(BF16), upstream * mask)
+                inner = jnp.sum(probs * g_probs, axis=-1, keepdims=True)
+                g_scores = (probs * (g_probs - inner)).astype(BF16)
+                g_query = g_query + dot(g_scores, key * mask)
+                g_key = g_key + dot_tn(g_scores, query * mask)
+            g_query = 0.125 * g_query.astype(BF16).astype(F32)
+            g_value = g_value.astype(BF16)
+            s.g_mixed[:, spots[0]] = g_query.astype(BF16)
+            s.g_mixed[:, spots[1]] = g_key.astype(BF16)
+            s.g_mixed[:, spots[2]] = g_value
+            s.sums[4:5, spots[0]] = column_sum(g_query)
+            s.sums[5:6, spots[0]] = column_sum(g_value.astype(F32))
+            return 0
+
+        lax.fori_loop(0, HEADS // 2, body, 0)
+
+    def first_norm_back():
+        s.total[...] = jnp.zeros((TOKENS, D), F32)
+
+        def body(level, _):
+            columns = lanes(D * level, D)
+            s.total[...] += dot_nt(s.g_mixed[:, columns], s.w_qkv[:, :, :, columns].reshape(D, D))
+            return 0
+
+        lax.fori_loop(0, 3, body, 0)
+
+        def rows_back(rows, sums):
+            upstream = s.total[rows, :]
+            found, scale = standardized(s.rows_in[rows, :].astype(F32))
+            result = s.g_middle[rows, :] + norm_back(upstream, found, scale, s.par[0:1, :])
+            s.gx_send[rows, :] = result.astype(BF16)
+            return (sums[0] + column_sum(upstream * found), sums[1] + column_sum(upstream))
+
+        empty = jnp.zeros((1, D), F32)
+        s.sums[0:1, :], s.sums[2:3, :] = by_rows(rows_back, (empty, empty))
+
+    def pack_small():
+        chips = lax.shift_right_logical(over((256, D), 0), 4)
+        pieces = piece24(over((256, D), 1))
+        spread = spread24()
+        rows = jnp.broadcast_to(s.sums[...][None], (16, 16, D)).reshape(256, D)
+        for side in (0, 1):
+            placed = dot_nt(jnp.where(pieces == 2 * chips + side, rows, 0.0).astype(BF16), spread)
+            s.g_small[:, :, :, 128 * side : 128 * side + 128] = placed.astype(BF16).reshape(4, 4, 16, 128)
+        put = (over((256, 16), 0) == 16 * over((256, 16), 1) + 8).astype(F32).astype(BF16)
+        spread = spread96()
+        pieces = piece96(over((16, FF), 1))
+        row = s.sums_fc1[0:1, :]
+        for side in (0, 1):
+            mine = pieces == 2 * over((16, FF), 0) + side
+            placed = dot_nt(jnp.where(mine, row, 0.0).astype(BF16), spread).astype(BF16)
+            here_ = s.g_small.at[:, :, :, pl.ds(128 * side, 128)]
+            here_[...] = here_[...] + dot(put, placed).astype(BF16).reshape(4, 4, 16, 128)
+
+    for j in range(3):
+        weight_grad_fc2(j)
+        scatters[j].pair()
+    next_gather()
+    next_scatter()
+    next_gather()
+    next_scatter()
+    next_gather()
+    next_scatter()
+    feed_back()
+
+    def to_patches(source, target):
+        return [
+            remote(
+                source.at[pl.ds(pl.multiple_of(64 * (2 * py + pc), 64), 64), :],
+                target.at[blk],
+                (wide, 2 * py + pc),
+            )
+            for py, pc in blk_peers
+        ]
+
+    moved = to_patches(s.enc_send, encoded)
+    encoded[blk] = s.enc_send[mine, :]
+    for j in range(4):
+        column_grad(s.normed2_t, s.active, 384 * j, s.g_fc1, 0, 1536, 384)
+        scatters[3 + j].pair()
+    next_scatter()
+    second_norm_back()
+    next_scatter()
+    for gather in gathers[5:9]:
+        sent(gather.copies())
+    column_grad(s.attended_t, s.g_branch, 0, s.w_fc1, 0, 384, 384)
+    scatters[7].pair()
+    s.g_attended[...] = dot_nt(s.g_branch[...], s.w_out[...].reshape(D, D)).astype(BF16)
+    next_scatter()
+    attend_back()
+    next_scatter()
+    for j in range(3):
+        column_grad(s.normed_t, s.g_mixed, 384 * j, s.w_fc1, D, 1152, 384)
+        scatters[8 + j].pair()
+    next_scatter()
+    first_norm_back()
+    moved += to_patches(s.gx_send, s.gx_recv)
+    s.gx_recv[blk] = s.gx_send[mine, :]
+    next_scatter()
+    pack_small()
+    scatters[11].pair()
+    while scatters_at[0] < len(scatters) + 3:
+        next_scatter()
+    for copy in moved + finals:
+        copy.wait_recv()
+    grad_patches[...] = s.gx_recv[...].astype(F32)
+    sent(started)
+
+
+def fast(
+    patches,
+    norm_gain,
+    norm_bias,
+    qkv_weight,
+    qv_bias,
+    out_weight,
+    fc1_weight,
+    fc1_bias,
+    fc2_weight,
+    res_bias,
+    cotangent,
+    frame_valid,
+):
+    outputs = [
+        ((4, 64, D), BF16),
+        ((4, 64, D), F32),
+        ((2, 24), F32),
+        ((2, 24), F32),
+        ((24, 3 * D), F32),
+        ((2, 24), F32),
+        ((24, D), F32),
+        ((24, FF), F32),
+        ((1, 96), F32),
+        ((96, D), F32),
+        ((2, 24), F32),
+    ]
+    vmem = pl.BlockSpec(memory_space=pltpu.VMEM)
+    found = list(pl.pallas_call(
+        layer_kernel,
+        out_shape=[jax.ShapeDtypeStruct(shape, dtype) for shape, dtype in outputs],
+        in_specs=[vmem] * 11 + [pl.BlockSpec(memory_space=pltpu.SMEM)],
+        out_specs=[vmem] * len(outputs),
+        scratch_shapes=list(scratch_shapes().values()),
+        compiler_params=pltpu.CompilerParams(
+            collective_id=0, has_side_effects=True, vmem_limit_bytes=63 * 2**20
+        ),
+    )(
+        patches,
+        norm_gain,
+        norm_bias,
+        qkv_weight,
+        qv_bias,
+        out_weight,
+        fc1_weight,
+        fc1_bias.reshape(1, 96),
+        fc2_weight,
+        res_bias,
+        cotangent,
+        frame_valid,
+    ))
+    found[8] = found[8].reshape(96)
+    return tuple(found)
+
+
 def solution(mesh):
     in_specs = (
         P("wide", "blk", None),
@@ -275,4 +1100,5 @@
         P(("wide", "blk"), None),
         P(None, ("wide", "blk")),
     )
-    return jax.shard_map(local, mesh=mesh, in_specs=in_specs, out_specs=out_specs, check_vma=False)
+    body = fast if dict(mesh.shape) == {"wide": 8, "blk": 4} else local
+    return jax.shard_map(body, mesh=mesh, in_specs=in_specs, out_specs=out_specs, check_vma=False)

time: 946 us -> 174 us (0.18)
  waiting for transfers between devices: 576 us -> 0 us
  blocking collectives: 235 us -> 0 us
  Pallas kernels: 0 us -> 165 us
  matrix products: 63.2 us -> 0 us
  local copies, waits for them, and re-layouts: 39.8 us -> 8.37 us
  other arithmetic: 16.1 us -> 0 us
  between operations: 15 us -> 0.68 us
    reduce_scatter x6 -> x0, waiting for transfers between devices: 479 us -> none  [the longest x1 142 us: local(): lax.psum_scatter(grad_fc2, ('wide', 'blk'), scatter_dimension=0, tiled=True)]
    pallas_call x0 -> x1, Pallas kernels: none -> 165 us  [fast(): pl.pallas_call(layer_kernel, out_shape=[jax.ShapeDtypeStruct(shape, dtype...]
    all_gather x4 -> x0, blocking collectives: 158 us -> none  [the longest x1 43.2 us: local(): lax.all_gather(norm_gain, ('wide', 'blk'), axis=1, tiled=True)]
    all_gather x6 -> x0, waiting for transfers between devices: 94.8 us -> none  [the longest x1 59.5 us: local(): lax.all_gather(fc2_weight, ('wide', 'blk'), axis=0, tiled=True)]
    unnamed x2 -> x0, blocking collectives: 77.2 us -> none
    dot_general x18 -> x0, matrix products: 63.2 us -> none  [the longest x1 12.3 us: local(): jnp.dot(grad_branch2, params[7].T, preferred_element_type=jnp.float32)]
    convert_element_type x14 -> x0, local copies, waits for them, and re-layouts: 11.3 us -> none  [the longest x2 4 us: local(): attended = attended.reshape(count, width).astype(jnp.bfloat16)]
  transfers between devices with their start and end apart: 12 -> 0, of which waited for: 8 -> 0; matrix products, arithmetic and copies ran while one was open for 9% -> 0% of each run, Pallas kernels for 0% -> 0%
where the time goes in v1:
time: 174 us
  Pallas kernels  165 us (95%)
  local copies, waits for them, and re-layouts  8.37 us (5%)
    pallas_call x1, Pallas kernels, fast(): pl.pallas_call(layer_kernel, out_shape=[jax.ShapeDtypeStruct(shape, dtype...  165 us
    unnamed x31, local copies, waits for them, and re-layouts  8.37 us

profile of v1, /device:TPU:0, one launch (start us, length us, event | category | flops | bytes accessed | tf_op | source)
XLA Modules:
  0.0 173.9 jit_solution(3992540234727047806)
XLA Ops:
  0.6 164.8 %shard_map.203 = (bf16[4,64,768]{2,1,0:T(8,128)(2,1)}, f32[4,64,768]{2,1,0:T(8,128)}, f32[2,24]{1,0:T(2,128)}, f32[2,24]{1,0:T(2,128)}, f32[24,2304]{1,0:T(8,128...) custom-call(bf16[4,64,768]{2,1,0:T(8,128)(2,1)} %patches.1, ...), custom_call_target="tpu_custom_call" | custom-call | tf_op jit(solution)/shard_map/pallas_call | solution.py:1048
  165.5 0.0 copy-start
  165.5 1.8 %copy.34 = bf16[4,64,768]{2,1,0:T(8,128)(2,1)} copy(bf16[4,64,768]{2,1,0:T(8,128)(2,1)} %get-tuple-element.44) | data formatting | bytes 786432
  167.3 0.0 copy-done
  167.3 0.0 copy-start.8
  167.3 0.0 copy-start.3
  167.3 0.9 copy.35
  168.2 0.0 copy-done.8
  168.2 0.0 copy-start.7
  168.2 0.6 copy.36
  168.8 0.1 copy-done.7
  168.9 0.6 copy.37
  169.4 0.0 copy-done.3
  169.4 0.0 copy-start.6
  169.4 0.0 copy-start.4
  169.4 0.0 copy-start.2
  169.4 0.7 copy.38
  170.1 0.0 copy-done.6
  170.1 0.6 copy.39
  170.7 0.0 copy-done.4
  170.7 0.6 copy.40
  171.3 0.0 copy-done.2
  171.3 0.0 copy-start.9
  171.3 0.0 copy-start.1
  171.3 0.7 copy.41
  172.1 0.0 copy-done.9
  172.1 0.5 copy.42
  172.6 0.0 copy-done.1
  172.6 0.0 copy-start.5
  172.6 0.7 copy.43
  173.3 0.0 copy-done.5
  173.3 0.6 copy.44
Async XLA Ops:
  165.5 1.9 %copy-start = (f32[4,64,768]{2,1,0:T(8,128)S(1)}, f32[4,64,768]{2,1,0:T(8,128)}, u32[]{:S(2)}) copy-start(f32[4,64,768]{2,1,0:T(8,128)} %get-tuple-element.45) | copy-start | bytes 2359300
  167.3 0.9 copy-start.8
  167.3 2.1 %copy-start.3 = (f32[24,2304]{1,0:T(8,128)S(1)}, f32[24,2304]{1,0:T(8,128)}, u32[]{:S(2)}) copy-start(f32[24,2304]{1,0:T(8,128)} %get-tuple-element.48) | copy-start | bytes 663556
  168.2 0.7 copy-start.7
  169.4 0.7 copy-start.6
  169.4 1.3 copy-start.4
  169.4 1.9 %copy-start.2 = (f32[24,3072]{1,0:T(8,128)S(1)}, f32[24,3072]{1,0:T(8,128)}, u32[]{:S(2)}) copy-start(f32[24,3072]{1,0:T(8,128)} %get-tuple-element.51) | copy-start | bytes 884740
  171.3 0.7 copy-start.9
  171.3 1.2 copy-start.1
  172.6 0.7 copy-start.5

commit v2 on v1

--- a/solution.py
+++ b/solution.py
@@ -256,7 +256,9 @@
 FF = 3072
 TOKENS = 256
 ROWS = 64
-ALL, LOW, HIGH = pl.ds(0, 4), pl.ds(0, 2), pl.ds(2, 2)
+ALL = pl.ds(0, 4)
+GATHER_WAYS = dict(q=(2, 2, 2), o=(2,), h=(2, 2, 1, 1), f=(2, 1, 0))
+SCATTER_WAYS = dict(f=(0, 3, 2), h=(3, 2, 3, 2), o=(2,), q=(2, 2, 2))
 
 
 def dot(left, right):
@@ -271,7 +273,7 @@
     return lax.dot_general(left, right, (((0,), (0,)), ((), ())), preferred_element_type=F32)
 
 
-COPIES = 300
+COPIES = 360
 
 
 def scratch_shapes():
@@ -319,12 +321,9 @@
         pr_small=vm(4, 4, 16, 128),
         pr_a=vm(4, 4, 48, 3072),
         pr_fc2=vm(4, 4, 2, 96, 384),
-        dx_small=vm(2, 16, 128),
-        dx_a=vm(2, 48, 3072),
-        dx_fc2=vm(2, 2, 96, 384),
-        dy_small=vm(2, 16, 128),
-        dy_a=vm(2, 48, 3072),
-        dy_fc2=vm(2, 2, 96, 384),
+        dx_small=vm(4, 16, 128),
+        dx_a=vm(4, 48, 3072),
+        dx_fc2=vm(4, 2, 96, 384),
         px_small=vm(4, 16, 128),
         px_a=vm(4, 48, 3072),
         px_fc2=vm(4, 2, 96, 384),
@@ -334,6 +333,7 @@
         pz_small=vm(3, 16, 128),
         pz_a=vm(3, 48, 3072),
         pz_fc2=vm(3, 2, 96, 384),
+        bz_fc2=vm(3, 4, 2, 96, 384),
         last_a=vm(48, 3072, dtype=F32),
         last_fc2=vm(96, 384, dtype=F32),
         send_sem=pltpu.SemaphoreType.DMA((COPIES,)),
@@ -375,13 +375,14 @@
     sibling = (wide, 2 * y + 1 - core)
     x_peer = (2 * z + 1 - x, blk)
     y_peer = (wide, 2 * (1 - y) + core)
+    d_peer = (2 * z + 1 - x, 2 * (1 - y) + core)
     y_cross = (wide, 2 * (1 - y) + 1 - core)
     z_of = [lax.rem(z + step, 4) for step in range(4)]
     z_peers = [(2 * z_of[step] + x, blk) for step in range(4)]
     blk_peers = [(y, 1 - core), (1 - y, core), (1 - y, 1 - core)]
 
     barrier = pltpu.get_barrier_semaphore()
-    peers = [sibling, x_peer, y_peer, y_cross] + z_peers[1:]
+    peers = [sibling, x_peer, y_peer, d_peer, y_cross] + z_peers[1:]
     for peer in peers:
         pl.semaphore_signal(barrier, inc=1, device_id=peer, device_id_type=MESH_ID)
 
@@ -433,47 +434,78 @@
     def to_frames(source, target):
         return [remote(source.at[2 * py + pc], target.at[mine, :], (wide, 2 * py + pc)) for py, pc in blk_peers]
 
-    rows_moved = to_frames(patches, s.rows_in)
     s.rows_in[mine, :] = patches[blk]
     s.cot_in[mine, :] = cotangent[blk]
 
     class Gather:
-        def __init__(self, part):
-            self.part = part
-
-        def along_z(self):
+        def __init__(self, part, low):
+            self.part, self.low, self.high = part, pl.ds(0, low), pl.ds(low, 4 - low)
+
+        def z(self):
             own = self.part(z, here)
-            self.z = [remote(own, own, z_peers[step]) for step in (1, 2, 3)]
-
-        def to_plane(self):
-            for copy in self.z:
+            self.z_copies = [remote(own, own, z_peers[step]) for step in (1, 2, 3)]
+
+        def p(self):
+            for copy in self.z_copies:
                 copy.wait_recv()
             column = self.part(ALL, here)
             self.x, self.y = remote(column, column, x_peer), remote(column, column, y_peer)
             self.pair = [remote(column, column, sibling)]
 
-        def forward(self):
+        def f(self):
             self.x.wait_recv()
-            some = self.part(LOW, at_x)
+            some = self.part(self.low, at_x)
             self.dy = remote(some, some, y_peer)
+            column = self.part(ALL, at_x)
+            self.pair.append(remote(column, column, sibling))
+
+        def g(self):
             self.y.wait_recv()
-            some = self.part(HIGH, at_y)
+            some = self.part(self.high, at_y)
             self.dx = remote(some, some, x_peer)
-            for column in (self.part(ALL, at_x), self.part(ALL, at_y)):
-                self.pair.append(remote(column, column, sibling))
-
-        def last(self):
+            column = self.part(ALL, at_y)
+            self.pair.append(remote(column, column, sibling))
+
+        def l(self):
             self.dy.wait_recv()
             self.dx.wait_recv()
             column = self.part(ALL, at_d)
             self.pair.append(remote(column, column, sibling))
 
-        def done(self):
+        def d(self):
             for copy in self.pair:
                 copy.wait_recv()
 
         def copies(self):
-            return self.z + self.pair + [self.x, self.y, self.dx, self.dy]
+            return self.z_copies + self.pair + [self.x, self.y, self.dx, self.dy]
+
+    class SquareGather:
+        def __init__(self, part):
+            self.part = part
+
+        def p(self):
+            own = self.part(z, here)
+            self.square = [remote(own, own, peer) for peer in (x_peer, y_peer, d_peer)]
+
+        def z(self):
+            for copy in self.square:
+                copy.wait_recv()
+            level = self.part(z, ALL)
+            self.z_copies = [remote(level, level, z_peers[step]) for step in (1, 2, 3)]
+            self.pair = [remote(level, level, sibling)]
+
+        def l(self):
+            for step, copy in zip((1, 2, 3), self.z_copies):
+                copy.wait_recv()
+                level = self.part(z_of[4 - step], ALL)
+                self.pair.append(remote(level, level, sibling))
+
+        def d(self):
+            for copy in self.pair:
+                copy.wait_recv()
+
+        def copies(self):
+            return self.square + self.z_copies + self.pair
 
     def column_part(ref, half, start, size):
         return lambda levels, place: ref.at[levels, place, :, lanes(half * core + start, size)]
@@ -481,20 +513,21 @@
     def row_part(ref, start, size):
         return lambda levels, place: ref.at[levels, place, core, pl.ds(start, size), :]
 
-    gathers = [Gather(column_part(s.w_small, 128, 0, 128))]
-    gathers += [Gather(column_part(s.w_qkv, 1152, 384 * j, 384)) for j in range(3)]
-    gathers += [Gather(column_part(s.w_out, 384, 0, 384))]
-    gathers += [Gather(column_part(s.w_fc1, 1536, 384 * j, 384)) for j in range(4)]
-    gathers += [Gather(row_part(s.w_fc2, 32 * j, 32)) for j in range(3)]
-
-    gathers[0].along_z()
+    def gather(part, way):
+        return Gather(part, way) if way else SquareGather(part)
+
+    gathers = {"s0": gather(column_part(s.w_small, 128, 0, 128), 2)}
+    for name, ref, half in (("q", s.w_qkv, 1152), ("o", s.w_out, 384), ("h", s.w_fc1, 1536)):
+        for j in range(half // 384):
+            gathers[name + str(j)] = gather(column_part(ref, half, 384 * j, 384), GATHER_WAYS[name][j])
+    for j, way in enumerate(GATHER_WAYS["f"]):
+        rows = 96 // len(GATHER_WAYS["f"])
+        gathers["f" + str(j)] = gather(row_part(s.w_fc2, rows * j, rows), way)
+
+
     pair.wait_recv()
     for ref, half, start in ((s.w_qkv, 1152, 0), (s.w_out, 384, 1152), (s.w_fc1, 1536, 1536)):
         ref[z, here, :, lanes(core * half, half)] = s.pair_rows[:, start : start + half].astype(BF16)
-    for gather in gathers[1:3]:
-        gather.along_z()
-    gathers[0].to_plane()
-
 
     def by_rows(body, carry=None):
         def step(i, held):
@@ -616,63 +649,27 @@
 
         lax.fori_loop(0, 2, body, 0)
 
-    def gather_step(at):
-        if at + 3 < len(gathers):
-            gathers[at + 3].along_z()
-        if at + 1 < len(gathers):
-            gathers[at + 1].to_plane()
-        if at < len(gathers):
-            gathers[at].forward()
-        if 0 <= at - 1 < len(gathers):
-            gathers[at - 1].last()
-        if 0 <= at - 2 < len(gathers):
-            gathers[at - 2].done()
-
-    gathers_at = [0]
-
-    def next_gather():
-        gather_step(gathers_at[0])
-        gathers_at[0] += 1
-
-    next_gather()
-    next_gather()
-    next_gather()
-    unpack_small()
-    for copy in rows_moved:
-        copy.wait_recv()
-    first_norm()
-    cot_moved = to_frames(cotangent, s.cot_in)
-    for j in range(3):
-        next_gather()
-        project_qkv(j)
-        project_qkv(j + 3)
-    attend()
-    next_gather()
-    project_out()
-    for j in range(4):
-        next_gather()
-        feed(j)
-
-    for copy in cot_moved:
-        copy.wait_recv()
     valid = frame_valid[blk].astype(F32)
 
-    def mask_cotangent(rows, _):
-        s.g_branch2[rows, :] = (s.cot_in[rows, :].astype(F32) * valid).astype(BF16)
-        return 0
-
-    by_rows(mask_cotangent, 0)
+    def mask_cotangent():
+        def body(rows, _):
+            s.g_branch2[rows, :] = (s.cot_in[rows, :].astype(F32) * valid).astype(BF16)
+            return 0
+
+        by_rows(body, 0)
+
 
     class Scatter:
-        def __init__(self, own, other, pr, dx, dy, px, py, pz, finish):
+        def __init__(self, own, other, pr, dx, dy, px, py, pz, finish, low=2):
             self.own, self.other, self.finish = own, other, finish
             self.pr, self.dx, self.dy, self.px, self.py, self.pz = pr, dx, dy, px, py, pz
-
-        def pair(self):
-            self.s = remote(self.other(), self.pr(ALL, ALL), sibling)
-
-        def plane(self):
-            self.s.wait_recv()
+            self.low, self.high = pl.ds(0, low), pl.ds(low, 4 - low)
+
+        def s(self):
+            self.pair = remote(self.other(), self.pr(ALL, ALL), sibling)
+
+        def add_pair(self):
+            self.pair.wait_recv()
 
             def add(level, _):
                 ref = self.own(level, ALL)
@@ -680,23 +677,29 @@
                 return 0
 
             lax.fori_loop(0, 4, add, 0)
-            self.a = remote(self.own(LOW, at_d), self.dx(), x_peer)
-            self.b = remote(self.own(HIGH, at_d), self.dy(), y_peer)
-            self.c = remote(self.own(LOW, at_x), self.px(LOW), x_peer)
-            self.d = remote(self.own(HIGH, at_y), self.py(HIGH), y_peer)
-
-        def plane2(self):
+
+        def p(self):
+            self.add_pair()
+            low, high = self.low, self.high
+            self.a = remote(self.own(low, at_d), self.dx(low), x_peer)
+            self.b = remote(self.own(high, at_d), self.dy(high), y_peer)
+            self.c = remote(self.own(low, at_x), self.px(low), x_peer)
+            self.d = remote(self.own(high, at_y), self.py(high), y_peer)
+
+        def f(self):
             self.a.wait_recv()
-            ref = self.own(LOW, at_y)
-            ref[...] = ref[...] + self.dx()[...]
-            self.e = remote(ref, self.py(LOW), y_peer)
+            ref = self.own(self.low, at_y)
+            ref[...] = ref[...] + self.dx(self.low)[...]
+            self.e = remote(ref, self.py(self.low), y_peer)
+
+        def g(self):
             self.b.wait_recv()
-            ref = self.own(HIGH, at_x)
-            ref[...] = ref[...] + self.dy()[...]
-            self.f = remote(ref, self.px(HIGH), x_peer)
-
-        def along_z(self):
-            for copy in (self.c, self.d, self.e, self.f):
+            ref = self.own(self.high, at_x)
+            ref[...] = ref[...] + self.dy(self.high)[...]
+            self.f_copy = remote(ref, self.px(self.high), x_peer)
+
+        def z(self):
+            for copy in (self.c, self.d, self.e, self.f_copy):
                 copy.wait_recv()
 
             def add(level, _):
@@ -709,10 +712,12 @@
                 return 0
 
             lax.fori_loop(0, 4, add, 0)
-            self.z = [remote(self.own(z_of[step], here), self.pz(step - 1), z_peers[step]) for step in (1, 2, 3)]
-
-        def last(self):
-            for copy in self.z:
+            self.z_copies = [
+                remote(self.own(z_of[step], here), self.pz(step - 1), z_peers[step]) for step in (1, 2, 3)
+            ]
+
+        def l(self):
+            for copy in self.z_copies:
                 copy.wait_recv()
             self.finish(self)
 
@@ -722,6 +727,40 @@
                 found = found + view(self.pz(i))[...].astype(F32)
             return found
 
+    class SquareScatter(Scatter):
+        def __init__(self, own, other, pr, bz, pz, finish):
+            self.own, self.other, self.finish = own, other, finish
+            self.pr, self.bz, self.pz = pr, bz, pz
+
+        def z(self):
+            self.add_pair()
+            self.z_copies = [
+                remote(self.own(z_of[step], ALL), self.bz(step - 1, ALL), z_peers[step]) for step in (1, 2, 3)
+            ]
+
+        def p(self):
+            for copy in self.z_copies:
+                copy.wait_recv()
+
+            def add(place, _):
+                ref = self.own(z, place)
+                found = ref[...].astype(F32)
+                for i in range(3):
+                    found = found + self.bz(i, place)[...].astype(F32)
+                ref[...] = found.astype(BF16)
+                return 0
+
+            lax.fori_loop(0, 4, add, 0)
+            targets = ((at_x, x_peer), (at_y, y_peer), (at_d, d_peer))
+            self.square = [
+                remote(self.own(z, place), self.pz(i), peer) for i, (place, peer) in enumerate(targets)
+            ]
+
+        def l(self):
+            for copy in self.square:
+                copy.wait_recv()
+            self.finish(self)
+
     def columns_of(ref, base, half, start, size):
         def own(levels, places):
             return ref.at[levels, places, :, lanes(base + half * core + start, size)]
@@ -731,7 +770,7 @@
 
         return own, other
 
-    def column_scatter(ref, base, half, start, size, spot, output):
+    def column_scatter(ref, base, half, start, size, spot, output, way):
         at = pl.ds(spot, size)
 
         def finish(scatter):
@@ -741,19 +780,29 @@
             finals.append(remote(s.last_a.at[other_rows, at], output.at[:, target], sibling))
             output[:, target] = s.last_a[own_rows, at]
 
+        if not way:
+            extra = pl.ds(spot, size)
+            return SquareScatter(
+                *columns_of(ref, base, half, start, size),
+                lambda levels, places: s.pr_a.at[levels, places, :, at],
+                lambda i, places: s.bz_a.at[i, places, :, extra],
+                lambda i: s.pz_a.at[i, :, at],
+                finish,
+            )
         return Scatter(
             *columns_of(ref, base, half, start, size),
             lambda levels, places: s.pr_a.at[levels, places, :, at],
-            lambda: s.dx_a.at[:, :, at],
-            lambda: s.dy_a.at[:, :, at],
+            lambda levels: s.dx_a.at[levels, :, at],
+            lambda levels: s.dx_a.at[levels, :, at],
             lambda levels: s.px_a.at[levels, :, at],
             lambda levels: s.py_a.at[levels, :, at],
             lambda i: s.pz_a.at[i, :, at],
             finish,
+            way,
         )
 
-    def fc2_scatter(j):
-        rows = pl.ds(32 * j, 32)
+    def fc2_scatter(j, size, way):
+        rows = pl.ds(size * j, size)
         half = lanes(384 * core, 384)
 
         def finish(scatter):
@@ -761,16 +810,23 @@
             finals.append(remote(s.last_fc2.at[rows, :], grad_fc2.at[rows, half], sibling))
             grad_fc2[rows, half] = scatter.summed(lambda ref: ref.at[core])
 
+        own = lambda levels, places: s.g_fc2.at[levels, places, :, rows, half]
+        other = lambda: s.g_fc2.at[:, :, :, rows, lanes(384 * (1 - core), 384)]
+        pr = lambda levels, places: s.pr_fc2.at[levels, places, :, rows, :]
+        pz = lambda i: s.pz_fc2.at[i, :, rows, :]
+        if not way:
+            return SquareScatter(own, other, pr, lambda i, places: s.bz_fc2.at[i, places, :, rows, :], pz, finish)
         return Scatter(
-            lambda levels, places: s.g_fc2.at[levels, places, :, rows, half],
-            lambda: s.g_fc2.at[:, :, :, rows, lanes(384 * (1 - core), 384)],
-            lambda levels, places: s.pr_fc2.at[levels, places, :, rows, :],
-            lambda: s.dx_fc2.at[:, :, rows, :],
-            lambda: s.dy_fc2.at[:, :, rows, :],
+            own,
+            other,
+            pr,
+            lambda levels: s.dx_fc2.at[levels, :, rows, :],
+            lambda levels: s.dx_fc2.at[levels, :, rows, :],
             lambda levels: s.px_fc2.at[levels, :, rows, :],
             lambda levels: s.py_fc2.at[levels, :, rows, :],
-            lambda i: s.pz_fc2.at[i, :, rows, :],
+            pz,
             finish,
+            way,
         )
 
     def small_finish(scatter):
@@ -782,44 +838,38 @@
         grad_fc1_bias[...] = found[8:9, 0:96]
 
     finals = []
-    scatters = [fc2_scatter(j) for j in range(3)]
-    scatters += [column_scatter(s.g_fc1, 0, 1536, 384 * j, 384, 384 * j, grad_fc1) for j in range(4)]
-    scatters += [column_scatter(s.w_fc1, 0, 384, 0, 384, 1536, grad_out)]
-    scatters += [column_scatter(s.w_fc1, 768, 1152, 384 * j, 384, 1920 + 384 * j, grad_qkv) for j in range(3)]
-    scatters += [
-        Scatter(
-            *columns_of(s.g_small, 0, 128, 0, 128),
-            lambda levels, places: s.pr_small.at[levels, places],
-            lambda: s.dx_small,
-            lambda: s.dy_small,
-            lambda levels: s.px_small.at[levels],
-            lambda levels: s.py_small.at[levels],
-            lambda i: s.pz_small.at[i],
-            small_finish,
-        )
-    ]
-
-    def scatter_step(at):
-        if at < len(scatters):
-            scatters[at].plane()
-        if 0 <= at - 1 < len(scatters):
-            scatters[at - 1].plane2()
-        if 0 <= at - 2 < len(scatters):
-            scatters[at - 2].along_z()
-        if 0 <= at - 3 < len(scatters):
-            scatters[at - 3].last()
-
-    scatters_at = [0]
-
-    def next_scatter():
-        scatter_step(scatters_at[0])
-        scatters_at[0] += 1
+    scatters = {}
+    for j, way in enumerate(SCATTER_WAYS["f"]):
+        scatters["f" + str(j)] = fc2_scatter(j, 96 // len(SCATTER_WAYS["f"]), way)
+    for name, ref, base, half, spot, output in (
+        ("h", s.g_fc1, 0, 1536, 0, grad_fc1),
+        ("o", s.w_fc1, 0, 384, 1536, grad_out),
+        ("q", s.w_fc1, D, 1152, 1920, grad_qkv),
+    ):
+        for j in range(half // 384):
+            way = SCATTER_WAYS[name][j]
+            scatters[name + str(j)] = column_scatter(
+                ref, base, half, 384 * j, 384, spot + 384 * j, output, way
+            )
+    scatters["s0"] = Scatter(
+        *columns_of(s.g_small, 0, 128, 0, 128),
+        lambda levels, places: s.pr_small.at[levels, places],
+        lambda levels: s.dx_small.at[levels],
+        lambda levels: s.dx_small.at[levels],
+        lambda levels: s.px_small.at[levels],
+        lambda levels: s.py_small.at[levels],
+        lambda i: s.pz_small.at[i],
+        small_finish,
+    )
 
     def weight_grad_fc2(j):
+        size = 96 // len(SCATTER_WAYS["f"])
+        rows = pl.ds(size * j, size)
+
         def body(turn, _):
             columns = lanes(384 * (turn * core + (1 - turn) * (1 - core)), 384)
-            found = dot(s.active_t[:, 32 * j : 32 * j + 32, :].reshape(1024, 256), s.g_branch2[:, columns])
-            s.g_fc2[:, :, :, 32 * j : 32 * j + 32, columns] = found.astype(BF16).reshape(4, 4, 2, 32, 384)
+            found = dot(s.active_t[:, rows, :].reshape(32 * size, 256), s.g_branch2[:, columns])
+            s.g_fc2[:, :, :, rows, columns] = found.astype(BF16).reshape(4, 4, 2, size, 384)
             return 0
 
         lax.fori_loop(0, 2, body, 0)
@@ -962,17 +1012,6 @@
             here_ = s.g_small.at[:, :, :, pl.ds(128 * side, 128)]
             here_[...] = here_[...] + dot(put, placed).astype(BF16).reshape(4, 4, 16, 128)
 
-    for j in range(3):
-        weight_grad_fc2(j)
-        scatters[j].pair()
-    next_gather()
-    next_scatter()
-    next_gather()
-    next_scatter()
-    next_gather()
-    next_scatter()
-    feed_back()
-
     def to_patches(source, target):
         return [
             remote(
@@ -983,38 +1022,253 @@
             for py, pc in blk_peers
         ]
 
-    moved = to_patches(s.enc_send, encoded)
-    encoded[blk] = s.enc_send[mine, :]
-    for j in range(4):
+    moved = {}
+
+    def send_rows():
+        moved["rows"] = to_frames(patches, s.rows_in)
+
+    def send_cotangent():
+        moved["cot"] = to_frames(cotangent, s.cot_in)
+
+    def received(name):
+        for copy in moved.pop(name):
+            copy.wait_recv()
+
+    def start_norm():
+        received("rows")
+        first_norm()
+
+    def start_cotangent():
+        received("cot")
+        mask_cotangent()
+
+    def send_encoded():
+        moved["enc"] = to_patches(s.enc_send, encoded)
+        encoded[blk] = s.enc_send[mine, :]
+
+    def send_grad_rows():
+        moved["grad"] = to_patches(s.gx_send, s.gx_recv)
+        s.gx_recv[blk] = s.gx_send[mine, :]
+
+    def free_fc1():
+        for name in ("h0", "h1", "h2", "h3"):
+            sent(gathers[name].copies())
+
+    def project_attended():
+        s.g_attended[...] = dot_nt(s.g_branch[...], s.w_out[...].reshape(D, D)).astype(BF16)
+
+    def project_both(j):
+        project_qkv(j)
+        project_qkv(j + 3)
+
+    def grad_fc1_weight(j):
         column_grad(s.normed2_t, s.active, 384 * j, s.g_fc1, 0, 1536, 384)
-        scatters[3 + j].pair()
-    next_scatter()
+
+    def grad_out_weight():
+        column_grad(s.attended_t, s.g_branch, 0, s.w_fc1, 0, 384, 384)
+
+    def grad_qkv_weight(j):
+        column_grad(s.normed_t, s.g_mixed, 384 * j, s.w_fc1, D, 1152, 384)
+
+    g, r = types.SimpleNamespace(**gathers), types.SimpleNamespace(**scatters)
+    g.f2.p()
+    g.s0.z()
+    g.q0.z()
+    send_rows()
+    g.q1.z()
+    g.s0.p()
+    g.q2.z()
+    g.q0.p()
+    g.s0.f()
+    g.o0.z()
+    g.h2.z()
+    g.q1.p()
+    g.q2.p()
+    g.q1.f()
+    g.q0.f()
+    g.q1.g()
+    g.q0.g()
+    g.h0.z()
+    g.o0.p()
+    g.h2.p()
+    g.h3.z()
+    g.q1.l()
+    g.s0.g()
+    g.q0.l()
+    g.h1.z()
+    g.f0.z()
+    g.q0.d()
+    g.h0.p()
+    g.o0.f()
+    g.h2.f()
+    g.q2.f()
+    g.h1.p()
+    g.s0.l()
+    g.f1.z()
+    g.q2.g()
+    send_cotangent()
+    g.s0.d()
+    unpack_small()
+    g.h3.p()
+    g.o0.g()
+    g.h2.g()
+    start_norm()
+    g.h0.f()
+    project_both(0)
+    g.f2.z()
+    g.h1.f()
+    g.f1.p()
+    g.h1.g()
+    g.h3.f()
+    g.q2.l()
+    g.o0.l()
+    g.h0.g()
+    g.q2.d()
+    g.f0.p()
+    g.q1.d()
+    project_both(1)
+    project_both(2)
+    g.h2.l()
+    g.o0.d()
+    attend()
+    g.h3.g()
+    project_out()
+    g.h1.l()
+    g.h2.d()
+    g.h1.d()
+    g.h0.l()
+    start_cotangent()
+    feed(1)
+    g.f1.f()
+    g.h0.d()
+    feed(2)
+    g.f1.g()
+    g.f0.f()
+    g.f2.l()
+    feed(0)
+    g.h3.l()
+    g.h3.d()
+    g.f0.g()
+    feed(3)
+    g.f1.l()
+    weight_grad_fc2(1)
+    g.f2.d()
+    r.f1.s()
+    weight_grad_fc2(2)
+    r.f2.s()
+    weight_grad_fc2(0)
+    g.f0.l()
+    r.f1.p()
+    r.f0.s()
+    r.f2.p()
+    g.f1.d()
+    g.f0.d()
+    feed_back()
+    send_encoded()
+    r.f1.f()
+    r.f1.g()
+    grad_fc1_weight(0)
+    r.f0.z()
+    r.h0.s()
+    grad_fc1_weight(2)
+    grad_fc1_weight(3)
+    r.f2.f()
+    r.h0.p()
+    r.f2.g()
+    r.h3.s()
+    r.h2.s()
     second_norm_back()
-    next_scatter()
-    for gather in gathers[5:9]:
-        sent(gather.copies())
-    column_grad(s.attended_t, s.g_branch, 0, s.w_fc1, 0, 384, 384)
-    scatters[7].pair()
-    s.g_attended[...] = dot_nt(s.g_branch[...], s.w_out[...].reshape(D, D)).astype(BF16)
-    next_scatter()
+    project_attended()
+    r.h3.p()
+    r.h2.p()
+    free_fc1()
+    r.h0.f()
     attend_back()
-    next_scatter()
-    for j in range(3):
-        column_grad(s.normed_t, s.g_mixed, 384 * j, s.w_fc1, D, 1152, 384)
-        scatters[8 + j].pair()
-    next_scatter()
+    r.f2.z()
+    r.h3.f()
+    r.h0.g()
+    r.h3.g()
+    grad_qkv_weight(1)
+    grad_out_weight()
+    r.h2.f()
+    r.q1.s()
+    r.f1.z()
+    r.h2.g()
+    grad_qkv_weight(0)
+    r.o0.s()
+    r.q1.p()
+    r.q0.s()
+    grad_fc1_weight(1)
+    r.q0.p()
+    r.h3.z()
+    grad_qkv_weight(2)
+    r.q1.f()
+    r.q2.s()
+    r.h1.s()
+    r.q1.g()
+    r.o0.p()
+    r.h0.z()
+    r.h1.p()
+    r.h2.z()
     first_norm_back()
-    moved += to_patches(s.gx_send, s.gx_recv)
-    s.gx_recv[blk] = s.gx_send[mine, :]
-    next_scatter()
+    r.q1.z()
     pack_small()
-    scatters[11].pair()
-    while scatters_at[0] < len(scatters) + 3:
-        next_scatter()
-    for copy in moved + finals:
+    r.f2.l()
+    r.s0.s()
+    r.h0.l()
+    r.o0.f()
+    r.o0.g()
+    r.s0.p()
+    r.h1.f()
+    r.q0.f()
+    r.f1.l()
+    r.h1.g()
+    r.q0.g()
+    r.o0.z()
+    r.s0.f()
+    r.q2.p()
+    r.h1.z()
+    r.q2.f()
+    r.h3.l()
+    r.q2.g()
+    r.h2.l()
+    r.q0.z()
+    r.f0.p()
+    send_grad_rows()
+    r.q1.l()
+    r.o0.l()
+    r.s0.g()
+    r.q2.z()
+    r.f0.l()
+    r.h1.l()
+    r.s0.z()
+    r.q0.l()
+    r.q2.l()
+    r.s0.l()
+    for name in list(moved):
+        received(name)
+    for copy in finals:
         copy.wait_recv()
     grad_patches[...] = s.gx_recv[...].astype(F32)
     sent(started)
+
+
+def emit_kernel(*refs):
+    count = len(refs) // 2
+    for i in range(count):
+        refs[count + i][...] = refs[i][...].astype(refs[count + i].dtype)
+
+
+def emit(arrays):
+    vmem = pl.BlockSpec(memory_space=pltpu.VMEM)
+    return list(
+        pl.pallas_call(
+            emit_kernel,
+            out_shape=[jax.ShapeDtypeStruct(a.shape, a.dtype) for a in arrays],
+            in_specs=[vmem] * len(arrays),
+            out_specs=[vmem] * len(arrays),
+        )(*arrays)
+    )
 
 
 def fast(
@@ -1068,6 +1322,7 @@
         cotangent,
         frame_valid,
     ))
+    found = emit(found)
     found[8] = found[8].reshape(96)
     return tuple(found)
 

time: 174 us -> 148 us (0.85)
  Pallas kernels: 165 us -> 147 us
  local copies, waits for them, and re-layouts: 8.37 us -> 0 us
    pallas_call x1, Pallas kernels: 165 us -> 144 us  [fast(): pl.pallas_call(layer_kernel, out_shape=[jax.ShapeDtypeStruct(shape, dtype...]
    unnamed x31 -> x0, local copies, waits for them, and re-layouts: 8.37 us -> none
    pallas_call x0 -> x1, Pallas kernels: none -> 2.87 us  [emit(): pl.pallas_call(emit_kernel, out_shape=[jax.ShapeDtypeStruct(a.shape, a.dt...]
where the time goes in v2:
time: 148 us
  Pallas kernels  147 us (99%)
    pallas_call x1, Pallas kernels, fast(): pl.pallas_call(layer_kernel, out_shape=[jax.ShapeDtypeStruct(shape, dtype...  144 us

profile of v2, /device:TPU:0, one launch (start us, length us, event | category | flops | bytes accessed | tf_op | source)
XLA Modules:
  0.0 147.6 jit_solution(5210560956899836951)
XLA Ops:
  0.6 143.9 %shard_map.203 = (bf16[4,64,768]{2,1,0:T(8,128)(2,1)}, f32[4,64,768]{2,1,0:T(8,128)}, f32[2,24]{1,0:T(2,128)}, f32[2,24]{1,0:T(2,128)}, f32[24,2304]{1,0:T(8,128...) custom-call(bf16[4,64,768]{2,1,0:T(8,128)(2,1)} %patches.1, ...), custom_call_target="tpu_custom_call" | custom-call | tf_op jit(solution)/shard_map/pallas_call | solution.py:1302
  144.5 2.9 %shard_map.204 = (bf16[4,64,768]{2,1,0:T(8,128)(2,1)}, f32[4,64,768]{2,1,0:T(8,128)}, f32[2,24]{1,0:T(2,128)}, f32[2,24]{1,0:T(2,128)}, f32[24,2304]{1,0:T(8,128...) custom-call(bf16[4,64,768]{2,1,0:T(8,128)(2,1)} %get-tuple-element.3, ...), custom_call_target="tpu_custom_call" | custom-call | tf_op jit(solution)/shard_map/pallas_call | solution.py:1265

commit v3 on v2

--- a/solution.py
+++ b/solution.py
@@ -256,9 +256,10 @@
 FF = 3072
 TOKENS = 256
 ROWS = 64
-ALL = pl.ds(0, 4)
-GATHER_WAYS = dict(q=(2, 2, 2), o=(2,), h=(2, 2, 1, 1), f=(2, 1, 0))
-SCATTER_WAYS = dict(f=(0, 3, 2), h=(3, 2, 3, 2), o=(2,), q=(2, 2, 2))
+ALL, BOTH = pl.ds(0, 4), pl.ds(0, 2)
+GATHER_WAYS = dict(q=(1, 2, 2), o=(2,))
+SCATTER_WAYS = dict(o=(2,), q=(2, 2, 3))
+FC2_GATHERS, FC2_SCATTERS = 3, 3
 
 
 def dot(left, right):
@@ -274,6 +275,7 @@
 
 
 COPIES = 360
+FC1_OUTPUT = 7
 
 
 def scratch_shapes():
@@ -284,13 +286,14 @@
         w_small=vm(4, 4, 16, 256),
         w_qkv=vm(4, 4, 48, 2304),
         w_out=vm(4, 4, 48, 768),
-        w_fc1=vm(4, 4, 48, 3072),
-        w_fc2=vm(4, 4, 2, 96, 768),
+        w_fc1=vm(4, 4, 48, 1536),
+        w_fc2=vm(4, 2, 2, 96, 768),
+        fc1_other=vm(48, 768),
         own_small=vm(16, 128, dtype=F32),
         pair_rows=vm(48, 3072, dtype=F32),
         pair_send=vm(24, 3072, dtype=F32),
         par=vm(16, 768, dtype=F32),
-        par_fc1=vm(8, 3072, dtype=F32),
+        par_fc1=vm(8, 1536, dtype=F32),
         rows_in=vm(256, 768),
         cot_in=vm(256, 768),
         normed=vm(256, 768),
@@ -299,12 +302,15 @@
         attended=vm(256, 768),
         attended_t=vm(768, 256),
         middle=vm(256, 768, dtype=F32),
-        normed2=vm(256, 768),
-        normed2_t=vm(768, 256),
-        slope=vm(256, 3072, dtype=F32),
-        active=vm(256, 3072),
-        active_t=vm(32, 96, 256),
-        g_branch2=vm(256, 768),
+        normed2=vm(512, 768),
+        normed2_t=vm(768, 512),
+        slope=vm(512, 1536, dtype=F32),
+        active=vm(512, 1536),
+        active_t=vm(16, 96, 512),
+        g_branch2=vm(512, 768),
+        part_send=vm(2, 256, 768),
+        part_recv=vm(2, 256, 768),
+        other=vm(256, 768, dtype=F32),
         total=vm(256, 768, dtype=F32),
         g_middle=vm(256, 768, dtype=F32),
         g_branch=vm(256, 768),
@@ -314,27 +320,33 @@
         gx_send=vm(256, 768),
         gx_recv=vm(4, 64, 768),
         sums=vm(16, 768, dtype=F32),
-        sums_fc1=vm(8, 3072, dtype=F32),
+        sums_fc1=vm(8, 1536, dtype=F32),
         g_small=vm(4, 4, 16, 256),
-        g_fc1=vm(4, 4, 48, 3072),
-        g_fc2=vm(4, 4, 2, 96, 768),
+        g_fc1=vm(4, 4, 48, 1536),
+        g_fc2=vm(4, 2, 2, 96, 768),
+        g_out=vm(4, 4, 48, 768),
+        g_qkv=vm(4, 4, 48, 2304),
         pr_small=vm(4, 4, 16, 128),
-        pr_a=vm(4, 4, 48, 3072),
-        pr_fc2=vm(4, 4, 2, 96, 384),
+        pr_a=vm(4, 4, 48, 1536),
+        pr_fc1=vm(4, 4, 48, 768),
+        pr_fc2=vm(4, 2, 2, 96, 384),
         dx_small=vm(4, 16, 128),
-        dx_a=vm(4, 48, 3072),
-        dx_fc2=vm(4, 2, 96, 384),
+        dx_a=vm(4, 48, 1536),
         px_small=vm(4, 16, 128),
-        px_a=vm(4, 48, 3072),
+        px_a=vm(4, 48, 1536),
+        px_fc1=vm(4, 2, 48, 768),
         px_fc2=vm(4, 2, 96, 384),
         py_small=vm(4, 16, 128),
-        py_a=vm(4, 48, 3072),
-        py_fc2=vm(4, 2, 96, 384),
+        py_a=vm(4, 48, 1536),
+        py_fc1=vm(48, 768),
         pz_small=vm(3, 16, 128),
-        pz_a=vm(3, 48, 3072),
+        pz_a=vm(3, 48, 1536),
+        pz_fc1=vm(3, 2, 48, 768),
         pz_fc2=vm(3, 2, 96, 384),
-        bz_fc2=vm(3, 4, 2, 96, 384),
-        last_a=vm(48, 3072, dtype=F32),
+        bz_a=vm(3, 4, 48, 1536),
+        last_a=vm(48, 1536, dtype=F32),
+        last_fc1=vm(2, 48, 768, dtype=F32),
+        send_fc1=vm(48, 768),
         last_fc2=vm(96, 384, dtype=F32),
         send_sem=pltpu.SemaphoreType.DMA((COPIES,)),
         recv_sem=pltpu.SemaphoreType.DMA((COPIES,)),
@@ -420,10 +432,17 @@
     s.own_small[8:9, 0:96] = fc1_bias[...].astype(F32)
     s.w_small[z, here, :, lanes(128 * core, 128)] = s.own_small[...].astype(BF16)
     own_rows = pl.ds(pl.multiple_of(24 * core, 8), 24)
-    for ref, half, start in ((qkv_weight, 1152, 0), (out_weight, 384, 1152), (fc1_weight, 1536, 1536)):
+    for ref, half, start in ((qkv_weight, 1152, 0), (out_weight, 384, 1152)):
         s.pair_send[:, start : start + half] = ref[:, lanes((1 - core) * half, half)].astype(F32)
         s.pair_rows[own_rows, start : start + half] = ref[:, lanes(core * half, half)].astype(F32)
-    s.w_fc2[z, here, core] = fc2_weight[...]
+    theirs = fc1_weight[:, lanes((1 - core) * 1536, 1536)].astype(F32)
+    ours = fc1_weight[:, lanes(core * 1536, 1536)].astype(F32)
+    for side in (0, 1):
+        for k in range(4):
+            at, found = 1536 + 768 * side + 192 * k, 384 * k + 192 * side
+            s.pair_send[:, at : at + 192] = theirs[:, found : found + 192]
+            s.pair_rows[own_rows, at : at + 192] = ours[:, found : found + 192]
+    s.w_fc2[z, x, core] = fc2_weight[...]
 
     pl.semaphore_wait(barrier, len(peers))
 
@@ -507,27 +526,69 @@
         def copies(self):
             return self.square + self.z_copies + self.pair
 
+    class PlaneGather:
+        def __init__(self, part, across=None):
+            self.part, self.across = part, across
+
+        def y(self):
+            source, target = self.across
+            self.y_copy = remote(source, target, y_peer)
+
+        def z(self):
+            if self.across:
+                self.y_copy.wait_recv()
+            own = self.part(z, x)
+            self.z_copies = [remote(own, own, z_peers[step]) for step in (1, 2, 3)]
+
+        def x(self):
+            for copy in self.z_copies:
+                copy.wait_recv()
+            column = self.part(ALL, x)
+            self.x_copy = remote(column, column, x_peer)
+            self.pair = [remote(column, column, sibling)]
+
+        def l(self):
+            self.x_copy.wait_recv()
+            column = self.part(ALL, 1 - x)
+            self.pair.append(remote(column, column, sibling))
+
+        def d(self):
+            for copy in self.pair:
+                copy.wait_recv()
+
     def column_part(ref, half, start, size):
         return lambda levels, place: ref.at[levels, place, :, lanes(half * core + start, size)]
 
-    def row_part(ref, start, size):
-        return lambda levels, place: ref.at[levels, place, core, pl.ds(start, size), :]
-
     def gather(part, way):
         return Gather(part, way) if way else SquareGather(part)
 
     gathers = {"s0": gather(column_part(s.w_small, 128, 0, 128), 2)}
-    for name, ref, half in (("q", s.w_qkv, 1152), ("o", s.w_out, 384), ("h", s.w_fc1, 1536)):
+    for name, ref, half in (("q", s.w_qkv, 1152), ("o", s.w_out, 384)):
         for j in range(half // 384):
             gathers[name + str(j)] = gather(column_part(ref, half, 384 * j, 384), GATHER_WAYS[name][j])
-    for j, way in enumerate(GATHER_WAYS["f"]):
-        rows = 96 // len(GATHER_WAYS["f"])
-        gathers["f" + str(j)] = gather(row_part(s.w_fc2, rows * j, rows), way)
-
+    def fc1_gather(j):
+        columns = lanes(768 * core + 384 * j, 384)
+        return PlaneGather(
+            lambda levels, side: s.w_fc1.at[levels, pl.ds(2 * side, 2), :, columns],
+            (s.fc1_other.at[:, 384 * j : 384 * j + 384], s.w_fc1.at[z, here, :, columns]),
+        )
+
+    def fc2_gather(j, size):
+        rows = pl.ds(size * j, size)
+        return PlaneGather(lambda levels, side: s.w_fc2.at[levels, side, core, rows, :])
+
+    for j in range(2):
+        gathers["h" + str(j)] = fc1_gather(j)
+    for j in range(FC2_GATHERS):
+        gathers["f" + str(j)] = fc2_gather(j, 96 // FC2_GATHERS)
 
     pair.wait_recv()
-    for ref, half, start in ((s.w_qkv, 1152, 0), (s.w_out, 384, 1152), (s.w_fc1, 1536, 1536)):
+    for ref, half, start in ((s.w_qkv, 1152, 0), (s.w_out, 384, 1152)):
         ref[z, here, :, lanes(core * half, half)] = s.pair_rows[:, start : start + half].astype(BF16)
+    halves = lanes(1536 + 768 * y, 768), lanes(1536 + 768 * (1 - y), 768)
+    s.w_fc1[z, here, :, lanes(768 * core, 768)] = s.pair_rows[:, halves[0]].astype(BF16)
+    s.fc1_other[...] = s.pair_rows[:, halves[1]].astype(BF16)
+
 
     def by_rows(body, carry=None):
         def step(i, held):
@@ -548,9 +609,12 @@
         columns = over((128, D), 1)
         return (columns - 24 * piece24(columns) == over((128, D), 0)).astype(F32).astype(BF16)
 
+    def hidden_unit(columns):
+        return columns + 192 * lax.shift_right_logical(columns * 21846, 22) + 192 * y
+
     def spread96():
-        columns = over((128, FF), 1)
-        return (columns - 96 * piece96(columns) == over((128, FF), 0)).astype(F32).astype(BF16)
+        columns = hidden_unit(over((128, FF // 2), 1))
+        return (columns - 96 * piece96(columns) == over((128, FF // 2), 0)).astype(F32).astype(BF16)
 
     def unpack_small():
         flat = s.w_small[...].reshape(256, 256)
@@ -565,11 +629,12 @@
         s.par[...] = found
         pick = (over((16, 256), 1) == 16 * over((16, 256), 0) + 8).astype(F32).astype(BF16)
         spread = spread96()
-        pieces = piece96(over((16, FF), 1))
-        found = jnp.zeros((16, FF), F32)
+        shape = (16, FF // 2)
+        pieces = piece96(hidden_unit(over(shape, 1)))
+        found = jnp.zeros(shape, F32)
         for side in (0, 1):
             rows = dot(pick, flat[:, 128 * side : 128 * side + 128]).astype(BF16)
-            found = found + jnp.where(pieces == 2 * over((16, FF), 0) + side, dot(rows, spread), 0.0)
+            found = found + jnp.where(pieces == 2 * over(shape, 0) + side, dot(rows, spread), 0.0)
         s.par_fc1[0:1, :] = jnp.sum(found, axis=0, keepdims=True)
 
     def standardized(rows):
@@ -626,25 +691,29 @@
             return 0
 
         by_rows(body, 0)
+
+    def transpose_out():
         s.attended_t[...] = s.attended[...].T
-        s.normed2_t[...] = s.normed2[...].T
-
-    def feed(j):
+        s.normed2_t[:, 0:256] = s.normed2[0:256, :].T
+
+    def feed(j, frame):
         def body(side, _):
-            start = 1536 * side + 384 * j
-            columns = lanes(start, 384)
-            s.total[:, 0:384] = dot(s.normed2[...], s.w_fc1[:, :, :, columns].reshape(D, 384))
+            columns = lanes(768 * side + 384 * j, 384)
+            tokens = pl.ds(256 * frame, 256)
+            s.other[:, 0:384] = dot(s.normed2[tokens, :], s.w_fc1[:, :, :, columns].reshape(D, 384))
 
             def gelu(rows, _):
-                hidden = s.total[rows, 0:384] + s.par_fc1[0:1, columns]
+                there = pl.ds(pl.multiple_of(rows.start + 256 * frame, ROWS), ROWS)
+                hidden = s.other[rows, 0:384] + s.par_fc1[0:1, columns]
                 normal = 0.5 + 0.5 * lax.erf(hidden * (1.0 / math.sqrt(2.0)))
                 bell = jnp.exp(-0.5 * hidden * hidden) * (1.0 / math.sqrt(2.0 * math.pi))
-                s.slope[rows, columns] = normal + hidden * bell
-                s.active[rows, columns] = (hidden * normal).astype(BF16)
+                s.slope[there, columns] = normal + hidden * bell
+                s.active[there, columns] = (hidden * normal).astype(BF16)
                 return 0
 
             by_rows(gelu, 0)
-            s.active_t[pl.ds(16 * side + 4 * j, 4)] = s.active[:, columns].T.reshape(4, 96, 256)
+            found = s.active[tokens, columns].T.reshape(4, 96, 256)
+            s.active_t[pl.ds(8 * side + 4 * j, 4), :, 256 * frame : 256 * frame + 256] = found
             return 0
 
         lax.fori_loop(0, 2, body, 0)
@@ -660,20 +729,22 @@
 
 
     class Scatter:
+        every = ALL
+
         def __init__(self, own, other, pr, dx, dy, px, py, pz, finish, low=2):
             self.own, self.other, self.finish = own, other, finish
             self.pr, self.dx, self.dy, self.px, self.py, self.pz = pr, dx, dy, px, py, pz
             self.low, self.high = pl.ds(0, low), pl.ds(low, 4 - low)
 
         def s(self):
-            self.pair = remote(self.other(), self.pr(ALL, ALL), sibling)
+            self.pair = remote(self.other(), self.pr(ALL, self.every), sibling)
 
         def add_pair(self):
             self.pair.wait_recv()
 
             def add(level, _):
-                ref = self.own(level, ALL)
-                ref[...] = ref[...] + self.pr(level, ALL)[...]
+                ref = self.own(level, self.every)
+                ref[...] = ref[...] + self.pr(level, self.every)[...]
                 return 0
 
             lax.fori_loop(0, 4, add, 0)
@@ -760,6 +831,45 @@
             for copy in self.square:
                 copy.wait_recv()
             self.finish(self)
+
+    class PlaneScatter(Scatter):
+        def __init__(self, own, other, pr, px, pz, finish, across=None):
+            self.own, self.other, self.finish, self.across = own, other, finish, across
+            self.pr, self.px, self.pz = pr, px, pz
+
+        def x(self):
+            self.add_pair()
+            self.x_copy = remote(self.own(ALL, 1 - x), self.px(ALL), x_peer)
+
+        def z(self):
+            self.x_copy.wait_recv()
+
+            def add(level, _):
+                ref = self.own(level, x)
+                ref[...] = ref[...] + self.px(level)[...]
+                return 0
+
+            lax.fori_loop(0, 4, add, 0)
+            self.z_copies = [
+                remote(self.own(z_of[step], x), self.pz(step - 1), z_peers[step]) for step in (1, 2, 3)
+            ]
+
+        def y(self):
+            for copy in self.z_copies:
+                copy.wait_recv()
+            source, target = self.across(self)
+            self.y_copy = remote(source, target, y_peer)
+
+        def l(self):
+            for copy in [self.y_copy] if self.across else self.z_copies:
+                copy.wait_recv()
+            self.finish(self)
+
+        def summed(self, view):
+            found = view(self.own(z, x))[...].astype(F32)
+            for i in range(3):
+                found = found + view(self.pz(i))[...].astype(F32)
+            return found
 
     def columns_of(ref, base, half, start, size):
         def own(levels, places):
@@ -801,7 +911,40 @@
             way,
         )
 
-    def fc2_scatter(j, size, way):
+    def fc1_scatter(j):
+        at = slice(384 * j, 384 * j + 384)
+
+        def own_columns(side):
+            return lanes(768 * side + 384 * j, 384)
+
+        def own(levels, side):
+            places = ALL if side is ALL else pl.ds(2 * side, 2)
+            return s.g_fc1.at[levels, places, :, own_columns(core)]
+
+        def across(scatter):
+            s.last_fc1[0, :, at] = scatter.summed(lambda ref: ref.at[y])
+            s.send_fc1[:, at] = scatter.summed(lambda ref: ref.at[1 - y]).astype(BF16)
+            return s.send_fc1.at[:, at], s.py_fc1.at[:, at]
+
+        def finish(scatter):
+            s.last_fc1[1, :, at] = s.py_fc1[:, at].astype(F32)
+            other_rows = pl.ds(pl.multiple_of(24 * (1 - core), 8), 24)
+            for i, half in enumerate((y, 1 - y)):
+                target = lanes(1536 * half + 768 * core + 384 * j, 384)
+                finals.append(remote(s.last_fc1.at[i, other_rows, at], grad_fc1.at[:, target], sibling))
+                grad_fc1[:, target] = s.last_fc1[i, own_rows, at]
+
+        return PlaneScatter(
+            own,
+            lambda: s.g_fc1.at[:, :, :, own_columns(1 - core)],
+            lambda levels, places: s.pr_fc1.at[levels, places, :, at],
+            lambda levels: s.px_fc1.at[levels, :, :, at],
+            lambda i: s.pz_fc1.at[i, :, :, at],
+            finish,
+            across,
+        )
+
+    def fc2_scatter(j, size):
         rows = pl.ds(size * j, size)
         half = lanes(384 * core, 384)
 
@@ -810,23 +953,13 @@
             finals.append(remote(s.last_fc2.at[rows, :], grad_fc2.at[rows, half], sibling))
             grad_fc2[rows, half] = scatter.summed(lambda ref: ref.at[core])
 
-        own = lambda levels, places: s.g_fc2.at[levels, places, :, rows, half]
-        other = lambda: s.g_fc2.at[:, :, :, rows, lanes(384 * (1 - core), 384)]
-        pr = lambda levels, places: s.pr_fc2.at[levels, places, :, rows, :]
-        pz = lambda i: s.pz_fc2.at[i, :, rows, :]
-        if not way:
-            return SquareScatter(own, other, pr, lambda i, places: s.bz_fc2.at[i, places, :, rows, :], pz, finish)
-        return Scatter(
-            own,
-            other,
-            pr,
-            lambda levels: s.dx_fc2.at[levels, :, rows, :],
-            lambda levels: s.dx_fc2.at[levels, :, rows, :],
+        return PlaneScatter(
+            lambda levels, side: s.g_fc2.at[levels, side if side is not ALL else BOTH, :, rows, half],
+            lambda: s.g_fc2.at[:, :, :, rows, lanes(384 * (1 - core), 384)],
+            lambda levels, side: s.pr_fc2.at[levels, side if side is not ALL else BOTH, :, rows, :],
             lambda levels: s.px_fc2.at[levels, :, rows, :],
-            lambda levels: s.py_fc2.at[levels, :, rows, :],
-            pz,
+            lambda i: s.pz_fc2.at[i, :, rows, :],
             finish,
-            way,
         )
 
     def small_finish(scatter):
@@ -839,17 +972,18 @@
 
     finals = []
     scatters = {}
-    for j, way in enumerate(SCATTER_WAYS["f"]):
-        scatters["f" + str(j)] = fc2_scatter(j, 96 // len(SCATTER_WAYS["f"]), way)
-    for name, ref, base, half, spot, output in (
-        ("h", s.g_fc1, 0, 1536, 0, grad_fc1),
-        ("o", s.w_fc1, 0, 384, 1536, grad_out),
-        ("q", s.w_fc1, D, 1152, 1920, grad_qkv),
+    for j in range(FC2_SCATTERS):
+        scatters["f" + str(j)] = fc2_scatter(j, 96 // FC2_SCATTERS)
+    for j in range(2):
+        scatters["h" + str(j)] = fc1_scatter(j)
+    for name, ref, half, spot, output in (
+        ("o", s.g_out, 384, 0, grad_out),
+        ("q", s.g_qkv, 1152, 384, grad_qkv),
     ):
         for j in range(half // 384):
             way = SCATTER_WAYS[name][j]
             scatters[name + str(j)] = column_scatter(
-                ref, base, half, 384 * j, 384, spot + 384 * j, output, way
+                ref, 0, half, 384 * j, 384, spot + 384 * j, output, way
             )
     scatters["s0"] = Scatter(
         *columns_of(s.g_small, 0, 128, 0, 128),
@@ -863,13 +997,13 @@
     )
 
     def weight_grad_fc2(j):
-        size = 96 // len(SCATTER_WAYS["f"])
+        size = 96 // FC2_SCATTERS
         rows = pl.ds(size * j, size)
 
         def body(turn, _):
             columns = lanes(384 * (turn * core + (1 - turn) * (1 - core)), 384)
-            found = dot(s.active_t[:, rows, :].reshape(32 * size, 256), s.g_branch2[:, columns])
-            s.g_fc2[:, :, :, rows, columns] = found.astype(BF16).reshape(4, 4, 2, size, 384)
+            found = dot(s.active_t[:, rows, :].reshape(16 * size, 512), s.g_branch2[:, columns])
+            s.g_fc2[:, :, :, rows, columns] = found.astype(BF16).reshape(4, 2, 2, size, 384)
             return 0
 
         lax.fori_loop(0, 2, body, 0)
@@ -886,31 +1020,50 @@
     def column_sums(ref, width):
         return jnp.sum(ref[...].astype(F32), axis=0, keepdims=True)
 
-    def feed_back():
+    def feed_back(frame):
+        tokens = pl.ds(256 * frame, 256)
         s.total[...] = jnp.zeros((TOKENS, D), F32)
 
-        def body(level, _):
-            columns = lanes(D * level, D)
-            weight = s.w_fc2[level].reshape(D, D)
-            s.total[...] += dot(s.active[:, columns], weight)
-            s.g_middle[...] = dot_nt(s.g_branch2[...], weight)
+        def body(part, _):
+            columns = lanes(D * part, D)
+            weight = s.w_fc2[pl.ds(2 * part, 2)].reshape(D, D)
+            s.total[...] += dot(s.active[tokens, columns], weight)
+            s.other[...] = dot_nt(s.g_branch2[tokens, :], weight)
 
             def slope(rows, sums):
-                found = (s.g_middle[rows, :] * s.slope[rows, columns]).astype(BF16)
-                s.active[rows, columns] = found
+                there = pl.ds(pl.multiple_of(rows.start + 256 * frame, ROWS), ROWS)
+                found = (s.other[rows, :] * s.slope[there, columns]).astype(BF16)
+                s.active[there, columns] = found
                 return sums + jnp.sum(found.astype(F32), axis=0, keepdims=True)
 
-            s.sums_fc1[0:1, columns] = by_rows(slope, jnp.zeros((1, D), F32))
+            s.sums_fc1[frame : frame + 1, columns] = by_rows(slope, jnp.zeros((1, D), F32))
             return 0
 
-        lax.fori_loop(0, 4, body, 0)
-
+        lax.fori_loop(0, 2, body, 0)
+        if frame:
+            s.part_send[0] = s.total[...].astype(BF16)
+
+    def output():
         def finish(rows, sums):
-            found = valid * (s.middle[rows, :] + (s.total[rows, :] + s.par[7:8, :]))
+            branch = s.total[rows, :] + s.part_recv[0, rows, :].astype(F32)
+            found = valid * (s.middle[rows, :] + (branch + s.par[7:8, :]))
             s.enc_send[rows, :] = found.astype(BF16)
             return sums + jnp.sum(s.g_branch2[rows, :].astype(F32), axis=0, keepdims=True)
 
         s.sums[7:8, :] = by_rows(finish, jnp.zeros((1, D), F32))
+
+    def feed_back_rows(frame):
+        tokens = pl.ds(256 * frame, 256)
+        s.other[...] = jnp.zeros((TOKENS, D), F32)
+
+        def body(part, _):
+            columns = lanes(D * part, D)
+            s.other[...] += dot_nt(s.active[tokens, columns], s.w_fc1[:, :, :, columns].reshape(D, D))
+            return 0
+
+        lax.fori_loop(0, 2, body, 0)
+        if frame:
+            s.part_send[1] = s.other[...].astype(BF16)
 
     def norm_back(upstream, found, scale, gain):
         weighted = upstream * gain
@@ -924,17 +1077,8 @@
         return jnp.sum(values, axis=0, keepdims=True)
 
     def second_norm_back():
-        s.total[...] = jnp.zeros((TOKENS, D), F32)
-
-        def body(level, _):
-            columns = lanes(D * level, D)
-            s.total[...] += dot_nt(s.active[:, columns], s.w_fc1[:, :, :, columns].reshape(D, D))
-            return 0
-
-        lax.fori_loop(0, 4, body, 0)
-
         def rows_back(rows, sums):
-            upstream = s.total[rows, :]
+            upstream = s.other[rows, :] + s.part_recv[1, rows, :].astype(F32)
             found, scale = standardized(s.middle[rows, :])
             middle = s.g_branch2[rows, :].astype(F32) + norm_back(upstream, found, scale, s.par[1:2, :])
             s.g_middle[rows, :] = middle
@@ -1004,10 +1148,11 @@
             s.g_small[:, :, :, 128 * side : 128 * side + 128] = placed.astype(BF16).reshape(4, 4, 16, 128)
         put = (over((256, 16), 0) == 16 * over((256, 16), 1) + 8).astype(F32).astype(BF16)
         spread = spread96()
-        pieces = piece96(over((16, FF), 1))
-        row = s.sums_fc1[0:1, :]
+        shape = (16, FF // 2)
+        pieces = piece96(hidden_unit(over(shape, 1)))
+        row = s.sums_fc1[0:1, :] + s.sums_fc1[1:2, :]
         for side in (0, 1):
-            mine = pieces == 2 * over((16, FF), 0) + side
+            mine = pieces == 2 * over(shape, 0) + side
             placed = dot_nt(jnp.where(mine, row, 0.0).astype(BF16), spread).astype(BF16)
             here_ = s.g_small.at[:, :, :, pl.ds(128 * side, 128)]
             here_[...] = here_[...] + dot(put, placed).astype(BF16).reshape(4, 4, 16, 128)
@@ -1050,10 +1195,6 @@
         moved["grad"] = to_patches(s.gx_send, s.gx_recv)
         s.gx_recv[blk] = s.gx_send[mine, :]
 
-    def free_fc1():
-        for name in ("h0", "h1", "h2", "h3"):
-            sent(gathers[name].copies())
-
     def project_attended():
         s.g_attended[...] = dot_nt(s.g_branch[...], s.w_out[...].reshape(D, D)).astype(BF16)
 
@@ -1061,189 +1202,194 @@
         project_qkv(j)
         project_qkv(j + 3)
 
+    def across(name, source, target):
+        moved[name] = [remote(source, target, y_peer)]
+
+    def send_normed():
+        across("normed", s.normed2.at[0:256, :], s.normed2.at[256:512, :])
+
+    def take_normed():
+        received("normed")
+
+    def transpose_other():
+        s.normed2_t[:, 256:512] = s.normed2[256:512, :].T
+
+    def send_masked():
+        across("masked", s.g_branch2.at[0:256, :], s.g_branch2.at[256:512, :])
+
+    def take_masked():
+        received("masked")
+
+    def send_part():
+        across("part", s.part_send.at[0], s.part_recv.at[0])
+
+    def start_output():
+        received("part")
+        output()
+
+    def send_back():
+        across("back", s.part_send.at[1], s.part_recv.at[1])
+
+    def start_second():
+        received("back")
+        second_norm_back()
+
     def grad_fc1_weight(j):
-        column_grad(s.normed2_t, s.active, 384 * j, s.g_fc1, 0, 1536, 384)
+        column_grad(s.normed2_t, s.active, 384 * j, s.g_fc1, 0, 768, 384)
 
     def grad_out_weight():
-        column_grad(s.attended_t, s.g_branch, 0, s.w_fc1, 0, 384, 384)
+        column_grad(s.attended_t, s.g_branch, 0, s.g_out, 0, 384, 384)
 
     def grad_qkv_weight(j):
-        column_grad(s.normed_t, s.g_mixed, 384 * j, s.w_fc1, D, 1152, 384)
+        column_grad(s.normed_t, s.g_mixed, 384 * j, s.g_qkv, 0, 1152, 384)
 
     g, r = types.SimpleNamespace(**gathers), types.SimpleNamespace(**scatters)
-    g.f2.p()
+    g.h1.y()
     g.s0.z()
+    g.o0.z()
+    send_cotangent()
+    g.h0.y()
     g.q0.z()
-    send_rows()
     g.q1.z()
     g.s0.p()
+    g.s0.f()
+    g.o0.p()
+    g.q0.p()
     g.q2.z()
-    g.q0.p()
-    g.s0.f()
-    g.o0.z()
-    g.h2.z()
     g.q1.p()
+    g.o0.f()
+    g.h0.z()
+    g.s0.g()
+    g.q0.f()
+    start_cotangent()
     g.q2.p()
+    g.o0.g()
     g.q1.f()
-    g.q0.f()
     g.q1.g()
     g.q0.g()
-    g.h0.z()
-    g.o0.p()
-    g.h2.p()
-    g.h3.z()
+    g.s0.l()
+    g.h1.z()
+    g.q2.f()
+    g.q2.g()
+    g.h0.x()
+    send_rows()
     g.q1.l()
-    g.s0.g()
     g.q0.l()
-    g.h1.z()
+    g.o0.l()
+    g.s0.d()
     g.f0.z()
+    g.f1.z()
+    unpack_small()
+    g.f2.z()
     g.q0.d()
-    g.h0.p()
-    g.o0.f()
-    g.h2.f()
-    g.q2.f()
-    g.h1.p()
-    g.s0.l()
-    g.f1.z()
-    g.q2.g()
-    send_cotangent()
-    g.s0.d()
-    unpack_small()
-    g.h3.p()
-    g.o0.g()
-    g.h2.g()
+    g.h1.x()
+    send_masked()
+    g.q2.l()
     start_norm()
-    g.h0.f()
     project_both(0)
-    g.f2.z()
-    g.h1.f()
-    g.f1.p()
-    g.h1.g()
-    g.h3.f()
-    g.q2.l()
-    g.o0.l()
-    g.h0.g()
+    g.q1.d()
     g.q2.d()
-    g.f0.p()
-    g.q1.d()
     project_both(1)
     project_both(2)
-    g.h2.l()
+    attend()
     g.o0.d()
-    attend()
-    g.h3.g()
     project_out()
+    send_normed()
+    g.f0.x()
     g.h1.l()
-    g.h2.d()
+    g.f1.x()
+    g.h0.l()
+    g.h0.d()
+    take_masked()
+    g.f2.x()
     g.h1.d()
-    g.h0.l()
-    start_cotangent()
-    feed(1)
-    g.f1.f()
-    g.h0.d()
-    feed(2)
-    g.f1.g()
-    g.f0.f()
-    g.f2.l()
-    feed(0)
-    g.h3.l()
-    g.h3.d()
-    g.f0.g()
-    feed(3)
+    g.f0.l()
+    feed(1, 0)
+    transpose_out()
+    feed(0, 0)
+    take_normed()
+    feed(1, 1)
+    feed(0, 1)
+    weight_grad_fc2(2)
+    r.f2.s()
     g.f1.l()
     weight_grad_fc2(1)
+    r.f2.x()
+    g.f2.l()
+    weight_grad_fc2(0)
+    g.f1.d()
+    r.f1.s()
+    g.f0.d()
+    r.f0.s()
     g.f2.d()
-    r.f1.s()
-    weight_grad_fc2(2)
-    r.f2.s()
-    weight_grad_fc2(0)
-    g.f0.l()
-    r.f1.p()
-    r.f0.s()
-    r.f2.p()
-    g.f1.d()
-    g.f0.d()
-    feed_back()
+    feed_back(1)
+    feed_back_rows(1)
+    send_back()
+    transpose_other()
+    r.f1.x()
+    r.f0.x()
+    feed_back(0)
+    grad_fc1_weight(0)
+    send_part()
+    grad_fc1_weight(1)
+    r.h1.s()
+    r.h0.s()
+    r.f2.z()
+    r.f1.z()
+    feed_back_rows(0)
+    r.h1.x()
+    r.h0.x()
+    start_second()
+    grad_out_weight()
+    r.o0.s()
+    r.f0.z()
+    project_attended()
+    r.o0.p()
+    attend_back()
+    grad_qkv_weight(2)
+    r.q2.s()
+    r.h1.z()
+    start_output()
     send_encoded()
-    r.f1.f()
-    r.f1.g()
-    grad_fc1_weight(0)
-    r.f0.z()
-    r.h0.s()
-    grad_fc1_weight(2)
-    grad_fc1_weight(3)
-    r.f2.f()
-    r.h0.p()
-    r.f2.g()
-    r.h3.s()
-    r.h2.s()
-    second_norm_back()
-    project_attended()
-    r.h3.p()
-    r.h2.p()
-    free_fc1()
-    r.h0.f()
-    attend_back()
-    r.f2.z()
-    r.h3.f()
-    r.h0.g()
-    r.h3.g()
+    r.q2.p()
+    r.h0.z()
     grad_qkv_weight(1)
-    grad_out_weight()
-    r.h2.f()
     r.q1.s()
-    r.f1.z()
-    r.h2.g()
-    grad_qkv_weight(0)
-    r.o0.s()
-    r.q1.p()
-    r.q0.s()
-    grad_fc1_weight(1)
-    r.q0.p()
-    r.h3.z()
-    grad_qkv_weight(2)
-    r.q1.f()
-    r.q2.s()
-    r.h1.s()
-    r.q1.g()
-    r.o0.p()
-    r.h0.z()
-    r.h1.p()
-    r.h2.z()
-    first_norm_back()
-    r.q1.z()
-    pack_small()
-    r.f2.l()
-    r.s0.s()
-    r.h0.l()
+    r.f1.l()
     r.o0.f()
     r.o0.g()
+    r.q1.p()
+    grad_qkv_weight(0)
+    r.q2.f()
+    r.q2.g()
+    first_norm_back()
+    r.o0.z()
+    r.f2.l()
+    r.q1.f()
+    r.q0.s()
+    r.q1.g()
+    pack_small()
+    r.s0.s()
+    r.f0.l()
+    r.q0.p()
+    r.q2.z()
     r.s0.p()
-    r.h1.f()
     r.q0.f()
-    r.f1.l()
-    r.h1.g()
+    r.q1.z()
     r.q0.g()
-    r.o0.z()
+    r.h1.y()
     r.s0.f()
-    r.q2.p()
-    r.h1.z()
-    r.q2.f()
-    r.h3.l()
-    r.q2.g()
-    r.h2.l()
+    r.h0.y()
+    send_grad_rows()
+    r.q2.l()
+    r.s0.g()
     r.q0.z()
-    r.f0.p()
-    send_grad_rows()
+    r.s0.z()
+    r.o0.l()
     r.q1.l()
-    r.o0.l()
-    r.s0.g()
-    r.q2.z()
-    r.f0.l()
     r.h1.l()
-    r.s0.z()
+    r.h0.l()
     r.q0.l()
-    r.q2.l()
     r.s0.l()
     for name in list(moved):
         received(name)
@@ -1256,7 +1402,13 @@
 def emit_kernel(*refs):
     count = len(refs) // 2
     for i in range(count):
-        refs[count + i][...] = refs[i][...].astype(refs[count + i].dtype)
+        if i == FC1_OUTPUT:
+            for side in (0, 1):
+                for k in range(8):
+                    source = refs[i][:, 1536 * side + 192 * k : 1536 * side + 192 * k + 192]
+                    refs[count + i][:, 384 * k + 192 * side : 384 * k + 192 * side + 192] = source
+        else:
+            refs[count + i][...] = refs[i][...]
 
 
 def emit(arrays):

time: 148 us -> 128 us (0.86)
  Pallas kernels: 147 us -> 127 us
    pallas_call x1, Pallas kernels: 144 us -> 124 us  [fast(): pl.pallas_call(layer_kernel, out_shape=[jax.ShapeDtypeStruct(shape, dtype...]
where the time goes in v3:
time: 128 us
  Pallas kernels  127 us (99%)
    pallas_call x1, Pallas kernels, fast(): pl.pallas_call(layer_kernel, out_shape=[jax.ShapeDtypeStruct(shape, dtype...  124 us
    pallas_call x1, Pallas kernels, emit(): pl.pallas_call(emit_kernel, out_shape=[jax.ShapeDtypeStruct(a.shape, a.dt...  2.89 us

profile of v3, /device:TPU:0, one launch (start us, length us, event | category | flops | bytes accessed | tf_op | source)
XLA Modules:
  0.0 128.0 jit_solution(10258596576678232635)
XLA Ops:
  0.6 124.3 %shard_map.203 = (bf16[4,64,768]{2,1,0:T(8,128)(2,1)}, f32[4,64,768]{2,1,0:T(8,128)}, f32[2,24]{1,0:T(2,128)}, f32[2,24]{1,0:T(2,128)}, f32[24,2304]{1,0:T(8,128...) custom-call(bf16[4,64,768]{2,1,0:T(8,128)(2,1)} %patches.1, ...), custom_call_target="tpu_custom_call" | custom-call | tf_op jit(solution)/shard_map/pallas_call | solution.py:1454
  124.9 2.9 %shard_map.204 = (bf16[4,64,768]{2,1,0:T(8,128)(2,1)}, f32[4,64,768]{2,1,0:T(8,128)}, f32[2,24]{1,0:T(2,128)}, f32[2,24]{1,0:T(2,128)}, f32[24,2304]{1,0:T(8,128...) custom-call(bf16[4,64,768]{2,1,0:T(8,128)(2,1)} %get-tuple-element.3, ...), custom_call_target="tpu_custom_call" | custom-call | tf_op jit(solution)/shard_map/pallas_call | solution.py:1417

commit v4 on v3

--- a/solution.py
+++ b/solution.py
@@ -256,10 +256,17 @@
 FF = 3072
 TOKENS = 256
 ROWS = 64
-ALL, BOTH = pl.ds(0, 4), pl.ds(0, 2)
-GATHER_WAYS = dict(q=(1, 2, 2), o=(2,))
-SCATTER_WAYS = dict(o=(2,), q=(2, 2, 3))
-FC2_GATHERS, FC2_SCATTERS = 3, 3
+ALL, THREE, BOTH = pl.ds(0, 4), pl.ds(0, 3), pl.ds(0, 2)
+GATHER_WAYS = dict(q=(-2, -2, -2), o=(-2,), f=(1, 1, 0))
+SCATTER_WAYS = dict(f=(0, 1, 1), o=(2,), q=(2, 2, 2))
+
+
+TILES = ((0, 1536), (768, 384), (1920, 1152))
+
+
+def tile(j, side):
+    first, second = TILES[j]
+    return first + side * (second - first)
 
 
 def dot(left, right):
@@ -274,7 +281,7 @@
     return lax.dot_general(left, right, (((0,), (0,)), ((), ())), preferred_element_type=F32)
 
 
-COPIES = 360
+SENDS, ARRIVALS = 80, 130
 FC1_OUTPUT = 7
 
 
@@ -295,7 +302,7 @@
         par=vm(16, 768, dtype=F32),
         par_fc1=vm(8, 1536, dtype=F32),
         rows_in=vm(256, 768),
-        cot_in=vm(256, 768),
+        cot_in=vm(512, 768),
         normed=vm(256, 768),
         normed_t=vm(768, 256),
         mixed=vm(256, 2304),
@@ -306,17 +313,22 @@
         normed2_t=vm(768, 512),
         slope=vm(512, 1536, dtype=F32),
         active=vm(512, 1536),
+        g_hidden=vm(512, 1536),
         active_t=vm(16, 96, 512),
         g_branch2=vm(512, 768),
-        part_send=vm(2, 256, 768),
-        part_recv=vm(2, 256, 768),
+        part_across=vm(256, 768),
+        part_recv=vm(128, 768),
+        base_send=vm(128, 768),
+        base_recv=vm(128, 768),
+        back_send=vm(256, 768),
+        back_recv=vm(256, 768),
         other=vm(256, 768, dtype=F32),
         total=vm(256, 768, dtype=F32),
         g_middle=vm(256, 768, dtype=F32),
         g_branch=vm(256, 768),
         g_attended=vm(256, 768),
         g_mixed=vm(256, 2304),
-        enc_send=vm(256, 768),
+        enc_send=vm(2, 128, 768),
         gx_send=vm(256, 768),
         gx_recv=vm(4, 64, 768),
         sums=vm(16, 768, dtype=F32),
@@ -344,12 +356,13 @@
         pz_fc1=vm(3, 2, 48, 768),
         pz_fc2=vm(3, 2, 96, 384),
         bz_a=vm(3, 4, 48, 1536),
+        bz_fc2=vm(3, 2, 2, 96, 384),
         last_a=vm(48, 1536, dtype=F32),
         last_fc1=vm(2, 48, 768, dtype=F32),
         send_fc1=vm(48, 768),
         last_fc2=vm(96, 384, dtype=F32),
-        send_sem=pltpu.SemaphoreType.DMA((COPIES,)),
-        recv_sem=pltpu.SemaphoreType.DMA((COPIES,)),
+        send_sem=pltpu.SemaphoreType.DMA((SENDS,)),
+        recv_sem=pltpu.SemaphoreType.DMA((ARRIVALS,)),
     )
 
 
@@ -398,21 +411,25 @@
     for peer in peers:
         pl.semaphore_signal(barrier, inc=1, device_id=peer, device_id_type=MESH_ID)
 
-    started, waited = [], set()
-
-    def sent(copies):
-        for copy in copies:
-            if id(copy) not in waited:
-                waited.add(id(copy))
-                copy.wait_send()
-
-    def remote(source, target, peer):
+    started, groups = [], []
+
+    class Group:
+        def __init__(self):
+            self.sem = s.recv_sem.at[len(groups)]
+            groups.append(self)
+
+        def wait(self, ref):
+            pltpu.make_async_copy(ref, ref, self.sem).wait()
+
+    def remote(source, target, peer, group=None):
         spot = len(started)
+        if spot >= SENDS:
+            started[spot - SENDS].wait_send()
         copy = pltpu.make_async_remote_copy(
             src_ref=source,
             dst_ref=target,
-            send_sem=s.send_sem.at[spot],
-            recv_sem=s.recv_sem.at[spot],
+            send_sem=s.send_sem.at[spot % SENDS],
+            recv_sem=(group or Group()).sem,
             device_id=peer,
             device_id_type=MESH_ID,
         )
@@ -432,9 +449,14 @@
     s.own_small[8:9, 0:96] = fc1_bias[...].astype(F32)
     s.w_small[z, here, :, lanes(128 * core, 128)] = s.own_small[...].astype(BF16)
     own_rows = pl.ds(pl.multiple_of(24 * core, 8), 24)
-    for ref, half, start in ((qkv_weight, 1152, 0), (out_weight, 384, 1152)):
-        s.pair_send[:, start : start + half] = ref[:, lanes((1 - core) * half, half)].astype(F32)
-        s.pair_rows[own_rows, start : start + half] = ref[:, lanes(core * half, half)].astype(F32)
+    for ref, start, columns in (
+        (qkv_weight, 0, partial(tile, 0)),
+        (qkv_weight, 384, partial(tile, 1)),
+        (qkv_weight, 768, partial(tile, 2)),
+        (out_weight, 1152, lambda side: 384 * side),
+    ):
+        s.pair_send[:, start : start + 384] = ref[:, lanes(columns(1 - core), 384)].astype(F32)
+        s.pair_rows[own_rows, start : start + 384] = ref[:, lanes(columns(core), 384)].astype(F32)
     theirs = fc1_weight[:, lanes((1 - core) * 1536, 1536)].astype(F32)
     ours = fc1_weight[:, lanes(core * 1536, 1536)].astype(F32)
     for side in (0, 1):
@@ -450,85 +472,93 @@
 
     mine = pl.ds(pl.multiple_of(64 * blk, 64), 64)
 
-    def to_frames(source, target):
-        return [remote(source.at[2 * py + pc], target.at[mine, :], (wide, 2 * py + pc)) for py, pc in blk_peers]
-
+    rows_moved = Group()
+    for py, pc in blk_peers:
+        remote(patches.at[2 * py + pc], s.rows_in.at[mine, :], (wide, 2 * py + pc), rows_moved)
     s.rows_in[mine, :] = patches[blk]
-    s.cot_in[mine, :] = cotangent[blk]
 
     class Gather:
         def __init__(self, part, low):
             self.part, self.low, self.high = part, pl.ds(0, low), pl.ds(low, 4 - low)
+            self.by_z, self.by_x, self.by_y, self.far, self.pair = (Group() for _ in range(5))
 
         def z(self):
             own = self.part(z, here)
-            self.z_copies = [remote(own, own, z_peers[step]) for step in (1, 2, 3)]
+            for peer in z_peers[1:]:
+                remote(own, own, peer, self.by_z)
 
         def p(self):
-            for copy in self.z_copies:
+            self.by_z.wait(self.part(THREE, here))
+            self.share(self.part(ALL, here))
+
+        def share(self, block):
+            remote(block, block, x_peer, self.by_x)
+            remote(block, block, y_peer, self.by_y)
+            remote(block, block, sibling, self.pair)
+
+        def f(self):
+            column = self.part(ALL, at_x)
+            self.by_x.wait(column)
+            some = self.part(self.low, at_x)
+            remote(some, some, y_peer, self.far)
+            remote(column, column, sibling, self.pair)
+
+        def g(self):
+            column = self.part(ALL, at_y)
+            self.by_y.wait(column)
+            some = self.part(self.high, at_y)
+            remote(some, some, x_peer, self.far)
+            remote(column, column, sibling, self.pair)
+
+        def l(self):
+            column = self.part(ALL, at_d)
+            self.far.wait(column)
+            remote(column, column, sibling, self.pair)
+
+        def d(self):
+            self.pair.wait(self.part(ALL, ALL))
+
+    class FineGather(Gather):
+        def z(self):
+            own = self.part(z, here)
+            self.z_copies = [remote(own, own, peer) for peer in z_peers[1:]]
+
+        def o(self):
+            self.share(self.part(z, here))
+
+        def p(self):
+            for step, copy in zip((1, 2, 3), self.z_copies):
                 copy.wait_recv()
-            column = self.part(ALL, here)
-            self.x, self.y = remote(column, column, x_peer), remote(column, column, y_peer)
-            self.pair = [remote(column, column, sibling)]
-
-        def f(self):
-            self.x.wait_recv()
-            some = self.part(self.low, at_x)
-            self.dy = remote(some, some, y_peer)
-            column = self.part(ALL, at_x)
-            self.pair.append(remote(column, column, sibling))
-
-        def g(self):
-            self.y.wait_recv()
-            some = self.part(self.high, at_y)
-            self.dx = remote(some, some, x_peer)
-            column = self.part(ALL, at_y)
-            self.pair.append(remote(column, column, sibling))
-
-        def l(self):
-            self.dy.wait_recv()
-            self.dx.wait_recv()
-            column = self.part(ALL, at_d)
-            self.pair.append(remote(column, column, sibling))
-
-        def d(self):
-            for copy in self.pair:
-                copy.wait_recv()
-
-        def copies(self):
-            return self.z_copies + self.pair + [self.x, self.y, self.dx, self.dy]
+                self.share(self.part(z_of[4 - step], here))
 
     class SquareGather:
         def __init__(self, part):
-            self.part = part
+            self.part, self.square, self.by_z, self.pair = part, Group(), Group(), Group()
 
         def p(self):
             own = self.part(z, here)
-            self.square = [remote(own, own, peer) for peer in (x_peer, y_peer, d_peer)]
+            for peer in (x_peer, y_peer, d_peer):
+                remote(own, own, peer, self.square)
 
         def z(self):
-            for copy in self.square:
-                copy.wait_recv()
+            self.square.wait(self.part(z, THREE))
             level = self.part(z, ALL)
-            self.z_copies = [remote(level, level, z_peers[step]) for step in (1, 2, 3)]
-            self.pair = [remote(level, level, sibling)]
+            for peer in z_peers[1:]:
+                remote(level, level, peer, self.by_z)
+            remote(level, level, sibling, self.pair)
 
         def l(self):
-            for step, copy in zip((1, 2, 3), self.z_copies):
-                copy.wait_recv()
-                level = self.part(z_of[4 - step], ALL)
-                self.pair.append(remote(level, level, sibling))
+            self.by_z.wait(self.part(THREE, ALL))
+            for step in (1, 2, 3):
+                level = self.part(z_of[step], ALL)
+                remote(level, level, sibling, self.pair)
 
         def d(self):
-            for copy in self.pair:
-                copy.wait_recv()
-
-        def copies(self):
-            return self.square + self.z_copies + self.pair
+            self.pair.wait(self.part(ALL, ALL))
 
     class PlaneGather:
         def __init__(self, part, across=None):
-            self.part, self.across = part, across
+            self.part, self.across, self.by_z, self.pair = part, across, Group(), Group()
 
         def y(self):
             source, target = self.across
@@ -538,53 +568,81 @@
             if self.across:
                 self.y_copy.wait_recv()
             own = self.part(z, x)
-            self.z_copies = [remote(own, own, z_peers[step]) for step in (1, 2, 3)]
+            for peer in z_peers[1:]:
+                remote(own, own, peer, self.by_z)
 
         def x(self):
-            for copy in self.z_copies:
-                copy.wait_recv()
+            self.by_z.wait(self.part(THREE, x))
             column = self.part(ALL, x)
             self.x_copy = remote(column, column, x_peer)
-            self.pair = [remote(column, column, sibling)]
+            remote(column, column, sibling, self.pair)
 
         def l(self):
             self.x_copy.wait_recv()
             column = self.part(ALL, 1 - x)
-            self.pair.append(remote(column, column, sibling))
+            remote(column, column, sibling, self.pair)
 
         def d(self):
-            for copy in self.pair:
-                copy.wait_recv()
-
-    def column_part(ref, half, start, size):
-        return lambda levels, place: ref.at[levels, place, :, lanes(half * core + start, size)]
+            self.pair.wait(self.part(ALL, BOTH))
+
+    class AcrossGather:
+        def __init__(self, part):
+            self.part, self.by_z, self.pair = part, Group(), Group()
+
+        def x(self):
+            own = self.part(z, x)
+            self.x_copy = remote(own, own, x_peer)
+
+        def z(self):
+            self.x_copy.wait_recv()
+            level = self.part(z, BOTH)
+            for peer in z_peers[1:]:
+                remote(level, level, peer, self.by_z)
+            remote(level, level, sibling, self.pair)
+
+        def l(self):
+            self.by_z.wait(self.part(THREE, BOTH))
+            for step in (1, 2, 3):
+                level = self.part(z_of[step], BOTH)
+                remote(level, level, sibling, self.pair)
+
+        def d(self):
+            self.pair.wait(self.part(ALL, BOTH))
+
+    def column_part(ref, start, size):
+        return lambda levels, place: ref.at[levels, place, :, lanes(start, size)]
 
     def gather(part, way):
-        return Gather(part, way) if way else SquareGather(part)
-
-    gathers = {"s0": gather(column_part(s.w_small, 128, 0, 128), 2)}
-    for name, ref, half in (("q", s.w_qkv, 1152), ("o", s.w_out, 384)):
-        for j in range(half // 384):
-            gathers[name + str(j)] = gather(column_part(ref, half, 384 * j, 384), GATHER_WAYS[name][j])
+        return Gather(part, way) if way > 0 else FineGather(part, -way) if way else SquareGather(part)
+
+    gathers = {
+        "s0": gather(column_part(s.w_small, 128 * core, 128), 2),
+        "o0": gather(column_part(s.w_out, 384 * core, 384), GATHER_WAYS["o"][0]),
+    }
+    for j in range(3):
+        gathers["q" + str(j)] = gather(column_part(s.w_qkv, tile(j, core), 384), GATHER_WAYS["q"][j])
+
     def fc1_gather(j):
         columns = lanes(768 * core + 384 * j, 384)
         return PlaneGather(
-            lambda levels, side: s.w_fc1.at[levels, pl.ds(2 * side, 2), :, columns],
+            lambda levels, side: s.w_fc1.at[levels, ALL if side is BOTH else pl.ds(2 * side, 2), :, columns],
             (s.fc1_other.at[:, 384 * j : 384 * j + 384], s.w_fc1.at[z, here, :, columns]),
         )
 
-    def fc2_gather(j, size):
+    def fc2_gather(j, size, way):
         rows = pl.ds(size * j, size)
-        return PlaneGather(lambda levels, side: s.w_fc2.at[levels, side, core, rows, :])
+        part = lambda levels, side: s.w_fc2.at[levels, side, core, rows, :]
+        return PlaneGather(part) if way else AcrossGather(part)
 
     for j in range(2):
         gathers["h" + str(j)] = fc1_gather(j)
-    for j in range(FC2_GATHERS):
-        gathers["f" + str(j)] = fc2_gather(j, 96 // FC2_GATHERS)
+    for j, way in enumerate(GATHER_WAYS["f"]):
+        gathers["f" + str(j)] = fc2_gather(j, 96 // len(GATHER_WAYS["f"]), way)
 
     pair.wait_recv()
-    for ref, half, start in ((s.w_qkv, 1152, 0), (s.w_out, 384, 1152)):
-        ref[z, here, :, lanes(core * half, half)] = s.pair_rows[:, start : start + half].astype(BF16)
+    for j in range(3):
+        s.w_qkv[z, here, :, lanes(tile(j, core), 384)] = s.pair_rows[:, 384 * j : 384 * j + 384].astype(BF16)
+    s.w_out[z, here, :, lanes(384 * core, 384)] = s.pair_rows[:, 1152:1536].astype(BF16)
     halves = lanes(1536 + 768 * y, 768), lanes(1536 + 768 * (1 - y), 768)
     s.w_fc1[z, here, :, lanes(768 * core, 768)] = s.pair_rows[:, halves[0]].astype(BF16)
     s.fc1_other[...] = s.pair_rows[:, halves[1]].astype(BF16)
@@ -651,13 +709,12 @@
         by_rows(body, 0)
         s.normed_t[...] = s.normed[...].T
 
-    def project_qkv(tile):
-        start = 384 * tile
+    def project_qkv(start):
         found = dot(s.normed[...], s.w_qkv[:, :, :, start : start + 384].reshape(D, 384))
-        if tile < 2:
+        if start < D:
             found = (found + s.par[4:5, start : start + 384]) * 0.125
-        if tile >= 4:
-            found = found + s.par[5:6, start - 1536 : start - 1152]
+        if start >= 2 * D:
+            found = found + s.par[5:6, start - 2 * D : start - 2 * D + 384]
         s.mixed[:, start : start + 384] = found.astype(BF16)
 
     def head_masks():
@@ -668,7 +725,7 @@
         expo = jnp.exp(scores - jnp.max(scores, axis=-1, keepdims=True))
         return expo * (1.0 / jnp.sum(expo, axis=-1, keepdims=True))
 
-    def attend():
+    def attend(part):
         def body(two, _):
             query, key, value = (s.mixed[:, lanes(128 * two + part, 128)] for part in (0, D, 2 * D))
             found = jnp.zeros((TOKENS, 128), F32)
@@ -678,7 +735,7 @@
             s.attended[:, lanes(128 * two, 128)] = found.astype(BF16)
             return 0
 
-        lax.fori_loop(0, HEADS // 2, body, 0)
+        lax.fori_loop(3 * part, 3 * part + 3, body, 0)
 
     def project_out():
         s.middle[...] = dot(s.attended[...], s.w_out[...].reshape(D, D))
@@ -718,14 +775,20 @@
 
         lax.fori_loop(0, 2, body, 0)
 
-    valid = frame_valid[blk].astype(F32)
+    ours_rows = pl.ds(pl.multiple_of(128 * y, 128), 128)
+    theirs_rows = pl.ds(pl.multiple_of(128 * (1 - y), 128), 128)
+    across_y = 2 * (1 - y) + core
+    valid, valid_across = frame_valid[blk].astype(F32), frame_valid[across_y].astype(F32)
 
     def mask_cotangent():
-        def body(rows, _):
-            s.g_branch2[rows, :] = (s.cot_in[rows, :].astype(F32) * valid).astype(BF16)
-            return 0
-
-        by_rows(body, 0)
+        for frame, factor in enumerate((valid, valid_across)):
+
+            def body(rows, _):
+                there = pl.ds(pl.multiple_of(rows.start + 256 * frame, ROWS), ROWS)
+                s.g_branch2[there, :] = (s.cot_in[there, :].astype(F32) * factor).astype(BF16)
+                return 0
+
+            by_rows(body, 0)
 
 
     class Scatter:
@@ -734,6 +797,7 @@
         def __init__(self, own, other, pr, dx, dy, px, py, pz, finish, low=2):
             self.own, self.other, self.finish = own, other, finish
             self.pr, self.dx, self.dy, self.px, self.py, self.pz = pr, dx, dy, px, py, pz
+            self.square, self.by_z = Group(), Group()
             self.low, self.high = pl.ds(0, low), pl.ds(low, 4 - low)
 
         def s(self):
@@ -754,24 +818,23 @@
             low, high = self.low, self.high
             self.a = remote(self.own(low, at_d), self.dx(low), x_peer)
             self.b = remote(self.own(high, at_d), self.dy(high), y_peer)
-            self.c = remote(self.own(low, at_x), self.px(low), x_peer)
-            self.d = remote(self.own(high, at_y), self.py(high), y_peer)
+            remote(self.own(low, at_x), self.px(low), x_peer, self.square)
+            remote(self.own(high, at_y), self.py(high), y_peer, self.square)
 
         def f(self):
             self.a.wait_recv()
             ref = self.own(self.low, at_y)
             ref[...] = ref[...] + self.dx(self.low)[...]
-            self.e = remote(ref, self.py(self.low), y_peer)
+            remote(ref, self.py(self.low), y_peer, self.square)
 
         def g(self):
             self.b.wait_recv()
             ref = self.own(self.high, at_x)
             ref[...] = ref[...] + self.dy(self.high)[...]
-            self.f_copy = remote(ref, self.px(self.high), x_peer)
+            remote(ref, self.px(self.high), x_peer, self.square)
 
         def z(self):
-            for copy in (self.c, self.d, self.e, self.f_copy):
-                copy.wait_recv()
+            self.square.wait(self.own(ALL, BOTH))
 
             def add(level, _):
                 ref = self.own(level, here)
@@ -783,13 +846,11 @@
                 return 0
 
             lax.fori_loop(0, 4, add, 0)
-            self.z_copies = [
-                remote(self.own(z_of[step], here), self.pz(step - 1), z_peers[step]) for step in (1, 2, 3)
-            ]
+            for step in (1, 2, 3):
+                remote(self.own(z_of[step], here), self.pz(step - 1), z_peers[step], self.by_z)
 
         def l(self):
-            for copy in self.z_copies:
-                copy.wait_recv()
+            self.by_z.wait(self.pz(THREE))
             self.finish(self)
 
         def summed(self, view):
@@ -802,16 +863,15 @@
         def __init__(self, own, other, pr, bz, pz, finish):
             self.own, self.other, self.finish = own, other, finish
             self.pr, self.bz, self.pz = pr, bz, pz
+            self.square, self.by_z = Group(), Group()
 
         def z(self):
             self.add_pair()
-            self.z_copies = [
-                remote(self.own(z_of[step], ALL), self.bz(step - 1, ALL), z_peers[step]) for step in (1, 2, 3)
-            ]
+            for step in (1, 2, 3):
+                remote(self.own(z_of[step], ALL), self.bz(step - 1, ALL), z_peers[step], self.by_z)
 
         def p(self):
-            for copy in self.z_copies:
-                copy.wait_recv()
+            self.by_z.wait(self.bz(THREE, ALL))
 
             def add(place, _):
                 ref = self.own(z, place)
@@ -823,19 +883,18 @@
 
             lax.fori_loop(0, 4, add, 0)
             targets = ((at_x, x_peer), (at_y, y_peer), (at_d, d_peer))
-            self.square = [
-                remote(self.own(z, place), self.pz(i), peer) for i, (place, peer) in enumerate(targets)
-            ]
+            for i, (place, peer) in enumerate(targets):
+                remote(self.own(z, place), self.pz(i), peer, self.square)
 
         def l(self):
-            for copy in self.square:
-                copy.wait_recv()
+            self.square.wait(self.pz(THREE))
             self.finish(self)
 
     class PlaneScatter(Scatter):
         def __init__(self, own, other, pr, px, pz, finish, across=None):
             self.own, self.other, self.finish, self.across = own, other, finish, across
             self.pr, self.px, self.pz = pr, px, pz
+            self.by_z = Group()
 
         def x(self):
             self.add_pair()
@@ -850,19 +909,19 @@
                 return 0
 
             lax.fori_loop(0, 4, add, 0)
-            self.z_copies = [
-                remote(self.own(z_of[step], x), self.pz(step - 1), z_peers[step]) for step in (1, 2, 3)
-            ]
+            for step in (1, 2, 3):
+                remote(self.own(z_of[step], x), self.pz(step - 1), z_peers[step], self.by_z)
 
         def y(self):
-            for copy in self.z_copies:
-                copy.wait_recv()
+            self.by_z.wait(self.pz(THREE))
             source, target = self.across(self)
             self.y_copy = remote(source, target, y_peer)
 
         def l(self):
-            for copy in [self.y_copy] if self.across else self.z_copies:
-                copy.wait_recv()
+            if self.across:
+                self.y_copy.wait_recv()
+            else:
+                self.by_z.wait(self.pz(THREE))
             self.finish(self)
 
         def summed(self, view):
@@ -871,21 +930,48 @@
                 found = found + view(self.pz(i))[...].astype(F32)
             return found
 
-    def columns_of(ref, base, half, start, size):
+    class AcrossScatter(Scatter):
+        def __init__(self, own, other, pr, bz, px, finish):
+            self.own, self.other, self.finish = own, other, finish
+            self.pr, self.bz, self.px = pr, bz, px
+            self.by_z = Group()
+
+        def z(self):
+            self.add_pair()
+            for step in (1, 2, 3):
+                remote(self.own(z_of[step], ALL), self.bz(step - 1), z_peers[step], self.by_z)
+
+        def x(self):
+            self.by_z.wait(self.bz(THREE))
+            ref = self.own(z, ALL)
+            found = ref[...].astype(F32)
+            for i in range(3):
+                found = found + self.bz(i)[...].astype(F32)
+            ref[...] = found.astype(BF16)
+            self.x_copy = remote(self.own(z, 1 - x), self.px(), x_peer)
+
+        def l(self):
+            self.x_copy.wait_recv()
+            self.finish(self)
+
+        def summed(self, view):
+            return view(self.own(z, x))[...].astype(F32) + view(self.px())[...].astype(F32)
+
+    def columns_of(ref, columns, size):
         def own(levels, places):
-            return ref.at[levels, places, :, lanes(base + half * core + start, size)]
+            return ref.at[levels, places, :, lanes(columns(core), size)]
 
         def other():
-            return ref.at[:, :, :, lanes(base + half * (1 - core) + start, size)]
+            return ref.at[:, :, :, lanes(columns(1 - core), size)]
 
         return own, other
 
-    def column_scatter(ref, base, half, start, size, spot, output, way):
+    def column_scatter(ref, columns, size, spot, output, way):
         at = pl.ds(spot, size)
 
         def finish(scatter):
             s.last_a[:, at] = scatter.summed(lambda ref: ref)
-            target = lanes(half * core + start, size)
+            target = lanes(columns(core), size)
             other_rows = pl.ds(pl.multiple_of(24 * (1 - core), 8), 24)
             finals.append(remote(s.last_a.at[other_rows, at], output.at[:, target], sibling))
             output[:, target] = s.last_a[own_rows, at]
@@ -893,14 +979,14 @@
         if not way:
             extra = pl.ds(spot, size)
             return SquareScatter(
-                *columns_of(ref, base, half, start, size),
+                *columns_of(ref, columns, size),
                 lambda levels, places: s.pr_a.at[levels, places, :, at],
                 lambda i, places: s.bz_a.at[i, places, :, extra],
                 lambda i: s.pz_a.at[i, :, at],
                 finish,
             )
         return Scatter(
-            *columns_of(ref, base, half, start, size),
+            *columns_of(ref, columns, size),
             lambda levels, places: s.pr_a.at[levels, places, :, at],
             lambda levels: s.dx_a.at[levels, :, at],
             lambda levels: s.dx_a.at[levels, :, at],
@@ -944,7 +1030,7 @@
             across,
         )
 
-    def fc2_scatter(j, size):
+    def fc2_scatter(j, size, way):
         rows = pl.ds(size * j, size)
         half = lanes(384 * core, 384)
 
@@ -953,10 +1039,19 @@
             finals.append(remote(s.last_fc2.at[rows, :], grad_fc2.at[rows, half], sibling))
             grad_fc2[rows, half] = scatter.summed(lambda ref: ref.at[core])
 
+        def sides(side):
+            return BOTH if side is ALL else side
+
+        own = lambda levels, side: s.g_fc2.at[levels, sides(side), :, rows, half]
+        other = lambda: s.g_fc2.at[:, :, :, rows, lanes(384 * (1 - core), 384)]
+        pr = lambda levels, side: s.pr_fc2.at[levels, sides(side), :, rows, :]
+        if not way:
+            bz = lambda i: s.bz_fc2.at[i, :, :, rows, :]
+            return AcrossScatter(own, other, pr, bz, lambda: s.pz_fc2.at[0, :, rows, :], finish)
         return PlaneScatter(
-            lambda levels, side: s.g_fc2.at[levels, side if side is not ALL else BOTH, :, rows, half],
-            lambda: s.g_fc2.at[:, :, :, rows, lanes(384 * (1 - core), 384)],
-            lambda levels, side: s.pr_fc2.at[levels, side if side is not ALL else BOTH, :, rows, :],
+            own,
+            other,
+            pr,
             lambda levels: s.px_fc2.at[levels, :, rows, :],
             lambda i: s.pz_fc2.at[i, :, rows, :],
             finish,
@@ -972,21 +1067,17 @@
 
     finals = []
     scatters = {}
-    for j in range(FC2_SCATTERS):
-        scatters["f" + str(j)] = fc2_scatter(j, 96 // FC2_SCATTERS)
+    for j, way in enumerate(SCATTER_WAYS["f"]):
+        scatters["f" + str(j)] = fc2_scatter(j, 96 // len(SCATTER_WAYS["f"]), way)
     for j in range(2):
         scatters["h" + str(j)] = fc1_scatter(j)
-    for name, ref, half, spot, output in (
-        ("o", s.g_out, 384, 0, grad_out),
-        ("q", s.g_qkv, 1152, 384, grad_qkv),
-    ):
-        for j in range(half // 384):
-            way = SCATTER_WAYS[name][j]
-            scatters[name + str(j)] = column_scatter(
-                ref, 0, half, 384 * j, 384, spot + 384 * j, output, way
-            )
+    scatters["o0"] = column_scatter(s.g_out, lambda side: 384 * side, 384, 0, grad_out, SCATTER_WAYS["o"][0])
+    for j in range(3):
+        scatters["q" + str(j)] = column_scatter(
+            s.g_qkv, partial(tile, j), 384, 384 + 384 * j, grad_qkv, SCATTER_WAYS["q"][j]
+        )
     scatters["s0"] = Scatter(
-        *columns_of(s.g_small, 0, 128, 0, 128),
+        *columns_of(s.g_small, lambda side: 128 * side, 128),
         lambda levels, places: s.pr_small.at[levels, places],
         lambda levels: s.dx_small.at[levels],
         lambda levels: s.dx_small.at[levels],
@@ -997,7 +1088,7 @@
     )
 
     def weight_grad_fc2(j):
-        size = 96 // FC2_SCATTERS
+        size = 96 // len(SCATTER_WAYS["f"])
         rows = pl.ds(size * j, size)
 
         def body(turn, _):
@@ -1008,49 +1099,62 @@
 
         lax.fori_loop(0, 2, body, 0)
 
-    def column_grad(left, right, start, ref, base, half, size):
+    def column_grad(left, right, ref, columns):
         def body(turn, _):
-            side = turn * core + (1 - turn) * (1 - core)
-            found = dot(left[...], right[:, lanes(half * side + start, size)])
-            ref[:, :, :, lanes(base + half * side + start, size)] = found.astype(BF16).reshape(4, 4, 48, size)
+            at = lanes(columns(turn * core + (1 - turn) * (1 - core)), 384)
+            ref[:, :, :, at] = dot(left[...], right[:, at]).astype(BF16).reshape(4, 4, 48, 384)
             return 0
 
         lax.fori_loop(0, 2, body, 0)
-
-    def column_sums(ref, width):
-        return jnp.sum(ref[...].astype(F32), axis=0, keepdims=True)
 
     def feed_back(frame):
         tokens = pl.ds(256 * frame, 256)
-        s.total[...] = jnp.zeros((TOKENS, D), F32)
 
         def body(part, _):
             columns = lanes(D * part, D)
-            weight = s.w_fc2[pl.ds(2 * part, 2)].reshape(D, D)
-            s.total[...] += dot(s.active[tokens, columns], weight)
-            s.other[...] = dot_nt(s.g_branch2[tokens, :], weight)
+            s.other[...] = dot_nt(s.g_branch2[tokens, :], s.w_fc2[pl.ds(2 * part, 2)].reshape(D, D))
 
             def slope(rows, sums):
                 there = pl.ds(pl.multiple_of(rows.start + 256 * frame, ROWS), ROWS)
                 found = (s.other[rows, :] * s.slope[there, columns]).astype(BF16)
-                s.active[there, columns] = found
+                s.g_hidden[there, columns] = found
                 return sums + jnp.sum(found.astype(F32), axis=0, keepdims=True)
 
             s.sums_fc1[frame : frame + 1, columns] = by_rows(slope, jnp.zeros((1, D), F32))
             return 0
 
         lax.fori_loop(0, 2, body, 0)
+
+    def feed_out(frame):
+        tokens = pl.ds(256 * frame, 256)
+        s.total[...] = jnp.zeros((TOKENS, D), F32)
+
+        def body(part, _):
+            weight = s.w_fc2[pl.ds(2 * part, 2)].reshape(D, D)
+            s.total[...] += dot(s.active[tokens, lanes(D * part, D)], weight)
+            return 0
+
+        lax.fori_loop(0, 2, body, 0)
         if frame:
-            s.part_send[0] = s.total[...].astype(BF16)
+            s.part_across[...] = s.total[...].astype(BF16)
+        else:
+
+            def add(rows, _):
+                s.total[rows, :] = s.middle[rows, :] + (s.total[rows, :] + s.par[7:8, :])
+                return 0
+
+            by_rows(add, 0)
+            s.base_send[...] = (valid * s.total[theirs_rows, :]).astype(BF16)
 
     def output():
-        def finish(rows, sums):
-            branch = s.total[rows, :] + s.part_recv[0, rows, :].astype(F32)
-            found = valid * (s.middle[rows, :] + (branch + s.par[7:8, :]))
-            s.enc_send[rows, :] = found.astype(BF16)
+        s.enc_send[0] = (valid * (s.total[ours_rows, :] + s.part_recv[...].astype(F32))).astype(BF16)
+        part = valid_across * s.part_across[ours_rows, :].astype(F32)
+        s.enc_send[1] = (s.base_recv[...].astype(F32) + part).astype(BF16)
+
+        def body(rows, sums):
             return sums + jnp.sum(s.g_branch2[rows, :].astype(F32), axis=0, keepdims=True)
 
-        s.sums[7:8, :] = by_rows(finish, jnp.zeros((1, D), F32))
+        s.sums[7:8, :] = by_rows(body, jnp.zeros((1, D), F32))
 
     def feed_back_rows(frame):
         tokens = pl.ds(256 * frame, 256)
@@ -1058,12 +1162,12 @@
 
         def body(part, _):
             columns = lanes(D * part, D)
-            s.other[...] += dot_nt(s.active[tokens, columns], s.w_fc1[:, :, :, columns].reshape(D, D))
+            s.other[...] += dot_nt(s.g_hidden[tokens, columns], s.w_fc1[:, :, :, columns].reshape(D, D))
             return 0
 
         lax.fori_loop(0, 2, body, 0)
         if frame:
-            s.part_send[1] = s.other[...].astype(BF16)
+            s.back_send[...] = s.other[...].astype(BF16)
 
     def norm_back(upstream, found, scale, gain):
         weighted = upstream * gain
@@ -1078,7 +1182,7 @@
 
     def second_norm_back():
         def rows_back(rows, sums):
-            upstream = s.other[rows, :] + s.part_recv[1, rows, :].astype(F32)
+            upstream = s.other[rows, :] + s.back_recv[rows, :].astype(F32)
             found, scale = standardized(s.middle[rows, :])
             middle = s.g_branch2[rows, :].astype(F32) + norm_back(upstream, found, scale, s.par[1:2, :])
             s.g_middle[rows, :] = middle
@@ -1093,7 +1197,7 @@
         empty = jnp.zeros((1, D), F32)
         s.sums[1:2, :], s.sums[3:4, :], s.sums[6:7, :] = by_rows(rows_back, (empty, empty, empty))
 
-    def attend_back():
+    def attend_back(part):
         def body(two, _):
             spots = [lanes(128 * two + part, 128) for part in (0, D, 2 * D)]
             query, key, value = (s.mixed[:, spot] for spot in spots)
@@ -1116,7 +1220,7 @@
             s.sums[5:6, spots[0]] = column_sum(g_value.astype(F32))
             return 0
 
-        lax.fori_loop(0, HEADS // 2, body, 0)
+        lax.fori_loop(3 * part, 3 * part + 3, body, 0)
 
     def first_norm_back():
         s.total[...] = jnp.zeros((TOKENS, D), F32)
@@ -1157,27 +1261,21 @@
             here_ = s.g_small.at[:, :, :, pl.ds(128 * side, 128)]
             here_[...] = here_[...] + dot(put, placed).astype(BF16).reshape(4, 4, 16, 128)
 
-    def to_patches(source, target):
-        return [
-            remote(
-                source.at[pl.ds(pl.multiple_of(64 * (2 * py + pc), 64), 64), :],
-                target.at[blk],
-                (wide, 2 * py + pc),
-            )
-            for py, pc in blk_peers
-        ]
-
-    moved = {}
-
-    def send_rows():
-        moved["rows"] = to_frames(patches, s.rows_in)
+    moved = {"rows": (rows_moved, s.rows_in.at[0:192, :])}
 
     def send_cotangent():
-        moved["cot"] = to_frames(cotangent, s.cot_in)
+        group = Group()
+        after = pl.ds(pl.multiple_of(64 * blk + 256, 64), 64)
+        for py, pc in blk_peers:
+            for there, frame in ((mine, 2 * py + pc), (after, 2 * (1 - py) + pc)):
+                remote(cotangent.at[frame], s.cot_in.at[there, :], (wide, 2 * py + pc), group)
+        moved["cot"] = group, s.cot_in.at[0:384, :]
+        s.cot_in[mine, :] = cotangent[blk]
+        s.cot_in[after, :] = cotangent[across_y]
 
     def received(name):
-        for copy in moved.pop(name):
-            copy.wait_recv()
+        group, ref = moved.pop(name)
+        group.wait(ref)
 
     def start_norm():
         received("rows")
@@ -1188,22 +1286,33 @@
         mask_cotangent()
 
     def send_encoded():
-        moved["enc"] = to_patches(s.enc_send, encoded)
-        encoded[blk] = s.enc_send[mine, :]
+        ours = pl.ds(pl.multiple_of(64 * core, 64), 64)
+        theirs = pl.ds(pl.multiple_of(64 * (1 - core), 64), 64)
+        group = Group()
+        for i, frame in enumerate((blk, across_y)):
+            remote(s.enc_send.at[i, theirs, :], encoded.at[frame], sibling, group)
+        moved["enc"] = group, encoded.at[BOTH]
+        encoded[blk] = s.enc_send[0, ours, :]
+        encoded[across_y] = s.enc_send[1, ours, :]
 
     def send_grad_rows():
-        moved["grad"] = to_patches(s.gx_send, s.gx_recv)
+        group = Group()
+        for py, pc in blk_peers:
+            rows = pl.ds(pl.multiple_of(64 * (2 * py + pc), 64), 64)
+            remote(s.gx_send.at[rows, :], s.gx_recv.at[blk], (wide, 2 * py + pc), group)
+        moved["grad"] = group, s.gx_recv.at[THREE]
         s.gx_recv[blk] = s.gx_send[mine, :]
 
     def project_attended():
         s.g_attended[...] = dot_nt(s.g_branch[...], s.w_out[...].reshape(D, D)).astype(BF16)
 
     def project_both(j):
-        project_qkv(j)
-        project_qkv(j + 3)
+        project_qkv(tile(j, 0))
+        project_qkv(tile(j, 1))
 
     def across(name, source, target):
-        moved[name] = [remote(source, target, y_peer)]
+        moved[name] = Group(), target
+        remote(source, target, y_peer, moved[name][0])
 
     def send_normed():
         across("normed", s.normed2.at[0:256, :], s.normed2.at[256:512, :])
@@ -1214,211 +1323,230 @@
     def transpose_other():
         s.normed2_t[:, 256:512] = s.normed2[256:512, :].T
 
-    def send_masked():
-        across("masked", s.g_branch2.at[0:256, :], s.g_branch2.at[256:512, :])
-
-    def take_masked():
-        received("masked")
-
     def send_part():
-        across("part", s.part_send.at[0], s.part_recv.at[0])
+        across("part", s.part_across.at[theirs_rows, :], s.part_recv)
+
+    def send_base():
+        across("base", s.base_send, s.base_recv)
 
     def start_output():
         received("part")
+        received("base")
         output()
 
     def send_back():
-        across("back", s.part_send.at[1], s.part_recv.at[1])
+        across("back", s.back_send, s.back_recv)
 
     def start_second():
         received("back")
         second_norm_back()
 
     def grad_fc1_weight(j):
-        column_grad(s.normed2_t, s.active, 384 * j, s.g_fc1, 0, 768, 384)
+        column_grad(s.normed2_t, s.g_hidden, s.g_fc1, lambda side: 768 * side + 384 * j)
 
     def grad_out_weight():
-        column_grad(s.attended_t, s.g_branch, 0, s.g_out, 0, 384, 384)
+        column_grad(s.attended_t, s.g_branch, s.g_out, lambda side: 384 * side)
 
     def grad_qkv_weight(j):
-        column_grad(s.normed_t, s.g_mixed, 384 * j, s.g_qkv, 0, 1152, 384)
+        column_grad(s.normed_t, s.g_mixed, s.g_qkv, partial(tile, j))
 
     g, r = types.SimpleNamespace(**gathers), types.SimpleNamespace(**scatters)
-    g.h1.y()
     g.s0.z()
-    g.o0.z()
-    send_cotangent()
-    g.h0.y()
     g.q0.z()
     g.q1.z()
+    g.q2.z()
+    g.q1.o()
+    g.f2.x()
+    g.o0.z()
     g.s0.p()
+    g.q2.o()
+    g.q0.o()
+    g.h0.y()
     g.s0.f()
+    g.o0.o()
+    g.q0.p()
+    g.s0.g()
+    g.h1.y()
+    g.h0.z()
+    g.q1.p()
+    g.s0.l()
+    g.q0.f()
+    g.q0.g()
+    g.h1.z()
+    g.q2.p()
     g.o0.p()
-    g.q0.p()
-    g.q2.z()
-    g.q1.p()
-    g.o0.f()
-    g.h0.z()
-    g.s0.g()
-    g.q0.f()
-    start_cotangent()
-    g.q2.p()
-    g.o0.g()
     g.q1.f()
     g.q1.g()
-    g.q0.g()
-    g.s0.l()
-    g.h1.z()
+    g.f0.z()
+    g.q0.l()
+    g.s0.d()
+    unpack_small()
     g.q2.f()
     g.q2.g()
+    g.o0.f()
+    g.q0.d()
+    start_norm()
+    g.o0.g()
+    g.f1.z()
     g.h0.x()
-    send_rows()
+    project_both(0)
     g.q1.l()
-    g.q0.l()
+    send_cotangent()
+    g.q2.l()
+    g.q1.d()
+    project_both(1)
+    attend(0)
+    g.q2.d()
+    project_both(2)
     g.o0.l()
-    g.s0.d()
-    g.f0.z()
-    g.f1.z()
-    unpack_small()
     g.f2.z()
-    g.q0.d()
     g.h1.x()
-    send_masked()
-    g.q2.l()
-    start_norm()
-    project_both(0)
-    g.q1.d()
-    g.q2.d()
-    project_both(1)
-    project_both(2)
-    attend()
+    attend(1)
     g.o0.d()
     project_out()
     send_normed()
+    g.h0.l()
+    transpose_out()
+    g.h0.d()
     g.f0.x()
+    feed(0, 0)
+    start_cotangent()
+    g.f1.x()
     g.h1.l()
-    g.f1.x()
-    g.h0.l()
-    g.h0.d()
-    take_masked()
-    g.f2.x()
     g.h1.d()
+    feed(1, 0)
     g.f0.l()
-    feed(1, 0)
-    transpose_out()
-    feed(0, 0)
     take_normed()
     feed(1, 1)
     feed(0, 1)
+    weight_grad_fc2(1)
+    r.f1.s()
+    g.f1.l()
+    g.f2.l()
     weight_grad_fc2(2)
     r.f2.s()
-    g.f1.l()
-    weight_grad_fc2(1)
-    r.f2.x()
-    g.f2.l()
+    r.f1.x()
     weight_grad_fc2(0)
-    g.f1.d()
-    r.f1.s()
-    g.f0.d()
     r.f0.s()
     g.f2.d()
+    g.f1.d()
+    g.f0.d()
     feed_back(1)
     feed_back_rows(1)
     send_back()
     transpose_other()
-    r.f1.x()
-    r.f0.x()
+    r.f0.z()
+    r.f2.x()
     feed_back(0)
-    grad_fc1_weight(0)
-    send_part()
     grad_fc1_weight(1)
     r.h1.s()
+    grad_fc1_weight(0)
+    r.h1.x()
+    feed_out(1)
+    feed_out(0)
     r.h0.s()
     r.f2.z()
+    send_part()
     r.f1.z()
     feed_back_rows(0)
-    r.h1.x()
     r.h0.x()
+    send_base()
     start_second()
+    project_attended()
     grad_out_weight()
     r.o0.s()
-    r.f0.z()
-    project_attended()
+    attend_back(0)
+    grad_qkv_weight(0)
+    r.q0.s()
+    r.h1.z()
     r.o0.p()
-    attend_back()
+    r.q0.p()
+    attend_back(1)
     grad_qkv_weight(2)
     r.q2.s()
-    r.h1.z()
-    start_output()
-    send_encoded()
-    r.q2.p()
     r.h0.z()
-    grad_qkv_weight(1)
-    r.q1.s()
-    r.f1.l()
     r.o0.f()
     r.o0.g()
-    r.q1.p()
-    grad_qkv_weight(0)
+    grad_qkv_weight(1)
+    r.q2.p()
+    r.q0.f()
+    r.q0.g()
+    r.q1.s()
+    start_output()
+    first_norm_back()
     r.q2.f()
     r.q2.g()
-    first_norm_back()
     r.o0.z()
-    r.f2.l()
-    r.q1.f()
-    r.q0.s()
-    r.q1.g()
+    r.q1.p()
+    r.q0.z()
     pack_small()
     r.s0.s()
+    r.s0.p()
+    r.q1.f()
+    r.q1.g()
+    r.f0.x()
+    r.q2.z()
+    r.h1.y()
+    r.o0.l()
+    r.h0.y()
+    r.q0.l()
+    r.s0.f()
+    r.s0.g()
+    send_grad_rows()
+    r.f1.l()
+    r.f2.l()
+    r.q1.z()
+    r.q2.l()
+    send_encoded()
+    r.h1.l()
     r.f0.l()
-    r.q0.p()
-    r.q2.z()
-    r.s0.p()
-    r.q0.f()
-    r.q1.z()
-    r.q0.g()
-    r.h1.y()
-    r.s0.f()
-    r.h0.y()
-    send_grad_rows()
-    r.q2.l()
-    r.s0.g()
-    r.q0.z()
     r.s0.z()
-    r.o0.l()
+    r.h0.l()
     r.q1.l()
-    r.h1.l()
-    r.h0.l()
-    r.q0.l()
     r.s0.l()
     for name in list(moved):
         received(name)
     for copy in finals:
         copy.wait_recv()
     grad_patches[...] = s.gx_recv[...].astype(F32)
-    sent(started)
+    for copy in started[-SENDS:]:
+        copy.wait_send()
 
 
 def emit_kernel(*refs):
-    count = len(refs) // 2
+    count = (len(refs) - 3) // 3
+    given, made, held = refs[:count], refs[count : 2 * count], refs[2 * count : 3 * count]
+    ordered, in_sem, out_sem = refs[3 * count :]
+    arrive = [pltpu.make_async_copy(given[i], held[i], in_sem.at[i]) for i in range(count)]
+    leave = [
+        pltpu.make_async_copy(ordered if i == FC1_OUTPUT else held[i], made[i], out_sem.at[i]) for i in range(count)
+    ]
+    for copy in arrive:
+        copy.start()
     for i in range(count):
+        arrive[i].wait()
         if i == FC1_OUTPUT:
             for side in (0, 1):
                 for k in range(8):
-                    source = refs[i][:, 1536 * side + 192 * k : 1536 * side + 192 * k + 192]
-                    refs[count + i][:, 384 * k + 192 * side : 384 * k + 192 * side + 192] = source
-        else:
-            refs[count + i][...] = refs[i][...]
+                    source = held[i][:, 1536 * side + 192 * k : 1536 * side + 192 * k + 192]
+                    ordered[:, 384 * k + 192 * side : 384 * k + 192 * side + 192] = source
+        leave[i].start()
+    for copy in leave:
+        copy.wait()
 
 
 def emit(arrays):
-    vmem = pl.BlockSpec(memory_space=pltpu.VMEM)
+    anywhere = pl.BlockSpec(memory_space=pl.ANY)
+    count = len(arrays)
     return list(
         pl.pallas_call(
             emit_kernel,
             out_shape=[jax.ShapeDtypeStruct(a.shape, a.dtype) for a in arrays],
-            in_specs=[vmem] * len(arrays),
-            out_specs=[vmem] * len(arrays),
+            in_specs=[anywhere] * count,
+            out_specs=[anywhere] * count,
+            scratch_shapes=[pltpu.VMEM(a.shape, a.dtype) for a in arrays]
+            + [pltpu.VMEM(arrays[FC1_OUTPUT].shape, F32)]
+            + [pltpu.SemaphoreType.DMA((count,))] * 2,
         )(*arrays)
     )
 

time: 128 us -> 119 us (0.930)
  Pallas kernels: 127 us -> 118 us
    pallas_call x1, Pallas kernels: 124 us -> 115 us  [fast(): pl.pallas_call(layer_kernel, out_shape=[jax.ShapeDtypeStruct(shape, dtype...]
where the time goes in v4:
time: 119 us
  Pallas kernels  118 us (99%)
    pallas_call x1, Pallas kernels, fast(): pl.pallas_call(layer_kernel, out_shape=[jax.ShapeDtypeStruct(shape, dtype...  115 us
    pallas_call x1, Pallas kernels, emit(): pl.pallas_call(emit_kernel, out_shape=[jax.ShapeDtypeStruct(a.shape, a.dt...  2.64 us

profile of v4, /device:TPU:0, one launch (start us, length us, event | category | flops | bytes accessed | tf_op | source)
XLA Modules:
  0.0 118.6 jit_solution(7219730157506135958)
XLA Ops:
  0.6 115.1 %shard_map.203 = (bf16[4,64,768]{2,1,0:T(8,128)(2,1)}, f32[4,64,768]{2,1,0:T(8,128)}, f32[2,24]{1,0:T(2,128)}, f32[2,24]{1,0:T(2,128)}, f32[24,2304]{1,0:T(8,128...) custom-call(bf16[4,64,768]{2,1,0:T(8,128)(2,1)} %patches.1, ...), custom_call_target="tpu_custom_call" | custom-call | tf_op jit(solution)/shard_map/pallas_call | solution.py:1582
  115.8 2.6 %shard_map.204 = (bf16[4,64,768]{2,1,0:T(8,128)(2,1)}, f32[4,64,768]{2,1,0:T(8,128)}, f32[2,24]{1,0:T(2,128)}, f32[2,24]{1,0:T(2,128)}, f32[24,2304]{1,0:T(8,128...) custom-call(bf16[4,64,768]{2,1,0:T(8,128)(2,1)} %get-tuple-element.3, ...), custom_call_target="tpu_custom_call" | custom-call | tf_op jit(solution)/shard_map/pallas_call | solution.py:1542

commit v5 on v4

--- a/solution.py
+++ b/solution.py
@@ -257,8 +257,10 @@
 TOKENS = 256
 ROWS = 64
 ALL, THREE, BOTH = pl.ds(0, 4), pl.ds(0, 3), pl.ds(0, 2)
-GATHER_WAYS = dict(q=(-2, -2, -2), o=(-2,), f=(1, 1, 0))
-SCATTER_WAYS = dict(f=(0, 1, 1), o=(2,), q=(2, 2, 2))
+GATHER_WAYS = dict(q=(-1, -2, -2), o=(-1,), f=(1, 0, 0))
+SCATTER_WAYS = dict(f=(0, 0, 1), o=(2,), q=(2, 2, 2))
+GATHER_LINES = dict(q=(0, 0, 0), o=(0,), h=(1, 1), f=(1, 1, 1))
+SCATTER_LINES = dict(q=(0, 0, 0), o=(0,), h=(1, 1), f=(1, 1, 1))
 
 
 TILES = ((0, 1536), (768, 384), (1920, 1152))
@@ -281,7 +283,7 @@
     return lax.dot_general(left, right, (((0,), (0,)), ((), ())), preferred_element_type=F32)
 
 
-SENDS, ARRIVALS = 80, 130
+SENDS, ARRIVALS = 80, 150
 FC1_OUTPUT = 7
 
 
@@ -356,7 +358,12 @@
         pz_fc1=vm(3, 2, 48, 768),
         pz_fc2=vm(3, 2, 96, 384),
         bz_a=vm(3, 4, 48, 1536),
+        cz_a=vm(3, 4, 48, 1536),
+        qz_a=vm(3, 48, 1536),
+        qz_fc1=vm(3, 2, 48, 768),
+        qz_fc2=vm(3, 2, 96, 384),
         bz_fc2=vm(3, 2, 2, 96, 384),
+        cz_fc2=vm(3, 2, 2, 96, 384),
         last_a=vm(48, 1536, dtype=F32),
         last_fc1=vm(2, 48, 768, dtype=F32),
         send_fc1=vm(48, 768),
@@ -404,6 +411,10 @@
     y_cross = (wide, 2 * (1 - y) + 1 - core)
     z_of = [lax.rem(z + step, 4) for step in range(4)]
     z_peers = [(2 * z_of[step] + x, blk) for step in range(4)]
+    z_order = (z_peers[1], z_peers[3], z_peers[2])
+    inner, end = lax.rem(z + 1, 4) >= 2, lax.rem(z + 1, 4) < 2
+    z_in, z_out = 1 + lax.rem(z, 2), 3 * lax.div(z, 2)
+    in_peer, out_peer = (2 * z_in + x, blk), (2 * z_out + x, blk)
     blk_peers = [(y, 1 - core), (1 - y, core), (1 - y, 1 - core)]
 
     barrier = pltpu.get_barrier_semaphore()
@@ -421,10 +432,17 @@
         def wait(self, ref):
             pltpu.make_async_copy(ref, ref, self.sem).wait()
 
-    def remote(source, target, peer, group=None):
+    def leave(spot):
+        copy, only = started[spot]
+        if only is None:
+            copy.wait_send()
+        else:
+            pl.when(only)(copy.wait_send)
+
+    def prepare(source, target, peer, group=None, only=None):
         spot = len(started)
         if spot >= SENDS:
-            started[spot - SENDS].wait_send()
+            leave(spot - SENDS)
         copy = pltpu.make_async_remote_copy(
             src_ref=source,
             dst_ref=target,
@@ -433,8 +451,15 @@
             device_id=peer,
             device_id_type=MESH_ID,
         )
-        copy.start()
-        started.append(copy)
+        started.append((copy, only))
+        return copy
+
+    def remote(source, target, peer, group=None, only=None):
+        copy = prepare(source, target, peer, group, only)
+        if only is None:
+            copy.start()
+        else:
+            pl.when(only)(copy.start)
         return copy
 
     def lanes(start, size):
@@ -477,18 +502,135 @@
         remote(patches.at[2 * py + pc], s.rows_in.at[mine, :], (wide, 2 * py + pc), rows_moved)
     s.rows_in[mine, :] = patches[blk]
 
-    class Gather:
-        def __init__(self, part, low):
+    class Direct:
+        def __init__(self, block):
+            self.block, self.arrived = block, Group()
+
+        def start(self):
+            own = self.block(z)
+            for peer in z_order:
+                remote(own, own, peer, self.arrived)
+
+        def wait(self):
+            self.arrived.wait(self.block(THREE))
+
+    class Line:
+        def __init__(self, block):
+            self.block, self.first = block, len(groups)
+            self.arrived = [Group() for _ in range(3)]
+
+        def start(self):
+            own = self.block(z)
+            to_in = types.SimpleNamespace(sem=s.recv_sem.at[self.first + lax.div(lax.rem(z + 1, 4), 2)])
+            remote(own, own, in_peer, to_in)
+            remote(own, own, out_peer, self.arrived[0], inner)
+
+        def pass_on(self):
+            outer, other = self.block(z_out), self.block(z_in)
+            inward = prepare(outer, outer, in_peer, self.arrived[2], inner)
+            outward = prepare(other, other, out_peer, self.arrived[1], inner)
+
+            @pl.when(inner)
+            def _():
+                self.arrived[0].wait(outer)
+                inward.start()
+                self.arrived[1].wait(other)
+                outward.start()
+
+        def pass_last(self):
+            far = self.block(3 - z_out)
+            outward = prepare(far, far, out_peer, self.arrived[2], inner)
+
+            @pl.when(inner)
+            def _():
+                self.arrived[2].wait(far)
+                outward.start()
+
+        def wait(self):
+            @pl.when(end)
+            def _():
+                for arrived, level in zip(self.arrived, (z_in, 3 - z_in, 3 - z)):
+                    arrived.wait(self.block(level))
+
+    class DirectSum:
+        def __init__(self, own, parts, _):
+            self.own, self.parts, self.arrived = own, parts, Group()
+
+        def start(self):
+            for step in (1, 3, 2):
+                remote(self.own(z_of[step]), self.parts(step - 1), z_peers[step], self.arrived)
+
+        def wait(self):
+            self.arrived.wait(self.parts(THREE))
+
+        def summed(self, view):
+            found = view(self.own(z))[...].astype(F32)
+            for i in range(3):
+                found = found + view(self.parts(i))[...].astype(F32)
+            return found
+
+    class LineSum:
+        def __init__(self, own, parts, more):
+            self.own, self.parts, self.more = own, parts, more
+            self.arrived = [Group() for _ in range(3)]
+
+        def start(self):
+            remote(self.own(pl.ds(1 - lax.div(z, 2), 3)), self.parts(THREE), in_peer, self.arrived[0], end)
+
+        def pass_on(self):
+            source = self.own(pl.ds(2 - 2 * lax.div(z, 2), 2))
+            inward = prepare(source, self.more(BOTH), in_peer, self.arrived[1], inner)
+
+            @pl.when(inner)
+            def _():
+                self.arrived[0].wait(self.parts(THREE))
+                for level in (z_in, 3 - z_out):
+                    ref = self.own(level)
+                    ref[...] = ref[...] + self.parts(level - 1 + lax.div(z, 2))[...]
+                inward.start()
+
+        def pass_last(self):
+            outward = prepare(self.own(z_out), self.more(2), out_peer, self.arrived[2], inner)
+
+            @pl.when(inner)
+            def _():
+                self.arrived[1].wait(self.more(BOTH))
+                base = 2 * lax.div(z, 2)
+                ref = self.own(z_out)
+                ref[...] = ref[...] + self.more(z_out - base)[...]
+                outward.start()
+                ref = self.own(z)
+                found = ref[...].astype(F32) + self.parts(z - 1 + lax.div(z, 2))[...].astype(F32)
+                ref[...] = (found + self.more(z - base)[...].astype(F32)).astype(BF16)
+
+        def wait(self):
+            @pl.when(end)
+            def _():
+                self.arrived[2].wait(self.more(2))
+                ref = self.own(z)
+                ref[...] = ref[...] + self.more(2)[...]
+
+        def summed(self, view):
+            return view(self.own(z))[...].astype(F32)
+
+    class Steps:
+        def w(self):
+            self.line.pass_on()
+
+        def v(self):
+            self.line.pass_last()
+
+    class Gather(Steps):
+        def __init__(self, part, low, line):
             self.part, self.low, self.high = part, pl.ds(0, low), pl.ds(low, 4 - low)
-            self.by_z, self.by_x, self.by_y, self.far, self.pair = (Group() for _ in range(5))
+            self.by_x, self.by_y, self.far, self.pair = (Group() for _ in range(4))
+            self.line = line(lambda levels: part(levels, here))
 
         def z(self):
-            own = self.part(z, here)
-            for peer in z_peers[1:]:
-                remote(own, own, peer, self.by_z)
+            self.line.start()
 
         def p(self):
-            self.by_z.wait(self.part(THREE, here))
+            self.line.wait()
             self.share(self.part(ALL, here))
 
         def share(self, block):
@@ -521,19 +663,20 @@
     class FineGather(Gather):
         def z(self):
             own = self.part(z, here)
-            self.z_copies = [remote(own, own, peer) for peer in z_peers[1:]]
+            self.z_copies = [remote(own, own, peer) for peer in z_order]
 
         def o(self):
             self.share(self.part(z, here))
 
         def p(self):
-            for step, copy in zip((1, 2, 3), self.z_copies):
+            for step, copy in zip((1, 3, 2), self.z_copies):
                 copy.wait_recv()
                 self.share(self.part(z_of[4 - step], here))
 
-    class SquareGather:
-        def __init__(self, part):
-            self.part, self.square, self.by_z, self.pair = part, Group(), Group(), Group()
+    class SquareGather(Steps):
+        def __init__(self, part, line):
+            self.part, self.square, self.pair = part, Group(), Group()
+            self.line = line(lambda levels: part(levels, ALL))
 
         def p(self):
             own = self.part(z, here)
@@ -542,13 +685,12 @@
 
         def z(self):
             self.square.wait(self.part(z, THREE))
+            self.line.start()
             level = self.part(z, ALL)
-            for peer in z_peers[1:]:
-                remote(level, level, peer, self.by_z)
             remote(level, level, sibling, self.pair)
 
         def l(self):
-            self.by_z.wait(self.part(THREE, ALL))
+            self.line.wait()
             for step in (1, 2, 3):
                 level = self.part(z_of[step], ALL)
                 remote(level, level, sibling, self.pair)
@@ -556,9 +698,10 @@
         def d(self):
             self.pair.wait(self.part(ALL, ALL))
 
-    class PlaneGather:
-        def __init__(self, part, across=None):
-            self.part, self.across, self.by_z, self.pair = part, across, Group(), Group()
+    class PlaneGather(Steps):
+        def __init__(self, part, line, across=None):
+            self.part, self.across, self.pair = part, across, Group()
+            self.line = line(lambda levels: part(levels, x))
 
         def y(self):
             source, target = self.across
@@ -567,12 +710,10 @@
         def z(self):
             if self.across:
                 self.y_copy.wait_recv()
-            own = self.part(z, x)
-            for peer in z_peers[1:]:
-                remote(own, own, peer, self.by_z)
+            self.line.start()
 
         def x(self):
-            self.by_z.wait(self.part(THREE, x))
+            self.line.wait()
             column = self.part(ALL, x)
             self.x_copy = remote(column, column, x_peer)
             remote(column, column, sibling, self.pair)
@@ -585,9 +726,10 @@
         def d(self):
             self.pair.wait(self.part(ALL, BOTH))
 
-    class AcrossGather:
-        def __init__(self, part):
-            self.part, self.by_z, self.pair = part, Group(), Group()
+    class AcrossGather(Steps):
+        def __init__(self, part, line):
+            self.part, self.pair = part, Group()
+            self.line = line(lambda levels: part(levels, BOTH))
 
         def x(self):
             own = self.part(z, x)
@@ -595,13 +737,12 @@
 
         def z(self):
             self.x_copy.wait_recv()
+            self.line.start()
             level = self.part(z, BOTH)
-            for peer in z_peers[1:]:
-                remote(level, level, peer, self.by_z)
             remote(level, level, sibling, self.pair)
 
         def l(self):
-            self.by_z.wait(self.part(THREE, BOTH))
+            self.line.wait()
             for step in (1, 2, 3):
                 level = self.part(z_of[step], BOTH)
                 remote(level, level, sibling, self.pair)
@@ -612,27 +753,30 @@
     def column_part(ref, start, size):
         return lambda levels, place: ref.at[levels, place, :, lanes(start, size)]
 
-    def gather(part, way):
-        return Gather(part, way) if way > 0 else FineGather(part, -way) if way else SquareGather(part)
+    def gather(part, way, chained=0):
+        kind = Gather if way > 0 else FineGather
+        line = Line if chained else Direct
+        return kind(part, abs(way), line) if way else SquareGather(part, line)
 
     gathers = {
         "s0": gather(column_part(s.w_small, 128 * core, 128), 2),
-        "o0": gather(column_part(s.w_out, 384 * core, 384), GATHER_WAYS["o"][0]),
+        "o0": gather(column_part(s.w_out, 384 * core, 384), GATHER_WAYS["o"][0], GATHER_LINES["o"][0]),
     }
     for j in range(3):
-        gathers["q" + str(j)] = gather(column_part(s.w_qkv, tile(j, core), 384), GATHER_WAYS["q"][j])
+        gathers["q" + str(j)] = gather(column_part(s.w_qkv, tile(j, core), 384), GATHER_WAYS["q"][j], GATHER_LINES["q"][j])
 
     def fc1_gather(j):
         columns = lanes(768 * core + 384 * j, 384)
         return PlaneGather(
             lambda levels, side: s.w_fc1.at[levels, ALL if side is BOTH else pl.ds(2 * side, 2), :, columns],
+            Line if GATHER_LINES["h"][j] else Direct,
             (s.fc1_other.at[:, 384 * j : 384 * j + 384], s.w_fc1.at[z, here, :, columns]),
         )
 
     def fc2_gather(j, size, way):
         rows = pl.ds(size * j, size)
         part = lambda levels, side: s.w_fc2.at[levels, side, core, rows, :]
-        return PlaneGather(part) if way else AcrossGather(part)
+        return (PlaneGather if way else AcrossGather)(part, Line if GATHER_LINES["f"][j] else Direct)
 
     for j in range(2):
         gathers["h" + str(j)] = fc1_gather(j)
@@ -780,24 +924,24 @@
     across_y = 2 * (1 - y) + core
     valid, valid_across = frame_valid[blk].astype(F32), frame_valid[across_y].astype(F32)
 
-    def mask_cotangent():
-        for frame, factor in enumerate((valid, valid_across)):
-
-            def body(rows, _):
-                there = pl.ds(pl.multiple_of(rows.start + 256 * frame, ROWS), ROWS)
-                s.g_branch2[there, :] = (s.cot_in[there, :].astype(F32) * factor).astype(BF16)
-                return 0
-
-            by_rows(body, 0)
-
-
-    class Scatter:
+    def mask_cotangent(frame):
+        def body(rows, _):
+            there = pl.ds(pl.multiple_of(rows.start + 256 * frame, ROWS), ROWS)
+            masked = s.cot_in[there, :].astype(F32) * (valid_across if frame else valid)
+            s.g_branch2[there, :] = masked.astype(BF16)
+            return 0
+
+        by_rows(body, 0)
+
+
+    class Scatter(Steps):
         every = ALL
 
-        def __init__(self, own, other, pr, dx, dy, px, py, pz, finish, low=2):
+        def __init__(self, own, other, pr, dx, dy, px, py, pz, finish, low=2, line=DirectSum, more=None):
             self.own, self.other, self.finish = own, other, finish
-            self.pr, self.dx, self.dy, self.px, self.py, self.pz = pr, dx, dy, px, py, pz
-            self.square, self.by_z = Group(), Group()
+            self.pr, self.dx, self.dy, self.px, self.py = pr, dx, dy, px, py
+            self.line = line(lambda levels: own(levels, here), pz, more)
+            self.square = Group()
             self.low, self.high = pl.ds(0, low), pl.ds(low, 4 - low)
 
         def s(self):
@@ -846,11 +990,35 @@
                 return 0
 
             lax.fori_loop(0, 4, add, 0)
-            for step in (1, 2, 3):
-                remote(self.own(z_of[step], here), self.pz(step - 1), z_peers[step], self.by_z)
+            self.line.start()
 
         def l(self):
-            self.by_z.wait(self.pz(THREE))
+            self.line.wait()
+            self.finish(self)
+
+        def summed(self, view):
+            return self.line.summed(view)
+
+    class SquareScatter(Scatter):
+        def __init__(self, own, other, pr, bz, pz, finish, line, more):
+            self.own, self.other, self.finish = own, other, finish
+            self.pr, self.pz, self.square = pr, pz, Group()
+            self.line = line(lambda levels: own(levels, ALL), bz, more)
+
+        def z(self):
+            self.add_pair()
+            self.line.start()
+
+        def p(self):
+            self.line.wait()
+            if isinstance(self.line, DirectSum):
+                self.own(z, ALL)[...] = self.line.summed(lambda ref: ref).astype(BF16)
+            targets = ((at_x, x_peer), (at_y, y_peer), (at_d, d_peer))
+            for i, (place, peer) in enumerate(targets):
+                remote(self.own(z, place), self.pz(i), peer, self.square)
+
+        def l(self):
+            self.square.wait(self.pz(THREE))
             self.finish(self)
 
         def summed(self, view):
@@ -859,42 +1027,11 @@
                 found = found + view(self.pz(i))[...].astype(F32)
             return found
 
-    class SquareScatter(Scatter):
-        def __init__(self, own, other, pr, bz, pz, finish):
-            self.own, self.other, self.finish = own, other, finish
-            self.pr, self.bz, self.pz = pr, bz, pz
-            self.square, self.by_z = Group(), Group()
-
-        def z(self):
-            self.add_pair()
-            for step in (1, 2, 3):
-                remote(self.own(z_of[step], ALL), self.bz(step - 1, ALL), z_peers[step], self.by_z)
-
-        def p(self):
-            self.by_z.wait(self.bz(THREE, ALL))
-
-            def add(place, _):
-                ref = self.own(z, place)
-                found = ref[...].astype(F32)
-                for i in range(3):
-                    found = found + self.bz(i, place)[...].astype(F32)
-                ref[...] = found.astype(BF16)
-                return 0
-
-            lax.fori_loop(0, 4, add, 0)
-            targets = ((at_x, x_peer), (at_y, y_peer), (at_d, d_peer))
-            for i, (place, peer) in enumerate(targets):
-                remote(self.own(z, place), self.pz(i), peer, self.square)
-
-        def l(self):
-            self.square.wait(self.pz(THREE))
-            self.finish(self)
-
     class PlaneScatter(Scatter):
-        def __init__(self, own, other, pr, px, pz, finish, across=None):
+        def __init__(self, own, other, pr, px, pz, finish, line, more, across=None):
             self.own, self.other, self.finish, self.across = own, other, finish, across
-            self.pr, self.px, self.pz = pr, px, pz
-            self.by_z = Group()
+            self.pr, self.px = pr, px
+            self.line = line(lambda levels: own(levels, x), pz, more)
 
         def x(self):
             self.add_pair()
@@ -909,11 +1046,10 @@
                 return 0
 
             lax.fori_loop(0, 4, add, 0)
-            for step in (1, 2, 3):
-                remote(self.own(z_of[step], x), self.pz(step - 1), z_peers[step], self.by_z)
+            self.line.start()
 
         def y(self):
-            self.by_z.wait(self.pz(THREE))
+            self.line.wait()
             source, target = self.across(self)
             self.y_copy = remote(source, target, y_peer)
 
@@ -921,33 +1057,23 @@
             if self.across:
                 self.y_copy.wait_recv()
             else:
-                self.by_z.wait(self.pz(THREE))
+                self.line.wait()
             self.finish(self)
 
-        def summed(self, view):
-            found = view(self.own(z, x))[...].astype(F32)
-            for i in range(3):
-                found = found + view(self.pz(i))[...].astype(F32)
-            return found
-
     class AcrossScatter(Scatter):
-        def __init__(self, own, other, pr, bz, px, finish):
+        def __init__(self, own, other, pr, bz, px, finish, line, more):
             self.own, self.other, self.finish = own, other, finish
-            self.pr, self.bz, self.px = pr, bz, px
-            self.by_z = Group()
+            self.pr, self.px = pr, px
+            self.line = line(lambda levels: own(levels, ALL), bz, more)
 
         def z(self):
             self.add_pair()
-            for step in (1, 2, 3):
-                remote(self.own(z_of[step], ALL), self.bz(step - 1), z_peers[step], self.by_z)
+            self.line.start()
 
         def x(self):
-            self.by_z.wait(self.bz(THREE))
-            ref = self.own(z, ALL)
-            found = ref[...].astype(F32)
-            for i in range(3):
-                found = found + self.bz(i)[...].astype(F32)
-            ref[...] = found.astype(BF16)
+            self.line.wait()
+            if isinstance(self.line, DirectSum):
+                self.own(z, ALL)[...] = self.line.summed(lambda ref: ref).astype(BF16)
             self.x_copy = remote(self.own(z, 1 - x), self.px(), x_peer)
 
         def l(self):
@@ -966,7 +1092,7 @@
 
         return own, other
 
-    def column_scatter(ref, columns, size, spot, output, way):
+    def column_scatter(ref, columns, size, spot, output, way, chained):
         at = pl.ds(spot, size)
 
         def finish(scatter):
@@ -977,13 +1103,14 @@
             output[:, target] = s.last_a[own_rows, at]
 
         if not way:
-            extra = pl.ds(spot, size)
             return SquareScatter(
                 *columns_of(ref, columns, size),
                 lambda levels, places: s.pr_a.at[levels, places, :, at],
-                lambda i, places: s.bz_a.at[i, places, :, extra],
+                lambda i: s.bz_a.at[i, :, :, at],
                 lambda i: s.pz_a.at[i, :, at],
                 finish,
+                LineSum if chained else DirectSum,
+                lambda i: s.cz_a.at[i, :, :, at],
             )
         return Scatter(
             *columns_of(ref, columns, size),
@@ -995,6 +1122,8 @@
             lambda i: s.pz_a.at[i, :, at],
             finish,
             way,
+            LineSum if chained else DirectSum,
+            lambda i: s.qz_a.at[i, :, at],
         )
 
     def fc1_scatter(j):
@@ -1027,6 +1156,8 @@
             lambda levels: s.px_fc1.at[levels, :, :, at],
             lambda i: s.pz_fc1.at[i, :, :, at],
             finish,
+            LineSum if SCATTER_LINES["h"][j] else DirectSum,
+            lambda i: s.qz_fc1.at[i, :, :, at],
             across,
         )
 
@@ -1047,7 +1178,9 @@
         pr = lambda levels, side: s.pr_fc2.at[levels, sides(side), :, rows, :]
         if not way:
             bz = lambda i: s.bz_fc2.at[i, :, :, rows, :]
-            return AcrossScatter(own, other, pr, bz, lambda: s.pz_fc2.at[0, :, rows, :], finish)
+            line = LineSum if SCATTER_LINES["f"][j] else DirectSum
+            more = lambda i: s.cz_fc2.at[i, :, :, rows, :]
+            return AcrossScatter(own, other, pr, bz, lambda: s.pz_fc2.at[0, :, rows, :], finish, line, more)
         return PlaneScatter(
             own,
             other,
@@ -1055,6 +1188,8 @@
             lambda levels: s.px_fc2.at[levels, :, rows, :],
             lambda i: s.pz_fc2.at[i, :, rows, :],
             finish,
+            LineSum if SCATTER_LINES["f"][j] else DirectSum,
+            lambda i: s.qz_fc2.at[i, :, rows, :],
         )
 
     def small_finish(scatter):
@@ -1071,10 +1206,10 @@
         scatters["f" + str(j)] = fc2_scatter(j, 96 // len(SCATTER_WAYS["f"]), way)
     for j in range(2):
         scatters["h" + str(j)] = fc1_scatter(j)
-    scatters["o0"] = column_scatter(s.g_out, lambda side: 384 * side, 384, 0, grad_out, SCATTER_WAYS["o"][0])
+    scatters["o0"] = column_scatter(s.g_out, lambda side: 384 * side, 384, 0, grad_out, SCATTER_WAYS["o"][0], SCATTER_LINES["o"][0])
     for j in range(3):
         scatters["q" + str(j)] = column_scatter(
-            s.g_qkv, partial(tile, j), 384, 384 + 384 * j, grad_qkv, SCATTER_WAYS["q"][j]
+            s.g_qkv, partial(tile, j), 384, 384 + 384 * j, grad_qkv, SCATTER_WAYS["q"][j], SCATTER_LINES["q"][j]
         )
     scatters["s0"] = Scatter(
         *columns_of(s.g_small, lambda side: 128 * side, 128),
@@ -1263,15 +1398,13 @@
 
     moved = {"rows": (rows_moved, s.rows_in.at[0:192, :])}
 
-    def send_cotangent():
-        group = Group()
-        after = pl.ds(pl.multiple_of(64 * blk + 256, 64), 64)
+    def send_cotangent(frame):
+        group, there = Group(), pl.ds(pl.multiple_of(64 * blk + 256 * frame, 64), 64)
         for py, pc in blk_peers:
-            for there, frame in ((mine, 2 * py + pc), (after, 2 * (1 - py) + pc)):
-                remote(cotangent.at[frame], s.cot_in.at[there, :], (wide, 2 * py + pc), group)
-        moved["cot"] = group, s.cot_in.at[0:384, :]
-        s.cot_in[mine, :] = cotangent[blk]
-        s.cot_in[after, :] = cotangent[across_y]
+            source = cotangent.at[2 * (1 - py if frame else py) + pc]
+            remote(source, s.cot_in.at[there, :], (wide, 2 * py + pc), group)
+        moved["cot" + str(frame)] = group, s.cot_in.at[256 * frame : 256 * frame + 192, :]
+        s.cot_in[there, :] = cotangent[across_y if frame else blk]
 
     def received(name):
         group, ref = moved.pop(name)
@@ -1281,9 +1414,9 @@
         received("rows")
         first_norm()
 
-    def start_cotangent():
-        received("cot")
-        mask_cotangent()
+    def start_cotangent(frame):
+        received("cot" + str(frame))
+        mask_cotangent(frame)
 
     def send_encoded():
         ours = pl.ds(pl.multiple_of(64 * core, 64), 64)
@@ -1352,156 +1485,178 @@
 
     g, r = types.SimpleNamespace(**gathers), types.SimpleNamespace(**scatters)
     g.s0.z()
+    g.q2.z()
+    g.q1.z()
+    g.q2.o()
     g.q0.z()
-    g.q1.z()
-    g.q2.z()
+    g.o0.z()
+    g.h0.y()
+    g.q0.o()
+    g.f2.x()
+    g.f1.x()
+    g.s0.p()
     g.q1.o()
-    g.f2.x()
-    g.o0.z()
-    g.s0.p()
-    g.q2.o()
-    g.q0.o()
-    g.h0.y()
+    g.o0.o()
+    g.q2.p()
+    g.h0.z()
     g.s0.f()
-    g.o0.o()
+    g.h1.y()
+    g.s0.g()
+    g.q1.p()
+    g.q2.f()
+    g.q2.g()
+    g.h1.z()
     g.q0.p()
-    g.s0.g()
-    g.h1.y()
-    g.h0.z()
-    g.q1.p()
+    g.o0.p()
     g.s0.l()
+    g.q1.f()
+    g.h0.w()
+    g.q2.l()
+    g.s0.d()
+    g.q1.g()
+    unpack_small()
+    g.h1.w()
     g.q0.f()
     g.q0.g()
-    g.h1.z()
-    g.q2.p()
-    g.o0.p()
-    g.q1.f()
-    g.q1.g()
+    g.h0.v()
+    g.o0.f()
+    start_norm()
     g.f0.z()
-    g.q0.l()
-    g.s0.d()
-    unpack_small()
-    g.q2.f()
-    g.q2.g()
-    g.o0.f()
-    g.q0.d()
-    start_norm()
     g.o0.g()
+    send_cotangent(1)
+    g.h1.v()
     g.f1.z()
-    g.h0.x()
-    project_both(0)
     g.q1.l()
-    send_cotangent()
-    g.q2.l()
-    g.q1.d()
-    project_both(1)
-    attend(0)
+    send_cotangent(0)
     g.q2.d()
     project_both(2)
+    g.f2.z()
+    g.q1.d()
+    g.q0.l()
+    g.h0.x()
+    project_both(1)
+    g.f0.w()
+    g.q0.d()
+    project_both(0)
+    attend(0)
     g.o0.l()
-    g.f2.z()
-    g.h1.x()
     attend(1)
     g.o0.d()
+    g.f2.w()
+    g.h1.x()
     project_out()
     send_normed()
+    g.f0.v()
+    g.f1.w()
+    start_cotangent(0)
     g.h0.l()
+    g.f2.v()
+    start_cotangent(1)
+    g.h0.d()
     transpose_out()
-    g.h0.d()
+    g.f1.v()
     g.f0.x()
     feed(0, 0)
-    start_cotangent()
-    g.f1.x()
     g.h1.l()
+    g.f2.l()
     g.h1.d()
     feed(1, 0)
+    g.f1.l()
+    take_normed()
+    feed(0, 1)
+    feed(1, 1)
     g.f0.l()
-    take_normed()
-    feed(1, 1)
-    feed(0, 1)
-    weight_grad_fc2(1)
-    r.f1.s()
-    g.f1.l()
-    g.f2.l()
     weight_grad_fc2(2)
+    g.f2.d()
+    weight_grad_fc2(0)
+    g.f0.d()
+    r.f0.s()
     r.f2.s()
-    r.f1.x()
-    weight_grad_fc2(0)
-    r.f0.s()
-    g.f2.d()
     g.f1.d()
-    g.f0.d()
     feed_back(1)
     feed_back_rows(1)
     send_back()
+    r.f0.z()
     transpose_other()
-    r.f0.z()
     r.f2.x()
     feed_back(0)
+    grad_fc1_weight(0)
+    r.h0.s()
     grad_fc1_weight(1)
+    r.h0.x()
+    feed_out(1)
     r.h1.s()
-    grad_fc1_weight(0)
+    weight_grad_fc2(1)
+    send_part()
+    r.f2.z()
+    r.f1.s()
+    feed_out(0)
     r.h1.x()
-    feed_out(1)
-    feed_out(0)
-    r.h0.s()
-    r.f2.z()
-    send_part()
+    feed_back_rows(0)
     r.f1.z()
-    feed_back_rows(0)
-    r.h0.x()
     send_base()
+    r.f0.w()
     start_second()
+    grad_out_weight()
     project_attended()
-    grad_out_weight()
     r.o0.s()
     attend_back(0)
+    r.h0.z()
+    r.o0.p()
     grad_qkv_weight(0)
     r.q0.s()
+    r.f2.w()
+    r.f1.w()
     r.h1.z()
-    r.o0.p()
     r.q0.p()
     attend_back(1)
+    r.o0.f()
+    r.o0.g()
     grad_qkv_weight(2)
     r.q2.s()
-    r.h0.z()
-    r.o0.f()
-    r.o0.g()
-    grad_qkv_weight(1)
-    r.q2.p()
+    r.h0.w()
     r.q0.f()
     r.q0.g()
+    r.f0.v()
+    grad_qkv_weight(1)
+    r.f2.v()
     r.q1.s()
+    r.q2.p()
     start_output()
-    first_norm_back()
-    r.q2.f()
-    r.q2.g()
+    r.f1.v()
     r.o0.z()
     r.q1.p()
+    r.h1.w()
+    first_norm_back()
+    r.h0.v()
+    pack_small()
+    r.q2.f()
+    r.s0.s()
+    r.q2.g()
     r.q0.z()
-    pack_small()
-    r.s0.s()
+    r.q1.f()
+    r.f2.l()
     r.s0.p()
-    r.q1.f()
+    r.f1.x()
     r.q1.g()
+    send_encoded()
     r.f0.x()
+    r.h0.y()
+    r.h1.v()
     r.q2.z()
+    r.s0.f()
+    send_grad_rows()
+    r.h0.l()
+    r.q1.z()
+    r.s0.g()
     r.h1.y()
+    r.q0.l()
     r.o0.l()
-    r.h0.y()
-    r.q0.l()
-    r.s0.f()
-    r.s0.g()
-    send_grad_rows()
+    r.q2.l()
+    r.s0.z()
+    r.f0.l()
+    r.h1.l()
     r.f1.l()
-    r.f2.l()
-    r.q1.z()
-    r.q2.l()
-    send_encoded()
-    r.h1.l()
-    r.f0.l()
-    r.s0.z()
-    r.h0.l()
     r.q1.l()
     r.s0.l()
     for name in list(moved):
@@ -1509,8 +1664,8 @@
     for copy in finals:
         copy.wait_recv()
     grad_patches[...] = s.gx_recv[...].astype(F32)
-    for copy in started[-SENDS:]:
-        copy.wait_send()
+    for spot in range(max(0, len(started) - SENDS), len(started)):
+        leave(spot)
 
 
 def emit_kernel(*refs):

time: 119 us -> 111 us (0.933)
  Pallas kernels: 118 us -> 110 us
    pallas_call x1, Pallas kernels: 115 us -> 107 us  [fast(): pl.pallas_call(layer_kernel, out_shape=[jax.ShapeDtypeStruct(shape, dtype...]
where the time goes in v5:
time: 111 us; the launch traced here: 110 us
  Pallas kernels  110 us (99%)
    pallas_call x1, Pallas kernels, fast(): pl.pallas_call(layer_kernel, out_shape=[jax.ShapeDtypeStruct(shape, dtype...  107 us
    pallas_call x1, Pallas kernels, emit(): pl.pallas_call(emit_kernel, out_shape=[jax.ShapeDtypeStruct(a.shape, a.dt...  2.64 us

profile of v5, /device:TPU:0, one launch (start us, length us, event | category | flops | bytes accessed | tf_op | source)
XLA Modules:
  0.0 110.4 jit_solution(11477969895254689816)
XLA Ops:
  0.6 106.9 %shard_map.203 = (bf16[4,64,768]{2,1,0:T(8,128)(2,1)}, f32[4,64,768]{2,1,0:T(8,128)}, f32[2,24]{1,0:T(2,128)}, f32[2,24]{1,0:T(2,128)}, f32[24,2304]{1,0:T(8,128...) custom-call(bf16[4,64,768]{2,1,0:T(8,128)(2,1)} %patches.1, ...), custom_call_target="tpu_custom_call" | custom-call | tf_op jit(solution)/shard_map/pallas_call | solution.py:1737
  107.6 2.6 %shard_map.204 = (bf16[4,64,768]{2,1,0:T(8,128)(2,1)}, f32[4,64,768]{2,1,0:T(8,128)}, f32[2,24]{1,0:T(2,128)}, f32[2,24]{1,0:T(2,128)}, f32[24,2304]{1,0:T(8,128...) custom-call(bf16[4,64,768]{2,1,0:T(8,128)(2,1)} %get-tuple-element.3, ...), custom_call_target="tpu_custom_call" | custom-call | tf_op jit(solution)/shard_map/pallas_call | solution.py:1697

commit v6 on v5

--- a/solution.py
+++ b/solution.py
@@ -257,18 +257,33 @@
 TOKENS = 256
 ROWS = 64
 ALL, THREE, BOTH = pl.ds(0, 4), pl.ds(0, 3), pl.ds(0, 2)
-GATHER_WAYS = dict(q=(-1, -2, -2), o=(-1,), f=(1, 0, 0))
-SCATTER_WAYS = dict(f=(0, 0, 1), o=(2,), q=(2, 2, 2))
-GATHER_LINES = dict(q=(0, 0, 0), o=(0,), h=(1, 1), f=(1, 1, 1))
-SCATTER_LINES = dict(q=(0, 0, 0), o=(0,), h=(1, 1), f=(1, 1, 1))
-
-
-TILES = ((0, 1536), (768, 384), (1920, 1152))
-
-
-def tile(j, side):
-    first, second = TILES[j]
-    return first + side * (second - first)
+GATHER_UNITS = (
+    ("q0", 0, 0, 3, -1, 0),
+    ("q1", 1, 0, 3, -2, 0),
+    ("q2", 2, 0, 3, -2, 0),
+    ("o0", 3, 0, 3, -1, 0),
+)
+SCATTER_UNITS = (
+    ("o0", 3, 0, 3, 2, 0),
+    ("q0", 0, 0, 3, 2, 0),
+    ("q1", 1, 0, 3, 2, 0),
+    ("q2", 2, 0, 3, 2, 0),
+)
+GATHER_FC2, SCATTER_FC2 = (1, 0, 0), (0, 0, 1)
+GATHER_LINES = dict(h=(1, 1), f=(1, 1, 1))
+SCATTER_LINES = dict(h=(1, 1), f=(1, 1, 1))
+
+
+PIECES = (((0, 12, 7), (6, 1, 13)), ((2, 14, 9), (8, 3, 15)), ((4, 16, 11), (10, 5, 17)))
+
+
+def piece(j, side, t):
+    first, second = PIECES[j][0][t], PIECES[j][1][t]
+    return 128 * (first + side * (second - first))
+
+
+def pair_places(j, i):
+    return 768 * j + 512 * i, 768 * j + 384 - 128 * i, 768 * j + 128 + 512 * i
 
 
 def dot(left, right):
@@ -283,7 +298,7 @@
     return lax.dot_general(left, right, (((0,), (0,)), ((), ())), preferred_element_type=F32)
 
 
-SENDS, ARRIVALS = 80, 150
+SENDS, ARRIVALS, KEPT = 48, 143, 28
 FC1_OUTPUT = 7
 
 
@@ -299,8 +314,10 @@
         w_fc2=vm(4, 2, 2, 96, 768),
         fc1_other=vm(48, 768),
         own_small=vm(16, 128, dtype=F32),
-        pair_rows=vm(48, 3072, dtype=F32),
-        pair_send=vm(24, 3072, dtype=F32),
+        pair_rows=vm(48, 1536, dtype=F32),
+        pair_send=vm(24, 1536, dtype=F32),
+        pair_rows_h=vm(48, 1536, dtype=F32),
+        pair_send_h=vm(24, 1536, dtype=F32),
         par=vm(16, 768, dtype=F32),
         par_fc1=vm(8, 1536, dtype=F32),
         rows_in=vm(256, 768),
@@ -348,6 +365,8 @@
         dx_a=vm(4, 48, 1536),
         px_small=vm(4, 16, 128),
         px_a=vm(4, 48, 1536),
+        px2_a=vm(4, 2, 48, 1536),
+        send_a=vm(48, 1536),
         px_fc1=vm(4, 2, 48, 768),
         px_fc2=vm(4, 2, 96, 384),
         py_small=vm(4, 16, 128),
@@ -368,6 +387,9 @@
         last_fc1=vm(2, 48, 768, dtype=F32),
         send_fc1=vm(48, 768),
         last_fc2=vm(96, 384, dtype=F32),
+        kept_fc2=vm(96, 384, dtype=F32),
+        gx_out=vm(4, 64, 768, dtype=F32),
+        local_sem=pltpu.SemaphoreType.DMA((KEPT,)),
         send_sem=pltpu.SemaphoreType.DMA((SENDS,)),
         recv_sem=pltpu.SemaphoreType.DMA((ARRIVALS,)),
     )
@@ -462,9 +484,24 @@
             pl.when(only)(copy.start)
         return copy
 
+    kept = []
+
+    class Local:
+        def __init__(self, source, target):
+            self.copy, self.waited = pltpu.make_async_copy(source, target, s.local_sem.at[len(kept)]), False
+            self.copy.start()
+            kept.append(self)
+
+        def wait(self):
+            if not self.waited:
+                self.waited = True
+                self.copy.wait()
+
     def lanes(start, size):
         return pl.ds(pl.multiple_of(start, 128), size)
 
+    mine = pl.ds(pl.multiple_of(64 * blk, 64), 64)
+    taken = [Local(fc2_weight, s.w_fc2.at[z, x, core]), Local(patches.at[blk], s.rows_in.at[mine, :])]
     s.own_small[...] = jnp.zeros((16, 128), F32)
     s.sums[...] = jnp.zeros((16, D), F32)
     s.own_small[0:2, 0:24] = norm_gain[...].astype(F32)
@@ -474,33 +511,31 @@
     s.own_small[8:9, 0:96] = fc1_bias[...].astype(F32)
     s.w_small[z, here, :, lanes(128 * core, 128)] = s.own_small[...].astype(BF16)
     own_rows = pl.ds(pl.multiple_of(24 * core, 8), 24)
-    for ref, start, columns in (
-        (qkv_weight, 0, partial(tile, 0)),
-        (qkv_weight, 384, partial(tile, 1)),
-        (qkv_weight, 768, partial(tile, 2)),
-        (out_weight, 1152, lambda side: 384 * side),
-    ):
-        s.pair_send[:, start : start + 384] = ref[:, lanes(columns(1 - core), 384)].astype(F32)
-        s.pair_rows[own_rows, start : start + 384] = ref[:, lanes(columns(core), 384)].astype(F32)
+    pieces = [(qkv_weight, 384 * j + 128 * t, partial(piece, j, t=t)) for j in range(3) for t in range(3)]
+    pieces += [(out_weight, 1152 + 128 * t, lambda side, t=t: 384 * side + 128 * t) for t in range(3)]
+    for ref, start, columns in pieces:
+        s.pair_send[:, start : start + 128] = ref[:, lanes(columns(1 - core), 128)].astype(F32)
+        s.pair_rows[own_rows, start : start + 128] = ref[:, lanes(columns(core), 128)].astype(F32)
     theirs = fc1_weight[:, lanes((1 - core) * 1536, 1536)].astype(F32)
     ours = fc1_weight[:, lanes(core * 1536, 1536)].astype(F32)
     for side in (0, 1):
         for k in range(4):
-            at, found = 1536 + 768 * side + 192 * k, 384 * k + 192 * side
-            s.pair_send[:, at : at + 192] = theirs[:, found : found + 192]
-            s.pair_rows[own_rows, at : at + 192] = ours[:, found : found + 192]
-    s.w_fc2[z, x, core] = fc2_weight[...]
+            at, found = 768 * side + 192 * k, 384 * k + 192 * side
+            s.pair_send_h[:, at : at + 192] = theirs[:, found : found + 192]
+            s.pair_rows_h[own_rows, at : at + 192] = ours[:, found : found + 192]
 
     pl.semaphore_wait(barrier, len(peers))
 
-    pair = remote(s.pair_send, s.pair_rows.at[own_rows, :], sibling)
-
-    mine = pl.ds(pl.multiple_of(64 * blk, 64), 64)
+    pairs = {}
+    for name, start in (("q0", 0), ("q1", 384), ("q2", 768), ("o", 1152)):
+        columns = slice(start, start + 384)
+        pairs[name] = remote(s.pair_send.at[:, columns], s.pair_rows.at[own_rows, columns], sibling)
+    pairs["h"] = remote(s.pair_send_h, s.pair_rows_h.at[own_rows, :], sibling)
+
 
     rows_moved = Group()
     for py, pc in blk_peers:
         remote(patches.at[2 * py + pc], s.rows_in.at[mine, :], (wide, 2 * py + pc), rows_moved)
-    s.rows_in[mine, :] = patches[blk]
 
     class Direct:
         def __init__(self, block):
@@ -613,6 +648,9 @@
         def summed(self, view):
             return view(self.own(z))[...].astype(F32)
 
+    def wait_fc2():
+        taken[0].wait()
+
     class Steps:
         def w(self):
             self.line.pass_on()
@@ -710,6 +748,8 @@
         def z(self):
             if self.across:
                 self.y_copy.wait_recv()
+            else:
+                wait_fc2()
             self.line.start()
 
         def x(self):
@@ -732,6 +772,7 @@
             self.line = line(lambda levels: part(levels, BOTH))
 
         def x(self):
+            wait_fc2()
             own = self.part(z, x)
             self.x_copy = remote(own, own, x_peer)
 
@@ -753,17 +794,23 @@
     def column_part(ref, start, size):
         return lambda levels, place: ref.at[levels, place, :, lanes(start, size)]
 
-    def gather(part, way, chained=0):
-        kind = Gather if way > 0 else FineGather
-        line = Line if chained else Direct
-        return kind(part, abs(way), line) if way else SquareGather(part, line)
-
-    gathers = {
-        "s0": gather(column_part(s.w_small, 128 * core, 128), 2),
-        "o0": gather(column_part(s.w_out, 384 * core, 384), GATHER_WAYS["o"][0], GATHER_LINES["o"][0]),
-    }
-    for j in range(3):
-        gathers["q" + str(j)] = gather(column_part(s.w_qkv, tile(j, core), 384), GATHER_WAYS["q"][j], GATHER_LINES["q"][j])
+    def column_gather(ref, start, size, way, chained):
+        part, line = column_part(ref, start, size), Line if chained else Direct
+        if way == 9:
+            own = part(z, here)
+            sides = lambda levels, side: part(levels, ALL if side is BOTH else pl.ds(2 * side, 2))
+            return PlaneGather(sides, line, (own, own))
+        if way == 0:
+            return SquareGather(part, line)
+        return (Gather if way > 0 else FineGather)(part, abs(way), line)
+
+    gathers = {"s0": column_gather(s.w_small, 128 * core, 128, 2, 0)}
+    for name, j, start, size, way, chained in GATHER_UNITS:
+        if j < 3:
+            ref, first = s.w_qkv, 768 * j + 384 * core
+        else:
+            ref, first = s.w_out, 384 * core
+        gathers[name] = column_gather(ref, first + 128 * start, 128 * size, way, chained)
 
     def fc1_gather(j):
         columns = lanes(768 * core + 384 * j, 384)
@@ -780,16 +827,21 @@
 
     for j in range(2):
         gathers["h" + str(j)] = fc1_gather(j)
-    for j, way in enumerate(GATHER_WAYS["f"]):
-        gathers["f" + str(j)] = fc2_gather(j, 96 // len(GATHER_WAYS["f"]), way)
-
-    pair.wait_recv()
-    for j in range(3):
-        s.w_qkv[z, here, :, lanes(tile(j, core), 384)] = s.pair_rows[:, 384 * j : 384 * j + 384].astype(BF16)
-    s.w_out[z, here, :, lanes(384 * core, 384)] = s.pair_rows[:, 1152:1536].astype(BF16)
-    halves = lanes(1536 + 768 * y, 768), lanes(1536 + 768 * (1 - y), 768)
-    s.w_fc1[z, here, :, lanes(768 * core, 768)] = s.pair_rows[:, halves[0]].astype(BF16)
-    s.fc1_other[...] = s.pair_rows[:, halves[1]].astype(BF16)
+    for j, way in enumerate(GATHER_FC2):
+        gathers["f" + str(j)] = fc2_gather(j, 96 // len(GATHER_FC2), way)
+
+    def assemble(name):
+        pairs[name].wait_recv()
+        if name == "h":
+            halves = lanes(768 * y, 768), lanes(768 * (1 - y), 768)
+            s.w_fc1[z, here, :, lanes(768 * core, 768)] = s.pair_rows_h[:, halves[0]].astype(BF16)
+            s.fc1_other[...] = s.pair_rows_h[:, halves[1]].astype(BF16)
+        elif name == "o":
+            s.w_out[z, here, :, lanes(384 * core, 384)] = s.pair_rows[:, 1152:1536].astype(BF16)
+        else:
+            j = int(name[1])
+            found = s.pair_rows[:, 384 * j : 384 * j + 384].astype(BF16)
+            s.w_qkv[z, here, :, lanes(768 * j + 384 * core, 384)] = found
 
 
     def by_rows(body, carry=None):
@@ -853,13 +905,18 @@
         by_rows(body, 0)
         s.normed_t[...] = s.normed[...].T
 
-    def project_qkv(start):
-        found = dot(s.normed[...], s.w_qkv[:, :, :, start : start + 384].reshape(D, 384))
-        if start < D:
-            found = (found + s.par[4:5, start : start + 384]) * 0.125
-        if start >= 2 * D:
-            found = found + s.par[5:6, start - 2 * D : start - 2 * D + 384]
-        s.mixed[:, start : start + 384] = found.astype(BF16)
+    def project_qkv(j):
+        found = dot(s.normed[...], s.w_qkv[:, :, :, 768 * j : 768 * j + 768].reshape(D, D))
+        for i in (0, 1):
+            query, key, value = (slice(at, at + 128) for at in pair_places(0, i))
+            natural = slice(128 * (2 * j + i), 128 * (2 * j + i) + 128)
+            parts = (
+                (query, (found[:, query] + s.par[4:5, natural]) * 0.125),
+                (key, found[:, key]),
+                (value, found[:, value] + s.par[5:6, natural]),
+            )
+            for at, part in parts:
+                s.mixed[:, 768 * j + at.start : 768 * j + at.stop] = part.astype(BF16)
 
     def head_masks():
         first = (over((TOKENS, 128), 1) < 64).astype(F32)
@@ -869,20 +926,27 @@
         expo = jnp.exp(scores - jnp.max(scores, axis=-1, keepdims=True))
         return expo * (1.0 / jnp.sum(expo, axis=-1, keepdims=True))
 
-    def attend(part):
-        def body(two, _):
-            query, key, value = (s.mixed[:, lanes(128 * two + part, 128)] for part in (0, D, 2 * D))
+    def attend(j):
+        def body(i, _):
+            query, key, value = (s.mixed[:, lanes(at, 128)] for at in pair_places(j, i))
             found = jnp.zeros((TOKENS, 128), F32)
             for mask in head_masks():
                 probs = softmax(dot_nt(query * mask, key)).astype(BF16)
                 found = found + dot(probs, value * mask)
-            s.attended[:, lanes(128 * two, 128)] = found.astype(BF16)
+            s.attended[:, lanes(128 * (2 * j + i), 128)] = found.astype(BF16)
             return 0
 
-        lax.fori_loop(3 * part, 3 * part + 3, body, 0)
-
-    def project_out():
-        s.middle[...] = dot(s.attended[...], s.w_out[...].reshape(D, D))
+        lax.fori_loop(0, 2, body, 0)
+
+    def some_rows(body, carry, start, count):
+        def step(i, held):
+            return body(pl.ds(pl.multiple_of(ROWS * i + start, ROWS), ROWS), held)
+
+        return lax.fori_loop(0, count // ROWS, step, carry)
+
+    def project_out(part):
+        half = pl.ds(128 * part, 128)
+        s.middle[half, :] = dot(s.attended[half, :], s.w_out[...].reshape(D, D))
 
         def body(rows, _):
             middle = s.rows_in[rows, :].astype(F32) + (s.middle[rows, :] + s.par[6:7, :])
@@ -891,33 +955,39 @@
             s.normed2[rows, :] = (found * s.par[1:2, :] + s.par[3:4, :]).astype(BF16)
             return 0
 
-        by_rows(body, 0)
+        some_rows(body, 0, 128 * part, 128)
 
     def transpose_out():
         s.attended_t[...] = s.attended[...].T
         s.normed2_t[:, 0:256] = s.normed2[0:256, :].T
 
-    def feed(j, frame):
+    def feed(j, start, count):
         def body(side, _):
             columns = lanes(768 * side + 384 * j, 384)
-            tokens = pl.ds(256 * frame, 256)
-            s.other[:, 0:384] = dot(s.normed2[tokens, :], s.w_fc1[:, :, :, columns].reshape(D, 384))
+            tokens = pl.ds(start, count)
+            s.other[0:count, 0:384] = dot(s.normed2[tokens, :], s.w_fc1[:, :, :, columns].reshape(D, 384))
 
             def gelu(rows, _):
-                there = pl.ds(pl.multiple_of(rows.start + 256 * frame, ROWS), ROWS)
+                there = pl.ds(pl.multiple_of(rows.start + start, ROWS), ROWS)
                 hidden = s.other[rows, 0:384] + s.par_fc1[0:1, columns]
+                bell = jnp.exp(-0.5 * hidden * hidden)
                 normal = 0.5 + 0.5 * lax.erf(hidden * (1.0 / math.sqrt(2.0)))
-                bell = jnp.exp(-0.5 * hidden * hidden) * (1.0 / math.sqrt(2.0 * math.pi))
-                s.slope[there, columns] = normal + hidden * bell
+                s.slope[there, columns] = normal + hidden * (bell * (1.0 / math.sqrt(2.0 * math.pi)))
                 s.active[there, columns] = (hidden * normal).astype(BF16)
                 return 0
 
-            by_rows(gelu, 0)
-            found = s.active[tokens, columns].T.reshape(4, 96, 256)
-            s.active_t[pl.ds(8 * side + 4 * j, 4), :, 256 * frame : 256 * frame + 256] = found
+            some_rows(gelu, 0, 0, count)
+            found = s.active[tokens, columns].T.reshape(4, 96, count)
+            s.active_t[pl.ds(8 * side + 4 * j, 4), :, start : start + count] = found
             return 0
 
         lax.fori_loop(0, 2, body, 0)
+
+    def feed_own(j):
+        feed(j, 0, 256)
+
+    def feed_other(j, part):
+        feed(j, 256 + 128 * part, 128)
 
     ours_rows = pl.ds(pl.multiple_of(128 * y, 128), 128)
     theirs_rows = pl.ds(pl.multiple_of(128 * (1 - y), 128), 128)
@@ -936,6 +1006,9 @@
 
     class Scatter(Steps):
         every = ALL
+
+        def view(self, ref):
+            return ref
 
         def __init__(self, own, other, pr, dx, dy, px, py, pz, finish, low=2, line=DirectSum, more=None):
             self.own, self.other, self.finish = own, other, finish
@@ -1028,8 +1101,8 @@
             return found
 
     class PlaneScatter(Scatter):
-        def __init__(self, own, other, pr, px, pz, finish, line, more, across=None):
-            self.own, self.other, self.finish, self.across = own, other, finish, across
+        def __init__(self, own, other, pr, px, pz, finish, line, more, across=None, view=None):
+            self.own, self.other, self.finish, self.across, self.view = own, other, finish, across, view
             self.pr, self.px = pr, px
             self.line = line(lambda levels: own(levels, x), pz, more)
 
@@ -1092,15 +1165,45 @@
 
         return own, other
 
-    def column_scatter(ref, columns, size, spot, output, way, chained):
+    def column_scatter(ref, columns, natural, size, spot, output, way, chained):
         at = pl.ds(spot, size)
 
         def finish(scatter):
-            s.last_a[:, at] = scatter.summed(lambda ref: ref)
-            target = lanes(columns(core), size)
+            total = scatter.summed(scatter.view)
+            if way == 9:
+                total = total + s.py_a[0, :, at].astype(F32)
+            s.last_a[:, at] = total
             other_rows = pl.ds(pl.multiple_of(24 * (1 - core), 8), 24)
-            finals.append(remote(s.last_a.at[other_rows, at], output.at[:, target], sibling))
-            output[:, target] = s.last_a[own_rows, at]
+            group = Group()
+            finals.append((group, s.last_a.at[own_rows, at]))
+            for t in range(size // 128):
+                some = slice(spot + 128 * t, spot + 128 * t + 128)
+                target = lanes(natural(core, t), 128)
+                remote(s.last_a.at[other_rows, some], output.at[:, target], sibling, group)
+                Local(s.last_a.at[own_rows, some], output.at[:, target])
+
+        if way == 9:
+
+            def across(scatter):
+                s.send_a[:, at] = scatter.summed(lambda ref: ref.at[1 - y]).astype(BF16)
+                return s.send_a.at[:, at], s.py_a.at[0, :, at]
+
+            def sides(ref):
+                return lambda levels, side: ref(levels, ALL if side is ALL else pl.ds(2 * side, 2))
+
+            own, other = columns_of(ref, columns, size)
+            return PlaneScatter(
+                sides(own),
+                other,
+                lambda levels, places: s.pr_a.at[levels, places, :, at],
+                lambda levels: s.px2_a.at[levels, :, :, at],
+                lambda i: s.bz_a.at[i, BOTH, :, at],
+                finish,
+                LineSum if chained else DirectSum,
+                lambda i: s.cz_a.at[i, BOTH, :, at],
+                across,
+                lambda ref: ref.at[y],
+            )
 
         if not way:
             return SquareScatter(
@@ -1146,8 +1249,9 @@
             other_rows = pl.ds(pl.multiple_of(24 * (1 - core), 8), 24)
             for i, half in enumerate((y, 1 - y)):
                 target = lanes(1536 * half + 768 * core + 384 * j, 384)
-                finals.append(remote(s.last_fc1.at[i, other_rows, at], grad_fc1.at[:, target], sibling))
-                grad_fc1[:, target] = s.last_fc1[i, own_rows, at]
+                copy = remote(s.last_fc1.at[i, other_rows, at], grad_fc1.at[:, target], sibling)
+                finals.append((copy, None))
+                Local(s.last_fc1.at[i, own_rows, at], grad_fc1.at[:, target])
 
         return PlaneScatter(
             own,
@@ -1167,8 +1271,9 @@
 
         def finish(scatter):
             s.last_fc2[rows, :] = scatter.summed(lambda ref: ref.at[1 - core])
-            finals.append(remote(s.last_fc2.at[rows, :], grad_fc2.at[rows, half], sibling))
-            grad_fc2[rows, half] = scatter.summed(lambda ref: ref.at[core])
+            finals.append((remote(s.last_fc2.at[rows, :], grad_fc2.at[rows, half], sibling), None))
+            s.kept_fc2[rows, :] = scatter.summed(lambda ref: ref.at[core])
+            Local(s.kept_fc2.at[rows, :], grad_fc2.at[rows, half])
 
         def sides(side):
             return BOTH if side is ALL else side
@@ -1202,15 +1307,22 @@
 
     finals = []
     scatters = {}
-    for j, way in enumerate(SCATTER_WAYS["f"]):
-        scatters["f" + str(j)] = fc2_scatter(j, 96 // len(SCATTER_WAYS["f"]), way)
+    for j, way in enumerate(SCATTER_FC2):
+        scatters["f" + str(j)] = fc2_scatter(j, 96 // len(SCATTER_FC2), way)
     for j in range(2):
         scatters["h" + str(j)] = fc1_scatter(j)
-    scatters["o0"] = column_scatter(s.g_out, lambda side: 384 * side, 384, 0, grad_out, SCATTER_WAYS["o"][0], SCATTER_LINES["o"][0])
-    for j in range(3):
-        scatters["q" + str(j)] = column_scatter(
-            s.g_qkv, partial(tile, j), 384, 384 + 384 * j, grad_qkv, SCATTER_WAYS["q"][j], SCATTER_LINES["q"][j]
+    for name, j, start, size, way, chained in SCATTER_UNITS:
+        if j < 3:
+            ref, output, spot, first = s.g_qkv, grad_qkv, 384 + 384 * j, 768 * j
+            natural = lambda side, t, j=j, start=start: piece(j, side, start + t)
+        else:
+            ref, output, spot, first = s.g_out, grad_out, 0, 0
+            natural = lambda side, t, start=start: 384 * side + 128 * (start + t)
+        columns = lambda side, first=first, start=start: first + 384 * side + 128 * start
+        scatters[name] = column_scatter(
+            ref, columns, natural, 128 * size, spot + 128 * start, output, way, chained
         )
+
     scatters["s0"] = Scatter(
         *columns_of(s.g_small, lambda side: 128 * side, 128),
         lambda levels, places: s.pr_small.at[levels, places],
@@ -1223,7 +1335,7 @@
     )
 
     def weight_grad_fc2(j):
-        size = 96 // len(SCATTER_WAYS["f"])
+        size = 96 // len(SCATTER_FC2)
         rows = pl.ds(size * j, size)
 
         def body(turn, _):
@@ -1291,18 +1403,19 @@
 
         s.sums[7:8, :] = by_rows(body, jnp.zeros((1, D), F32))
 
-    def feed_back_rows(frame):
-        tokens = pl.ds(256 * frame, 256)
-        s.other[...] = jnp.zeros((TOKENS, D), F32)
-
-        def body(part, _):
-            columns = lanes(D * part, D)
-            s.other[...] += dot_nt(s.g_hidden[tokens, columns], s.w_fc1[:, :, :, columns].reshape(D, D))
-            return 0
-
-        lax.fori_loop(0, 2, body, 0)
-        if frame:
-            s.back_send[...] = s.other[...].astype(BF16)
+    def feed_back_rows(start, count):
+        found = jnp.zeros((count, D), F32)
+        for part in (0, 1):
+            columns = slice(D * part, D * part + D)
+            hidden = s.g_hidden[pl.ds(start, count), columns]
+            found = found + dot_nt(hidden, s.w_fc1[:, :, :, columns].reshape(D, D))
+        return found
+
+    def feed_back_own():
+        s.other[...] = feed_back_rows(0, 256)
+
+    def feed_back_other():
+        s.back_send[...] = feed_back_rows(256, 256).astype(BF16)
 
     def norm_back(upstream, found, scale, gain):
         weighted = upstream * gain
@@ -1315,7 +1428,7 @@
     def column_sum(values):
         return jnp.sum(values, axis=0, keepdims=True)
 
-    def second_norm_back():
+    def second_norm_back(part):
         def rows_back(rows, sums):
             upstream = s.other[rows, :] + s.back_recv[rows, :].astype(F32)
             found, scale = standardized(s.middle[rows, :])
@@ -1329,14 +1442,18 @@
                 sums[2] + column_sum(branch.astype(F32)),
             )
 
-        empty = jnp.zeros((1, D), F32)
-        s.sums[1:2, :], s.sums[3:4, :], s.sums[6:7, :] = by_rows(rows_back, (empty, empty, empty))
-
-    def attend_back(part):
-        def body(two, _):
-            spots = [lanes(128 * two + part, 128) for part in (0, D, 2 * D)]
+        before = [jnp.zeros((1, D), F32)] * 3
+        if part:
+            before = [s.sums[row : row + 1, :] for row in (1, 3, 6)]
+        found = some_rows(rows_back, tuple(before), 128 * part, 128)
+        s.sums[1:2, :], s.sums[3:4, :], s.sums[6:7, :] = found
+
+    def attend_back(j):
+        def body(i, _):
+            spots = [lanes(at, 128) for at in pair_places(j, i)]
+            natural = lanes(128 * (2 * j + i), 128)
             query, key, value = (s.mixed[:, spot] for spot in spots)
-            upstream = s.g_attended[:, spots[0]]
+            upstream = s.g_attended[:, natural]
             g_query, g_key, g_value = (jnp.zeros((TOKENS, 128), F32) for _ in range(3))
             for mask in head_masks():
                 probs = softmax(dot_nt(query * mask, key))
@@ -1351,11 +1468,11 @@
             s.g_mixed[:, spots[0]] = g_query.astype(BF16)
             s.g_mixed[:, spots[1]] = g_key.astype(BF16)
             s.g_mixed[:, spots[2]] = g_value
-            s.sums[4:5, spots[0]] = column_sum(g_query)
-            s.sums[5:6, spots[0]] = column_sum(g_value.astype(F32))
+            s.sums[4:5, natural] = column_sum(g_query)
+            s.sums[5:6, natural] = column_sum(g_value.astype(F32))
             return 0
 
-        lax.fori_loop(3 * part, 3 * part + 3, body, 0)
+        lax.fori_loop(0, 2, body, 0)
 
     def first_norm_back():
         s.total[...] = jnp.zeros((TOKENS, D), F32)
@@ -1398,13 +1515,15 @@
 
     moved = {"rows": (rows_moved, s.rows_in.at[0:192, :])}
 
+    cot_kept = {}
+
     def send_cotangent(frame):
         group, there = Group(), pl.ds(pl.multiple_of(64 * blk + 256 * frame, 64), 64)
         for py, pc in blk_peers:
             source = cotangent.at[2 * (1 - py if frame else py) + pc]
             remote(source, s.cot_in.at[there, :], (wide, 2 * py + pc), group)
         moved["cot" + str(frame)] = group, s.cot_in.at[256 * frame : 256 * frame + 192, :]
-        s.cot_in[there, :] = cotangent[across_y if frame else blk]
+        cot_kept[frame] = Local(cotangent.at[across_y if frame else blk], s.cot_in.at[there, :])
 
     def received(name):
         group, ref = moved.pop(name)
@@ -1412,10 +1531,12 @@
 
     def start_norm():
         received("rows")
+        taken[1].wait()
         first_norm()
 
     def start_cotangent(frame):
         received("cot" + str(frame))
+        cot_kept[frame].wait()
         mask_cotangent(frame)
 
     def send_encoded():
@@ -1424,9 +1545,9 @@
         group = Group()
         for i, frame in enumerate((blk, across_y)):
             remote(s.enc_send.at[i, theirs, :], encoded.at[frame], sibling, group)
-        moved["enc"] = group, encoded.at[BOTH]
-        encoded[blk] = s.enc_send[0, ours, :]
-        encoded[across_y] = s.enc_send[1, ours, :]
+        moved["enc"] = group, s.enc_send.at[0, :, :]
+        Local(s.enc_send.at[0, ours, :], encoded.at[blk])
+        Local(s.enc_send.at[1, ours, :], encoded.at[across_y])
 
     def send_grad_rows():
         group = Group()
@@ -1439,19 +1560,17 @@
     def project_attended():
         s.g_attended[...] = dot_nt(s.g_branch[...], s.w_out[...].reshape(D, D)).astype(BF16)
 
-    def project_both(j):
-        project_qkv(tile(j, 0))
-        project_qkv(tile(j, 1))
-
     def across(name, source, target):
         moved[name] = Group(), target
         remote(source, target, y_peer, moved[name][0])
 
-    def send_normed():
-        across("normed", s.normed2.at[0:256, :], s.normed2.at[256:512, :])
-
-    def take_normed():
-        received("normed")
+    def send_normed(part):
+        start = 128 * part
+        own, other = (s.normed2.at[at : at + 128, :] for at in (start, 256 + start))
+        across("normed" + str(part), own, other)
+
+    def take_normed(part):
+        received("normed" + str(part))
 
     def transpose_other():
         s.normed2_t[:, 256:512] = s.normed2[256:512, :].T
@@ -1467,12 +1586,13 @@
         received("base")
         output()
 
-    def send_back():
-        across("back", s.back_send, s.back_recv)
-
-    def start_second():
-        received("back")
-        second_norm_back()
+    def send_back(part):
+        rows = slice(128 * part, 128 * part + 128)
+        across("back" + str(part), s.back_send.at[rows, :], s.back_recv.at[rows, :])
+
+    def start_second(part):
+        received("back" + str(part))
+        second_norm_back(part)
 
     def grad_fc1_weight(j):
         column_grad(s.normed2_t, s.g_hidden, s.g_fc1, lambda side: 768 * side + 384 * j)
@@ -1481,189 +1601,210 @@
         column_grad(s.attended_t, s.g_branch, s.g_out, lambda side: 384 * side)
 
     def grad_qkv_weight(j):
-        column_grad(s.normed_t, s.g_mixed, s.g_qkv, partial(tile, j))
+        column_grad(s.normed_t, s.g_mixed, s.g_qkv, lambda side: 768 * j + 384 * side)
 
     g, r = types.SimpleNamespace(**gathers), types.SimpleNamespace(**scatters)
     g.s0.z()
+    assemble("q0")
+    g.q0.z()
+    assemble("q1")
+    g.f1.x()
+    assemble("h")
+    g.q0.o()
+    assemble("q2")
+    g.q1.z()
     g.q2.z()
-    g.q1.z()
+    g.s0.p()
+    g.f2.x()
+    assemble("o")
     g.q2.o()
-    g.q0.z()
+    g.q1.o()
+    g.q0.p()
+    g.h0.y()
+    g.h1.y()
     g.o0.z()
-    g.h0.y()
-    g.q0.o()
-    g.f2.x()
-    g.f1.x()
-    g.s0.p()
-    g.q1.o()
     g.o0.o()
+    g.q1.p()
+    g.q0.f()
+    g.q0.g()
+    g.s0.f()
+    g.h0.z()
     g.q2.p()
-    g.h0.z()
-    g.s0.f()
-    g.h1.y()
+    g.h1.z()
     g.s0.g()
-    g.q1.p()
-    g.q2.f()
-    g.q2.g()
-    g.h1.z()
-    g.q0.p()
     g.o0.p()
-    g.s0.l()
     g.q1.f()
     g.h0.w()
-    g.q2.l()
+    g.q1.g()
+    g.q0.l()
+    g.h1.w()
+    g.q2.f()
+    g.h0.v()
+    g.q2.g()
+    g.s0.l()
+    g.q0.d()
+    g.f2.z()
     g.s0.d()
-    g.q1.g()
-    unpack_small()
-    g.h1.w()
-    g.q0.f()
-    g.q0.g()
-    g.h0.v()
     g.o0.f()
-    start_norm()
     g.f0.z()
+    g.h1.v()
     g.o0.g()
     send_cotangent(1)
-    g.h1.v()
+    send_cotangent(0)
+    unpack_small()
     g.f1.z()
+    g.h0.x()
+    start_norm()
+    g.q2.l()
+    project_qkv(0)
+    g.f2.w()
     g.q1.l()
-    send_cotangent(0)
+    attend(0)
+    g.q1.d()
+    project_qkv(1)
+    g.o0.l()
+    g.f0.w()
     g.q2.d()
-    project_both(2)
-    g.f2.z()
-    g.q1.d()
-    g.q0.l()
-    g.h0.x()
-    project_both(1)
-    g.f0.w()
-    g.q0.d()
-    project_both(0)
-    attend(0)
-    g.o0.l()
+    project_qkv(2)
+    g.h1.x()
     attend(1)
+    attend(2)
+    g.f0.v()
     g.o0.d()
-    g.f2.w()
-    g.h1.x()
-    project_out()
-    send_normed()
-    g.f0.v()
     g.f1.w()
+    project_out(0)
+    send_normed(0)
+    project_out(1)
     start_cotangent(0)
+    g.f2.v()
+    g.f0.x()
     g.h0.l()
-    g.f2.v()
+    transpose_out()
+    g.f1.v()
+    send_normed(1)
     start_cotangent(1)
     g.h0.d()
-    transpose_out()
-    g.f1.v()
-    g.f0.x()
-    feed(0, 0)
+    feed_own(0)
     g.h1.l()
+    take_normed(0)
     g.f2.l()
+    feed_other(0, 0)
     g.h1.d()
-    feed(1, 0)
+    feed_own(1)
+    feed_other(1, 0)
     g.f1.l()
-    take_normed()
-    feed(0, 1)
-    feed(1, 1)
+    take_normed(1)
+    feed_other(1, 1)
+    feed_other(0, 1)
     g.f0.l()
+    weight_grad_fc2(0)
+    r.f0.s()
     weight_grad_fc2(2)
+    r.f2.s()
     g.f2.d()
-    weight_grad_fc2(0)
+    g.f1.d()
     g.f0.d()
-    r.f0.s()
-    r.f2.s()
-    g.f1.d()
     feed_back(1)
-    feed_back_rows(1)
-    send_back()
     r.f0.z()
+    feed_back_other()
     transpose_other()
+    send_back(0)
     r.f2.x()
     feed_back(0)
-    grad_fc1_weight(0)
-    r.h0.s()
     grad_fc1_weight(1)
-    r.h0.x()
-    feed_out(1)
     r.h1.s()
     weight_grad_fc2(1)
+    r.f1.s()
+    send_back(1)
+    feed_back_own()
+    r.h1.x()
+    r.f1.z()
+    feed_out(1)
+    grad_fc1_weight(0)
+    r.f2.z()
     send_part()
-    r.f2.z()
-    r.f1.s()
+    r.h0.s()
+    start_second(0)
     feed_out(0)
-    r.h1.x()
-    feed_back_rows(0)
-    r.f1.z()
+    r.h0.x()
+    start_second(1)
+    r.f0.w()
     send_base()
-    r.f0.w()
-    start_second()
     grad_out_weight()
     project_attended()
     r.o0.s()
     attend_back(0)
-    r.h0.z()
+    r.h1.z()
+    r.f1.w()
     r.o0.p()
     grad_qkv_weight(0)
     r.q0.s()
+    attend_back(1)
+    grad_qkv_weight(1)
+    r.h0.z()
     r.f2.w()
-    r.f1.w()
-    r.h1.z()
+    r.q1.s()
     r.q0.p()
-    attend_back(1)
+    attend_back(2)
+    r.h1.w()
+    r.f1.v()
     r.o0.f()
     r.o0.g()
-    grad_qkv_weight(2)
-    r.q2.s()
+    start_output()
+    r.q1.p()
+    first_norm_back()
+    r.f2.v()
     r.h0.w()
     r.q0.f()
     r.q0.g()
     r.f0.v()
-    grad_qkv_weight(1)
-    r.f2.v()
-    r.q1.s()
+    r.o0.z()
+    r.h1.v()
+    grad_qkv_weight(2)
+    r.q1.f()
+    r.q2.s()
+    r.q1.g()
+    pack_small()
+    r.s0.s()
     r.q2.p()
-    start_output()
-    r.f1.v()
-    r.o0.z()
-    r.q1.p()
-    r.h1.w()
-    first_norm_back()
+    r.s0.p()
     r.h0.v()
-    pack_small()
+    r.q0.z()
+    r.q1.z()
     r.q2.f()
-    r.s0.s()
     r.q2.g()
-    r.q0.z()
-    r.q1.f()
+    r.h1.y()
+    r.f1.x()
+    r.s0.f()
     r.f2.l()
-    r.s0.p()
-    r.f1.x()
-    r.q1.g()
-    send_encoded()
+    r.s0.g()
     r.f0.x()
     r.h0.y()
-    r.h1.v()
+    send_grad_rows()
     r.q2.z()
-    r.s0.f()
-    send_grad_rows()
+    send_encoded()
+    r.s0.z()
+    r.q0.l()
+    r.f0.l()
     r.h0.l()
-    r.q1.z()
-    r.s0.g()
-    r.h1.y()
-    r.q0.l()
+    r.f1.l()
     r.o0.l()
+    r.q1.l()
+    r.h1.l()
     r.q2.l()
-    r.s0.z()
-    r.f0.l()
-    r.h1.l()
-    r.f1.l()
-    r.q1.l()
     r.s0.l()
+    received("grad")
+    s.gx_out[...] = s.gx_recv[...].astype(F32)
+    Local(s.gx_out, grad_patches)
     for name in list(moved):
         received(name)
-    for copy in finals:
-        copy.wait_recv()
-    grad_patches[...] = s.gx_recv[...].astype(F32)
+    for arrived, ref in finals:
+        if ref is None:
+            arrived.wait_recv()
+        else:
+            arrived.wait(ref)
+    for copy in kept:
+        copy.wait()
     for spot in range(max(0, len(started) - SENDS), len(started)):
         leave(spot)
 
@@ -1733,12 +1874,12 @@
         ((96, D), F32),
         ((2, 24), F32),
     ]
-    vmem = pl.BlockSpec(memory_space=pltpu.VMEM)
+    vmem, anywhere = pl.BlockSpec(memory_space=pltpu.VMEM), pl.BlockSpec(memory_space=pl.ANY)
     found = list(pl.pallas_call(
         layer_kernel,
         out_shape=[jax.ShapeDtypeStruct(shape, dtype) for shape, dtype in outputs],
-        in_specs=[vmem] * 11 + [pl.BlockSpec(memory_space=pltpu.SMEM)],
-        out_specs=[vmem] * len(outputs),
+        in_specs=[anywhere if i in (0, 8, 10) else vmem for i in range(11)] + [pl.BlockSpec(memory_space=pltpu.SMEM)],
+        out_specs=[anywhere if shape[0] > 2 else vmem for shape, _ in outputs],
         scratch_shapes=list(scratch_shapes().values()),
         compiler_params=pltpu.CompilerParams(
             collective_id=0, has_side_effects=True, vmem_limit_bytes=63 * 2**20

time: 111 us -> 108 us (0.973)
  Pallas kernels: 110 us -> 107 us
    pallas_call x1, Pallas kernels: 107 us -> 105 us  [fast(): pl.pallas_call(layer_kernel, out_shape=[jax.ShapeDtypeStruct(shape, dtype...]
where the time goes in v6:
time: 108 us
  Pallas kernels  107 us (99%)
    pallas_call x1, Pallas kernels, fast(): pl.pallas_call(layer_kernel, out_shape=[jax.ShapeDtypeStruct(shape, dtype...  105 us
    pallas_call x1, Pallas kernels, emit(): pl.pallas_call(emit_kernel, out_shape=[jax.ShapeDtypeStruct(a.shape, a.dt...  2.64 us

profile of v6, /device:TPU:0, one launch (start us, length us, event | category | flops | bytes accessed | tf_op | source)
XLA Modules:
  0.0 108.1 jit_solution(15680094989266711050)
XLA Ops:
  0.6 104.6 %shard_map.203 = (bf16[4,64,768]{2,1,0:T(8,128)(2,1)}, f32[4,64,768]{2,1,0:T(8,128)}, f32[2,24]{1,0:T(2,128)}, f32[2,24]{1,0:T(2,128)}, f32[24,2304]{1,0:T(8,128...) custom-call(bf16[4,64,768]{2,1,0:T(8,128)(2,1)} %patches.1, ...), custom_call_target="tpu_custom_call" | custom-call | tf_op jit(solution)/shard_map/pallas_call | solution.py:1878
  105.3 2.6 %shard_map.204 = (bf16[4,64,768]{2,1,0:T(8,128)(2,1)}, f32[4,64,768]{2,1,0:T(8,128)}, f32[2,24]{1,0:T(2,128)}, f32[2,24]{1,0:T(2,128)}, f32[24,2304]{1,0:T(8,128...) custom-call(bf16[4,64,768]{2,1,0:T(8,128)(2,1)} %get-tuple-element.3, ...), custom_call_target="tpu_custom_call" | custom-call | tf_op jit(solution)/shard_map/pallas_call | solution.py:1838

commit v7 on v6

--- a/solution.py
+++ b/solution.py
@@ -266,12 +266,15 @@
 SCATTER_UNITS = (
     ("o0", 3, 0, 3, 2, 0),
     ("q0", 0, 0, 3, 2, 0),
-    ("q1", 1, 0, 3, 2, 0),
-    ("q2", 2, 0, 3, 2, 0),
+    ("q1a", 1, 0, 2, 2, 0),
+    ("q1b", 1, 2, 1, 2, 0),
+    ("q2a", 2, 0, 2, 2, 0),
+    ("q2b", 2, 2, 1, 2, 0),
 )
 GATHER_FC2, SCATTER_FC2 = (1, 0, 0), (0, 0, 1)
 GATHER_LINES = dict(h=(1, 1), f=(1, 1, 1))
 SCATTER_LINES = dict(h=(1, 1), f=(1, 1, 1))
+FIRST_UNIT = "q0"
 
 
 PIECES = (((0, 12, 7), (6, 1, 13)), ((2, 14, 9), (8, 3, 15)), ((4, 16, 11), (10, 5, 17)))
@@ -298,8 +301,8 @@
     return lax.dot_general(left, right, (((0,), (0,)), ((), ())), preferred_element_type=F32)
 
 
-SENDS, ARRIVALS, KEPT = 48, 143, 28
-FC1_OUTPUT = 7
+SENDS, ARRIVALS, KEPT = 40, 145, 10
+FC1_OUTPUT, ROWS_OUTPUT = 7, 1
 
 
 def scratch_shapes():
@@ -349,7 +352,6 @@
         g_mixed=vm(256, 2304),
         enc_send=vm(2, 128, 768),
         gx_send=vm(256, 768),
-        gx_recv=vm(4, 64, 768),
         sums=vm(16, 768, dtype=F32),
         sums_fc1=vm(8, 1536, dtype=F32),
         g_small=vm(4, 4, 16, 256),
@@ -388,7 +390,6 @@
         send_fc1=vm(48, 768),
         last_fc2=vm(96, 384, dtype=F32),
         kept_fc2=vm(96, 384, dtype=F32),
-        gx_out=vm(4, 64, 768, dtype=F32),
         local_sem=pltpu.SemaphoreType.DMA((KEPT,)),
         send_sem=pltpu.SemaphoreType.DMA((SENDS,)),
         recv_sem=pltpu.SemaphoreType.DMA((ARRIVALS,)),
@@ -497,6 +498,19 @@
                 self.waited = True
                 self.copy.wait()
 
+    class Written:
+        def __init__(self, ref):
+            self.ref, self.arrived, self.copy = ref, Group(), None
+            self.sem = s.local_sem.at[len(kept)]
+            kept.append(self)
+
+        def write(self, source, target):
+            pltpu.make_async_copy(source, target, self.sem).start()
+
+        def wait(self):
+            self.arrived.wait(self.ref)
+            pltpu.make_async_copy(self.ref, self.ref, self.sem).wait()
+
     def lanes(start, size):
         return pl.ds(pl.multiple_of(start, 128), size)
 
@@ -511,31 +525,43 @@
     s.own_small[8:9, 0:96] = fc1_bias[...].astype(F32)
     s.w_small[z, here, :, lanes(128 * core, 128)] = s.own_small[...].astype(BF16)
     own_rows = pl.ds(pl.multiple_of(24 * core, 8), 24)
-    pieces = [(qkv_weight, 384 * j + 128 * t, partial(piece, j, t=t)) for j in range(3) for t in range(3)]
-    pieces += [(out_weight, 1152 + 128 * t, lambda side, t=t: 384 * side + 128 * t) for t in range(3)]
-    for ref, start, columns in pieces:
-        s.pair_send[:, start : start + 128] = ref[:, lanes(columns(1 - core), 128)].astype(F32)
-        s.pair_rows[own_rows, start : start + 128] = ref[:, lanes(columns(core), 128)].astype(F32)
-    theirs = fc1_weight[:, lanes((1 - core) * 1536, 1536)].astype(F32)
-    ours = fc1_weight[:, lanes(core * 1536, 1536)].astype(F32)
-    for side in (0, 1):
-        for k in range(4):
-            at, found = 768 * side + 192 * k, 384 * k + 192 * side
-            s.pair_send_h[:, at : at + 192] = theirs[:, found : found + 192]
-            s.pair_rows_h[own_rows, at : at + 192] = ours[:, found : found + 192]
+    pairs = {}
+
+    def prepare_rows(name):
+        if name == "h":
+            theirs = fc1_weight[:, lanes((1 - core) * 1536, 1536)].astype(F32)
+            ours = fc1_weight[:, lanes(core * 1536, 1536)].astype(F32)
+            for side in (0, 1):
+                for k in range(4):
+                    at, found = 768 * side + 192 * k, 384 * k + 192 * side
+                    s.pair_send_h[:, at : at + 192] = theirs[:, found : found + 192]
+                    s.pair_rows_h[own_rows, at : at + 192] = ours[:, found : found + 192]
+            return
+        j = 3 if name == "o" else int(name[1])
+        for t in range(3):
+            ref, at = (out_weight if name == "o" else qkv_weight), slice(384 * j + 128 * t, 384 * j + 128 * t + 128)
+            columns = (lambda side: 384 * side + 128 * t) if name == "o" else partial(piece, j, t=t)
+            s.pair_send[:, at] = ref[:, lanes(columns(1 - core), 128)].astype(F32)
+            s.pair_rows[own_rows, at] = ref[:, lanes(columns(core), 128)].astype(F32)
+
+    def send_pair(name):
+        source, target = s.pair_send_h, s.pair_rows_h.at[own_rows, :]
+        if name != "h":
+            j = 3 if name == "o" else int(name[1])
+            columns = slice(384 * j, 384 * j + 384)
+            source, target = s.pair_send.at[:, columns], s.pair_rows.at[own_rows, columns]
+        pairs[name] = remote(source, target, sibling)
+
+    def exchange(name):
+        prepare_rows(name)
+        send_pair(name)
+
+    prepare_rows(FIRST_UNIT)
 
     pl.semaphore_wait(barrier, len(peers))
 
-    pairs = {}
-    for name, start in (("q0", 0), ("q1", 384), ("q2", 768), ("o", 1152)):
-        columns = slice(start, start + 384)
-        pairs[name] = remote(s.pair_send.at[:, columns], s.pair_rows.at[own_rows, columns], sibling)
-    pairs["h"] = remote(s.pair_send_h, s.pair_rows_h.at[own_rows, :], sibling)
-
-
-    rows_moved = Group()
-    for py, pc in blk_peers:
-        remote(patches.at[2 * py + pc], s.rows_in.at[mine, :], (wide, 2 * py + pc), rows_moved)
+    send_pair(FIRST_UNIT)
+
 
     class Direct:
         def __init__(self, block):
@@ -1174,13 +1200,11 @@
                 total = total + s.py_a[0, :, at].astype(F32)
             s.last_a[:, at] = total
             other_rows = pl.ds(pl.multiple_of(24 * (1 - core), 8), 24)
-            group = Group()
-            finals.append((group, s.last_a.at[own_rows, at]))
             for t in range(size // 128):
                 some = slice(spot + 128 * t, spot + 128 * t + 128)
                 target = lanes(natural(core, t), 128)
-                remote(s.last_a.at[other_rows, some], output.at[:, target], sibling, group)
-                Local(s.last_a.at[own_rows, some], output.at[:, target])
+                remote(s.last_a.at[other_rows, some], output.at[:, target], sibling, columns_written.arrived)
+                columns_written.write(s.last_a.at[own_rows, some], output.at[:, target])
 
         if way == 9:
 
@@ -1249,9 +1273,8 @@
             other_rows = pl.ds(pl.multiple_of(24 * (1 - core), 8), 24)
             for i, half in enumerate((y, 1 - y)):
                 target = lanes(1536 * half + 768 * core + 384 * j, 384)
-                copy = remote(s.last_fc1.at[i, other_rows, at], grad_fc1.at[:, target], sibling)
-                finals.append((copy, None))
-                Local(s.last_fc1.at[i, own_rows, at], grad_fc1.at[:, target])
+                remote(s.last_fc1.at[i, other_rows, at], grad_fc1.at[:, target], sibling, fc1_written.arrived)
+                fc1_written.write(s.last_fc1.at[i, own_rows, at], grad_fc1.at[:, target])
 
         return PlaneScatter(
             own,
@@ -1271,9 +1294,9 @@
 
         def finish(scatter):
             s.last_fc2[rows, :] = scatter.summed(lambda ref: ref.at[1 - core])
-            finals.append((remote(s.last_fc2.at[rows, :], grad_fc2.at[rows, half], sibling), None))
+            remote(s.last_fc2.at[rows, :], grad_fc2.at[rows, half], sibling, fc2_written.arrived)
             s.kept_fc2[rows, :] = scatter.summed(lambda ref: ref.at[core])
-            Local(s.kept_fc2.at[rows, :], grad_fc2.at[rows, half])
+            fc2_written.write(s.kept_fc2.at[rows, :], grad_fc2.at[rows, half])
 
         def sides(side):
             return BOTH if side is ALL else side
@@ -1305,7 +1328,8 @@
         grad_res[...] = found[6:8, 0:24]
         grad_fc1_bias[...] = found[8:9, 0:96]
 
-    finals = []
+    columns_written, fc1_written = Written(s.last_a.at[own_rows, :]), Written(s.last_a.at[own_rows, :])
+    fc2_written = Written(s.last_fc2)
     scatters = {}
     for j, way in enumerate(SCATTER_FC2):
         scatters["f" + str(j)] = fc2_scatter(j, 96 // len(SCATTER_FC2), way)
@@ -1513,7 +1537,13 @@
             here_ = s.g_small.at[:, :, :, pl.ds(128 * side, 128)]
             here_[...] = here_[...] + dot(put, placed).astype(BF16).reshape(4, 4, 16, 128)
 
-    moved = {"rows": (rows_moved, s.rows_in.at[0:192, :])}
+    moved = {}
+
+    def send_rows():
+        group = Group()
+        for py, pc in blk_peers:
+            remote(patches.at[2 * py + pc], s.rows_in.at[mine, :], (wide, 2 * py + pc), group)
+        moved["rows"] = group, s.rows_in.at[0:192, :]
 
     cot_kept = {}
 
@@ -1553,9 +1583,9 @@
         group = Group()
         for py, pc in blk_peers:
             rows = pl.ds(pl.multiple_of(64 * (2 * py + pc), 64), 64)
-            remote(s.gx_send.at[rows, :], s.gx_recv.at[blk], (wide, 2 * py + pc), group)
-        moved["grad"] = group, s.gx_recv.at[THREE]
-        s.gx_recv[blk] = s.gx_send[mine, :]
+            remote(s.gx_send.at[rows, :], grad_patches.at[blk], (wide, 2 * py + pc), group)
+        moved["grad"] = group, s.gx_send.at[0:192, :]
+        Local(s.gx_send.at[mine, :], grad_patches.at[blk])
 
     def project_attended():
         s.g_attended[...] = dot_nt(s.g_branch[...], s.w_out[...].reshape(D, D)).astype(BF16)
@@ -1604,205 +1634,214 @@
         column_grad(s.normed_t, s.g_mixed, s.g_qkv, lambda side: 768 * j + 384 * side)
 
     g, r = types.SimpleNamespace(**gathers), types.SimpleNamespace(**scatters)
+    send_rows()
     g.s0.z()
+    exchange("q2")
     assemble("q0")
     g.q0.z()
+    g.f1.x()
+    g.f2.x()
+    assemble("q2")
+    g.q2.z()
+    g.q0.o()
+    exchange("h")
+    exchange("q1")
+    exchange("o")
     assemble("q1")
-    g.f1.x()
+    g.s0.p()
+    g.q1.z()
+    assemble("o")
+    g.o0.z()
+    g.q2.o()
+    g.o0.o()
+    g.q0.p()
     assemble("h")
-    g.q0.o()
-    assemble("q2")
-    g.q1.z()
-    g.q2.z()
-    g.s0.p()
-    g.f2.x()
-    assemble("o")
-    g.q2.o()
+    g.h1.y()
+    g.s0.f()
     g.q1.o()
-    g.q0.p()
-    g.h0.y()
-    g.h1.y()
-    g.o0.z()
-    g.o0.o()
-    g.q1.p()
+    g.s0.g()
+    g.q2.p()
     g.q0.f()
     g.q0.g()
-    g.s0.f()
+    g.h0.y()
+    g.s0.l()
+    g.h1.z()
+    g.q1.p()
+    g.f2.z()
+    g.o0.p()
+    g.h1.w()
     g.h0.z()
-    g.q2.p()
-    g.h1.z()
-    g.s0.g()
-    g.o0.p()
+    g.q2.f()
+    g.s0.d()
+    unpack_small()
+    g.q0.l()
+    g.q2.g()
+    start_norm()
     g.q1.f()
+    g.q1.g()
+    g.h1.v()
+    g.o0.f()
+    send_cotangent(0)
+    g.o0.g()
+    g.q0.d()
     g.h0.w()
-    g.q1.g()
-    g.q0.l()
-    g.h1.w()
-    g.q2.f()
+    g.f0.z()
+    project_qkv(0)
+    attend(0)
+    g.h1.x()
+    g.q2.l()
+    g.q1.l()
     g.h0.v()
-    g.q2.g()
-    g.s0.l()
-    g.q0.d()
-    g.f2.z()
-    g.s0.d()
-    g.o0.f()
-    g.f0.z()
-    g.h1.v()
-    g.o0.g()
+    g.q2.d()
+    g.q1.d()
     send_cotangent(1)
-    send_cotangent(0)
-    unpack_small()
+    g.f0.w()
     g.f1.z()
-    g.h0.x()
-    start_norm()
-    g.q2.l()
-    project_qkv(0)
-    g.f2.w()
-    g.q1.l()
-    attend(0)
-    g.q1.d()
     project_qkv(1)
     g.o0.l()
-    g.f0.w()
-    g.q2.d()
+    attend(1)
+    g.o0.d()
     project_qkv(2)
-    g.h1.x()
-    attend(1)
+    g.h0.x()
+    g.f2.w()
     attend(2)
+    project_out(0)
     g.f0.v()
-    g.o0.d()
+    send_normed(0)
+    start_cotangent(0)
     g.f1.w()
-    project_out(0)
-    send_normed(0)
+    g.h1.l()
+    g.f2.v()
     project_out(1)
-    start_cotangent(0)
-    g.f2.v()
+    transpose_out()
+    g.h1.d()
+    send_normed(1)
+    feed_own(1)
+    g.f1.v()
+    start_cotangent(1)
     g.f0.x()
     g.h0.l()
-    transpose_out()
-    g.f1.v()
-    send_normed(1)
-    start_cotangent(1)
+    take_normed(0)
+    feed_other(1, 0)
+    g.f2.l()
     g.h0.d()
     feed_own(0)
-    g.h1.l()
-    take_normed(0)
-    g.f2.l()
     feed_other(0, 0)
-    g.h1.d()
-    feed_own(1)
-    feed_other(1, 0)
     g.f1.l()
     take_normed(1)
     feed_other(1, 1)
+    g.f0.l()
     feed_other(0, 1)
-    g.f0.l()
+    weight_grad_fc2(1)
+    g.f2.d()
+    r.f1.s()
+    g.f1.d()
+    weight_grad_fc2(2)
+    g.f0.d()
+    r.f2.s()
+    feed_back(1)
+    r.f1.z()
+    feed_back_other()
+    send_back(0)
+    send_back(1)
+    r.f2.x()
+    transpose_other()
+    feed_back(0)
+    grad_fc1_weight(0)
+    r.h0.s()
     weight_grad_fc2(0)
     r.f0.s()
-    weight_grad_fc2(2)
-    r.f2.s()
-    g.f2.d()
-    g.f1.d()
-    g.f0.d()
-    feed_back(1)
+    feed_back_own()
+    r.h0.x()
+    feed_out(1)
     r.f0.z()
-    feed_back_other()
-    transpose_other()
-    send_back(0)
-    r.f2.x()
-    feed_back(0)
     grad_fc1_weight(1)
     r.h1.s()
-    weight_grad_fc2(1)
-    r.f1.s()
-    send_back(1)
-    feed_back_own()
+    start_second(0)
+    send_part()
+    feed_out(0)
+    r.f2.z()
     r.h1.x()
-    r.f1.z()
-    feed_out(1)
-    grad_fc1_weight(0)
-    r.f2.z()
-    send_part()
-    r.h0.s()
-    start_second(0)
-    feed_out(0)
-    r.h0.x()
     start_second(1)
-    r.f0.w()
+    project_attended()
+    r.f1.w()
     send_base()
-    grad_out_weight()
-    project_attended()
-    r.o0.s()
     attend_back(0)
-    r.h1.z()
-    r.f1.w()
-    r.o0.p()
+    r.h0.z()
     grad_qkv_weight(0)
     r.q0.s()
+    r.f0.w()
     attend_back(1)
+    r.q0.p()
     grad_qkv_weight(1)
-    r.h0.z()
+    r.q1b.s()
+    grad_out_weight()
+    start_output()
+    r.q1a.s()
+    r.h1.z()
     r.f2.w()
-    r.q1.s()
-    r.q0.p()
+    r.o0.s()
+    r.q1b.p()
+    r.q0.f()
+    r.q0.g()
+    r.f1.v()
+    r.q1a.p()
+    r.h0.w()
+    r.o0.p()
     attend_back(2)
+    r.f2.v()
+    r.q0.z()
+    grad_qkv_weight(2)
+    r.q1a.f()
+    r.q2b.s()
+    r.q1a.g()
+    r.h0.v()
+    r.f0.v()
+    r.q2a.s()
+    r.q1b.f()
     r.h1.w()
-    r.f1.v()
+    r.q2b.p()
     r.o0.f()
     r.o0.g()
-    start_output()
-    r.q1.p()
     first_norm_back()
-    r.f2.v()
-    r.h0.w()
-    r.q0.f()
-    r.q0.g()
-    r.f0.v()
+    r.q1a.z()
+    r.q2b.f()
+    r.q2a.p()
+    pack_small()
+    r.h1.v()
+    r.q2b.g()
+    r.s0.s()
+    r.q0.l()
     r.o0.z()
-    r.h1.v()
-    grad_qkv_weight(2)
-    r.q1.f()
-    r.q2.s()
-    r.q1.g()
-    pack_small()
-    r.s0.s()
-    r.q2.p()
     r.s0.p()
-    r.h0.v()
-    r.q0.z()
-    r.q1.z()
-    r.q2.f()
-    r.q2.g()
+    r.q1b.g()
+    r.q2a.f()
+    r.h0.y()
+    r.q2a.g()
+    r.q2b.z()
+    r.s0.f()
     r.h1.y()
+    send_grad_rows()
+    r.s0.g()
+    r.q1b.z()
     r.f1.x()
-    r.s0.f()
+    r.q2a.z()
+    r.f0.x()
+    r.q1a.l()
+    r.o0.l()
     r.f2.l()
-    r.s0.g()
-    r.f0.x()
-    r.h0.y()
-    send_grad_rows()
-    r.q2.z()
+    r.h1.l()
+    r.s0.z()
+    r.q2b.l()
+    r.f1.l()
+    r.h0.l()
+    r.f0.l()
+    r.q1b.l()
     send_encoded()
-    r.s0.z()
-    r.q0.l()
-    r.f0.l()
-    r.h0.l()
-    r.f1.l()
-    r.o0.l()
-    r.q1.l()
-    r.h1.l()
-    r.q2.l()
+    r.q2a.l()
     r.s0.l()
-    received("grad")
-    s.gx_out[...] = s.gx_recv[...].astype(F32)
-    Local(s.gx_out, grad_patches)
     for name in list(moved):
         received(name)
-    for arrived, ref in finals:
-        if ref is None:
-            arrived.wait_recv()
-        else:
-            arrived.wait(ref)
     for copy in kept:
         copy.wait()
     for spot in range(max(0, len(started) - SENDS), len(started)):
@@ -1810,17 +1849,18 @@
 
 
 def emit_kernel(*refs):
-    count = (len(refs) - 3) // 3
+    count = (len(refs) - 4) // 3
     given, made, held = refs[:count], refs[count : 2 * count], refs[2 * count : 3 * count]
-    ordered, in_sem, out_sem = refs[3 * count :]
+    ordered, wide_rows, in_sem, out_sem = refs[3 * count :]
+    ready = {FC1_OUTPUT: ordered, ROWS_OUTPUT: wide_rows}
     arrive = [pltpu.make_async_copy(given[i], held[i], in_sem.at[i]) for i in range(count)]
-    leave = [
-        pltpu.make_async_copy(ordered if i == FC1_OUTPUT else held[i], made[i], out_sem.at[i]) for i in range(count)
-    ]
+    leave = [pltpu.make_async_copy(ready.get(i, held[i]), made[i], out_sem.at[i]) for i in range(count)]
     for copy in arrive:
         copy.start()
     for i in range(count):
         arrive[i].wait()
+        if i == ROWS_OUTPUT:
+            wide_rows[...] = held[i][...].astype(F32)
         if i == FC1_OUTPUT:
             for side in (0, 1):
                 for k in range(8):
@@ -1834,14 +1874,15 @@
 def emit(arrays):
     anywhere = pl.BlockSpec(memory_space=pl.ANY)
     count = len(arrays)
+    dtypes = [F32 if i == ROWS_OUTPUT else a.dtype for i, a in enumerate(arrays)]
     return list(
         pl.pallas_call(
             emit_kernel,
-            out_shape=[jax.ShapeDtypeStruct(a.shape, a.dtype) for a in arrays],
+            out_shape=[jax.ShapeDtypeStruct(a.shape, dtype) for a, dtype in zip(arrays, dtypes)],
             in_specs=[anywhere] * count,
             out_specs=[anywhere] * count,
             scratch_shapes=[pltpu.VMEM(a.shape, a.dtype) for a in arrays]
-            + [pltpu.VMEM(arrays[FC1_OUTPUT].shape, F32)]
+            + [pltpu.VMEM(arrays[i].shape, F32) for i in (FC1_OUTPUT, ROWS_OUTPUT)]
             + [pltpu.SemaphoreType.DMA((count,))] * 2,
         )(*arrays)
     )
@@ -1863,7 +1904,7 @@
 ):
     outputs = [
         ((4, 64, D), BF16),
-        ((4, 64, D), F32),
+        ((4, 64, D), BF16),
         ((2, 24), F32),
         ((2, 24), F32),
         ((24, 3 * D), F32),

time: 108 us -> 107 us (level)
    pallas_call x1, Pallas kernels: 105 us -> 103 us  [fast(): pl.pallas_call(layer_kernel, out_shape=[jax.ShapeDtypeStruct(shape, dtype...]
where the time goes in v7:
time: 107 us
  Pallas kernels  106 us (99%)
    pallas_call x1, Pallas kernels, fast(): pl.pallas_call(layer_kernel, out_shape=[jax.ShapeDtypeStruct(shape, dtype...  103 us
    pallas_call x1, Pallas kernels, emit(): pl.pallas_call(emit_kernel, out_shape=[jax.ShapeDtypeStruct(a.shape, dtyp...  2.55 us

profile of v7, /device:TPU:0, one launch (start us, length us, event | category | flops | bytes accessed | tf_op | source)
XLA Modules:
  0.0 106.7 jit_solution(14585437977138525886)
XLA Ops:
  0.6 103.4 %shard_map.203 = (bf16[4,64,768]{2,1,0:T(8,128)(2,1)}, bf16[4,64,768]{2,1,0:T(8,128)(2,1)}, f32[2,24]{1,0:T(2,128)}, f32[2,24]{1,0:T(2,128)}, f32[24,2304]{1,0:T...) custom-call(bf16[4,64,768]{2,1,0:T(8,128)(2,1)} %patches.1, ...), custom_call_target="tpu_custom_call" | custom-call | tf_op jit(solution)/shard_map/pallas_call | solution.py:1919
  104.0 2.6 %shard_map.204 = (bf16[4,64,768]{2,1,0:T(8,128)(2,1)}, f32[4,64,768]{2,1,0:T(8,128)}, f32[2,24]{1,0:T(2,128)}, f32[2,24]{1,0:T(2,128)}, f32[24,2304]{1,0:T(8,128...) custom-call(bf16[4,64,768]{2,1,0:T(8,128)(2,1)} %get-tuple-element.3, ...), custom_call_target="tpu_custom_call" | custom-call | tf_op jit(solution)/shard_map/pallas_call | solution.py:1879

commit v8 on v7

--- a/solution.py
+++ b/solution.py
@@ -441,7 +441,9 @@
     blk_peers = [(y, 1 - core), (1 - y, core), (1 - y, 1 - core)]
 
     barrier = pltpu.get_barrier_semaphore()
-    peers = [sibling, x_peer, y_peer, d_peer, y_cross] + z_peers[1:]
+    peers = [sibling, x_peer, y_peer, y_cross] + z_peers[1:]
+    if any(unit[4] == 0 for unit in GATHER_UNITS + SCATTER_UNITS):
+        peers.append(d_peer)
     for peer in peers:
         pl.semaphore_signal(barrier, inc=1, device_id=peer, device_id_type=MESH_ID)
 
@@ -516,14 +518,6 @@
 
     mine = pl.ds(pl.multiple_of(64 * blk, 64), 64)
     taken = [Local(fc2_weight, s.w_fc2.at[z, x, core]), Local(patches.at[blk], s.rows_in.at[mine, :])]
-    s.own_small[...] = jnp.zeros((16, 128), F32)
-    s.sums[...] = jnp.zeros((16, D), F32)
-    s.own_small[0:2, 0:24] = norm_gain[...].astype(F32)
-    s.own_small[2:4, 0:24] = norm_bias[...].astype(F32)
-    s.own_small[4:6, 0:24] = qv_bias[...].astype(F32)
-    s.own_small[6:8, 0:24] = res_bias[...].astype(F32)
-    s.own_small[8:9, 0:96] = fc1_bias[...].astype(F32)
-    s.w_small[z, here, :, lanes(128 * core, 128)] = s.own_small[...].astype(BF16)
     own_rows = pl.ds(pl.multiple_of(24 * core, 8), 24)
     pairs = {}
 
@@ -1635,6 +1629,14 @@
 
     g, r = types.SimpleNamespace(**gathers), types.SimpleNamespace(**scatters)
     send_rows()
+    s.own_small[...] = jnp.zeros((16, 128), F32)
+    s.sums[...] = jnp.zeros((16, D), F32)
+    s.own_small[0:2, 0:24] = norm_gain[...].astype(F32)
+    s.own_small[2:4, 0:24] = norm_bias[...].astype(F32)
+    s.own_small[4:6, 0:24] = qv_bias[...].astype(F32)
+    s.own_small[6:8, 0:24] = res_bias[...].astype(F32)
+    s.own_small[8:9, 0:96] = fc1_bias[...].astype(F32)
+    s.w_small[z, here, :, lanes(128 * core, 128)] = s.own_small[...].astype(BF16)
     g.s0.z()
     exchange("q2")
     assemble("q0")

time: 107 us -> 107 us (level)
  no operation moved by 1% of the time
where the time goes in v8:
time: 107 us
  Pallas kernels  106 us (99%)
    pallas_call x1, Pallas kernels, fast(): pl.pallas_call(layer_kernel, out_shape=[jax.ShapeDtypeStruct(shape, dtype...  104 us
    pallas_call x1, Pallas kernels, emit(): pl.pallas_call(emit_kernel, out_shape=[jax.ShapeDtypeStruct(a.shape, dtyp...  2.55 us

profile of v8, /device:TPU:0, one launch (start us, length us, event | category | flops | bytes accessed | tf_op | source)
XLA Modules:
  0.0 106.9 jit_solution(15528048571957611620)
XLA Ops:
  0.6 103.5 %shard_map.203 = (bf16[4,64,768]{2,1,0:T(8,128)(2,1)}, bf16[4,64,768]{2,1,0:T(8,128)(2,1)}, f32[2,24]{1,0:T(2,128)}, f32[2,24]{1,0:T(2,128)}, f32[24,2304]{1,0:T...) custom-call(bf16[4,64,768]{2,1,0:T(8,128)(2,1)} %patches.1, ...), custom_call_target="tpu_custom_call" | custom-call | tf_op jit(solution)/shard_map/pallas_call | solution.py:1921
  104.2 2.6 %shard_map.204 = (bf16[4,64,768]{2,1,0:T(8,128)(2,1)}, f32[4,64,768]{2,1,0:T(8,128)}, f32[2,24]{1,0:T(2,128)}, f32[2,24]{1,0:T(2,128)}, f32[24,2304]{1,0:T(8,128...) custom-call(bf16[4,64,768]{2,1,0:T(8,128)(2,1)} %get-tuple-element.3, ...), custom_call_target="tpu_custom_call" | custom-call | tf_op jit(solution)/shard_map/pallas_call | solution.py:1881
